TPU v7x, 32 devices: a whole 2x2x4 slice. The times are simulated.
32 devices in a mesh: blk: 4 (over z), section: 8 (over y, x, core).
Axes of the slice: x: 2, y: 2, z: 4, core: 2. Of those that a mesh axis runs over, the one named last changes fastest.
Arguments:
- text_emb: bfloat16 [8, 1024, 1024], P(None, ('blk', 'section')), may hold values from -6 to 6
- covariate: bfloat16 [8, 256, 1024], P('section', 'blk'), may hold values from -6 to 6
- labels: int32 [8, 1024], P('section', 'blk'), may hold values from 0 to 255, as said below
- logit_scale: float32 [1], replicated, may hold values from 0.02 to 0.08
- logit_bias: float32 [1], replicated, may hold values from -3 to -1
Outputs:
- text_grad: float32 [8, 1024, 1024], P('section', 'blk')
- cov_grad: float32 [8, 256, 1024], P('section', 'blk')
Inputs may be any that keep to these rules, and one draw needn't show every extreme that they name: `labels`: every covariate row of a group is the positive of exactly 4 text rows of that group.
All inputs are finite; a program needn't handle non-finite values.
Results may differ from a plain program's by a relative error of at most 0.0025.
Values may be sent and summed in bfloat16 or wider, within the bound.
No kernel may reach another device: no remote copies, remote signals or barrier semaphores. Data moves between devices by JAX's collectives and lax.ppermute only.
A program may use at most 64 MiB of HBM per device.

v0:
```python
import jax
import jax.numpy as jnp
from jax import lax
from jax.sharding import PartitionSpec as P


def shifted_2(value, axis, steps):
    count = lax.axis_size(axis)
    pairs = [(source, (source + steps) % count) for source in range(count)]
    return lax.ppermute(value, axis, pairs)


def local(text_emb, covariate, labels, logit_scale, logit_bias):
    panel = lax.all_to_all(text_emb, "section", split_axis=0, concat_axis=1, tiled=True)[0]
    cov_own = covariate[0]
    row_labels = labels[0]
    cycle_len = lax.axis_size("blk")
    cycle_pos = lax.axis_index("blk")
    piece_rows = cov_own.shape[0]
    factor = logit_scale[0]
    offset = logit_bias[0]
    local_ids = jnp.arange(piece_rows, dtype=jnp.int32)

    def cycle_step(carry, visits):
        cov_piece, running, text_acc = carry
        source = (cycle_pos - visits) % cycle_len
        logits = (
            factor
            * lax.dot_general(
                cov_piece, panel, (((1,), (1,)), ((), ())), preferred_element_type=jnp.float32
            )
            + offset
        )
        row_ids = source * piece_rows + local_ids
        positive = (row_labels[None, :] == row_ids[:, None]).astype(jnp.float32)
        weights_bf = (factor * (jax.nn.sigmoid(logits) - positive)).astype(jnp.bfloat16)
        cov_term = jnp.dot(weights_bf, panel, preferred_element_type=jnp.float32)
        text_acc = text_acc + lax.dot_general(
            weights_bf, cov_piece, (((0,), (0,)), ((), ())), preferred_element_type=jnp.float32
        )
        shifted = shifted_2(cov_piece, "blk", 1)
        running = shifted_2(running + cov_term, "blk", 1)
        saved = jnp.zeros((), jnp.float32)
        return ((shifted, running, text_acc), saved)

    start_sum = jnp.zeros(cov_own.shape, jnp.float32)
    start_text = jnp.zeros(panel.shape, jnp.float32)
    (final_piece, running, text_grad), saved = lax.scan(
        cycle_step, (cov_own, start_sum, start_text), jnp.arange(cycle_len, dtype=jnp.int32)
    )
    return (text_grad[None], running[None])


def solution(mesh):
    return jax.shard_map(
        local,
        mesh=mesh,
        in_specs=(
            P(None, ("blk", "section"), None),
            P("section", "blk", None),
            P("section", "blk"),
            P(),
            P(),
        ),
        out_specs=(P("section", "blk", None), P("section", "blk", None)),
        check_vma=False,
    )
```

profile of v0, /device:TPU:2, one launch (start us, length us, event | category | flops | bytes accessed | tf_op | source)
XLA Modules:
  0.0 67.0 jit_solution(3358907915066200877)
XLA Ops:
  0.6 4.3 %all-to-all-start = ((bf16[8,32,1024]{2,1,0:T(8,128)(2,1)}), bf16[8,32,1024]{2,1,0:T(8,128)(2,1)S(1)}, u32[]{:S(2)}, u32[]{:S(2)}) async-start(bf16[8,32,1024]{2,1,0:T(8,128)(2,1)} %param.7), calls=%async_computation | async-start | bytes 1048576 | tf_op jit(solution)/shard_map/all_to_all | solution.py:14
  4.9 8.3 %all-to-all-done = bf16[8,32,1024]{2,1,0:T(8,128)(2,1)S(1)} async-done(((bf16[8,32,1024]{2,1,0:T(8,128)(2,1)}), bf16[8,32,1024]{2,1,0:T(8,128)(2,1)S(1)}, u32[]{:S(2)}, u32[]{:S(2)}) %all-to-all-start) | async-done | bytes 524320 | tf_op jit(solution)/shard_map/all_to_all | solution.py:14
  13.2 0.9 %copy-done.1 = bf16[1,64,1024]{2,1,0:T(8,128)(2,1)S(1)} copy-done((bf16[1,64,1024]{2,1,0:T(8,128)(2,1)S(1)}, bf16[1,64,1024]{2,1,0:T(8,128)(2,1)}, u32[]{:S(2)}) %copy-start.1) | copy-done | bytes 131096
  14.1 51.8 %while.17 = (s32[]{:T(128)}, bf16[64,1024]{1,0:T(8,128)(2,1)S(1)}, f32[64,1024]{1,0:T(8,128)S(1)}, f32[256,1024]{1,0:T(8,128)S(1)}, f32[]{:T(128)}, /*index=5*/b...) while((s32[]{:T(128)}, bf16[64,1024]{1,0:T(8,128)(2,1)S(1)}, ...), condition=%wide.region_1.2_spmd.clone, body=%wide.region_0.1_spmd.clone.sunk | while | flops 101417040 | bytes 5867396 | solution.py:48
  14.1 1.6 %collective-permute-start = (bf16[64,1024]{1,0:T(8,128)(2,1)S(1)}, bf16[64,1024]{1,0:T(8,128)(2,1)S(1)}, u32[]{:S(2)}, u32[]{:S(2)}) collective-permute-start(bf16[64,1024]{1,0:T(8,128)(2,1)S(1)} %copy.12), channel_id=1, source_target_pairs={{0,8},{8,16},{16,24},{24,0},{1,9},{9,17},{17,25},{25,1},{2,10},{10... | collective-permute-start | bytes 393224 | tf_op jit(solution)/shard_map/while/body/eval_jaxpr/ppermute | solution.py:10
  15.7 0.6 dynamic_slice.9
  16.9 1.6 %fusion.29 = bf16[64,256]{1,0:T(8,128)(2,1)S(1)} fusion(bf16[64,1024]{1,0:T(8,128)(2,1)S(1)} %copy.12, bf16[256,1024]{1,0:T(8,128)(2,1)S(1)} %get-tuple-element.294, s32[256]{0:T(256)S(1)} %bitcast.34, f32[]{:T(128)} %get-tuple-element.295, f32[]{:T(128)} %get-tuple-element.293, s32[64]{0:T(128)S(1)} %iota_add_fusion.2), kind=kOutput, calls=%fused_computation.11.clone.1 | convolution fusion | flops 33718272 | bytes 689416 | tf_op jit(solution)/shard_map/while/body/eval_jaxpr/dot_general | solution.py:29
  18.5 0.2 convolution_add_fusion.4
  18.7 1.6 %collective-permute-start.1 = (f32[64,1024]{1,0:T(8,128)S(1)}, f32[64,1024]{1,0:T(8,128)S(1)}, u32[]{:S(2)}, u32[]{:S(2)}) collective-permute-start(f32[64,1024]{1,0:T(8,128)S(1)} %convolution_add_fusion.4), channel_id=1, source_target_pairs={{0,8},{8,16},{16,24},{24,0},{1,9},{9,17},{17,25},{25,1},{2,10},{10... | collective-permute-start | bytes 786440 | tf_op jit(solution)/shard_map/while/body/eval_jaxpr/ppermute | solution.py:10
  20.4 0.4 convolution_add_fusion.5
  20.8 0.7 %collective-permute-done = bf16[64,1024]{1,0:T(8,128)(2,1)S(1)} collective-permute-done((bf16[64,1024]{1,0:T(8,128)(2,1)S(1)}, bf16[64,1024]{1,0:T(8,128)(2,1)S(1)}, u32[]{:S(2)}, u32[]{:S(2)}) %collective-permute-start) | collective-permute-done | bytes 131104 | tf_op jit(solution)/shard_map/while/body/eval_jaxpr/ppermute | solution.py:10
  21.5 7.1 %collective-permute-done.1 = f32[64,1024]{1,0:T(8,128)S(1)} collective-permute-done((f32[64,1024]{1,0:T(8,128)S(1)}, f32[64,1024]{1,0:T(8,128)S(1)}, u32[]{:S(2)}, u32[]{:S(2)}) %collective-permute-start.1) | collective-permute-done | bytes 262176 | tf_op jit(solution)/shard_map/while/body/eval_jaxpr/ppermute | solution.py:10
  28.6 0.6 dynamic_slice.9
  29.8 1.6 %fusion.29 = bf16[64,256]{1,0:T(8,128)(2,1)S(1)} fusion(bf16[64,1024]{1,0:T(8,128)(2,1)S(1)} %copy.12, bf16[256,1024]{1,0:T(8,128)(2,1)S(1)} %get-tuple-element.294, s32[256]{0:T(256)S(1)} %bitcast.34, f32[]{:T(128)} %get-tuple-element.295, f32[]{:T(128)} %get-tuple-element.293, s32[64]{0:T(128)S(1)} %iota_add_fusion.2), kind=kOutput, calls=%fused_computation.11.clone.1 | convolution fusion | flops 33718272 | bytes 689416 | tf_op jit(solution)/shard_map/while/body/eval_jaxpr/dot_general | solution.py:29
  31.4 0.2 convolution_add_fusion.4
  31.6 1.4 %collective-permute-start.1 = (f32[64,1024]{1,0:T(8,128)S(1)}, f32[64,1024]{1,0:T(8,128)S(1)}, u32[]{:S(2)}, u32[]{:S(2)}) collective-permute-start(f32[64,1024]{1,0:T(8,128)S(1)} %convolution_add_fusion.4), channel_id=1, source_target_pairs={{0,8},{8,16},{16,24},{24,0},{1,9},{9,17},{17,25},{25,1},{2,10},{10... | collective-permute-start | bytes 786440 | tf_op jit(solution)/shard_map/while/body/eval_jaxpr/ppermute | solution.py:10
  33.0 0.4 convolution_add_fusion.5
  33.4 2.4 %collective-permute-done = bf16[64,1024]{1,0:T(8,128)(2,1)S(1)} collective-permute-done((bf16[64,1024]{1,0:T(8,128)(2,1)S(1)}, bf16[64,1024]{1,0:T(8,128)(2,1)S(1)}, u32[]{:S(2)}, u32[]{:S(2)}) %collective-permute-start) | collective-permute-done | bytes 131104 | tf_op jit(solution)/shard_map/while/body/eval_jaxpr/ppermute | solution.py:10
  35.8 5.2 %collective-permute-done.1 = f32[64,1024]{1,0:T(8,128)S(1)} collective-permute-done((f32[64,1024]{1,0:T(8,128)S(1)}, f32[64,1024]{1,0:T(8,128)S(1)}, u32[]{:S(2)}, u32[]{:S(2)}) %collective-permute-start.1) | collective-permute-done | bytes 262176 | tf_op jit(solution)/shard_map/while/body/eval_jaxpr/ppermute | solution.py:10
  41.1 0.6 dynamic_slice.9
  42.3 1.6 %fusion.29 = bf16[64,256]{1,0:T(8,128)(2,1)S(1)} fusion(bf16[64,1024]{1,0:T(8,128)(2,1)S(1)} %copy.12, bf16[256,1024]{1,0:T(8,128)(2,1)S(1)} %get-tuple-element.294, s32[256]{0:T(256)S(1)} %bitcast.34, f32[]{:T(128)} %get-tuple-element.295, f32[]{:T(128)} %get-tuple-element.293, s32[64]{0:T(128)S(1)} %iota_add_fusion.2), kind=kOutput, calls=%fused_computation.11.clone.1 | convolution fusion | flops 33718272 | bytes 689416 | tf_op jit(solution)/shard_map/while/body/eval_jaxpr/dot_general | solution.py:29
  43.9 0.2 convolution_add_fusion.4
  44.2 0.4 convolution_add_fusion.5
  44.6 4.3 %collective-permute-done = bf16[64,1024]{1,0:T(8,128)(2,1)S(1)} collective-permute-done((bf16[64,1024]{1,0:T(8,128)(2,1)S(1)}, bf16[64,1024]{1,0:T(8,128)(2,1)S(1)}, u32[]{:S(2)}, u32[]{:S(2)}) %collective-permute-start) | collective-permute-done | bytes 131104 | tf_op jit(solution)/shard_map/while/body/eval_jaxpr/ppermute | solution.py:10
  48.9 4.6 %collective-permute-done.1 = f32[64,1024]{1,0:T(8,128)S(1)} collective-permute-done((f32[64,1024]{1,0:T(8,128)S(1)}, f32[64,1024]{1,0:T(8,128)S(1)}, u32[]{:S(2)}, u32[]{:S(2)}) %collective-permute-start.1) | collective-permute-done | bytes 262176 | tf_op jit(solution)/shard_map/while/body/eval_jaxpr/ppermute | solution.py:10
  53.5 0.6 dynamic_slice.9
  54.7 1.6 %fusion.29 = bf16[64,256]{1,0:T(8,128)(2,1)S(1)} fusion(bf16[64,1024]{1,0:T(8,128)(2,1)S(1)} %copy.12, bf16[256,1024]{1,0:T(8,128)(2,1)S(1)} %get-tuple-element.294, s32[256]{0:T(256)S(1)} %bitcast.34, f32[]{:T(128)} %get-tuple-element.295, f32[]{:T(128)} %get-tuple-element.293, s32[64]{0:T(128)S(1)} %iota_add_fusion.2), kind=kOutput, calls=%fused_computation.11.clone.1 | convolution fusion | flops 33718272 | bytes 689416 | tf_op jit(solution)/shard_map/while/body/eval_jaxpr/dot_general | solution.py:29
  56.6 0.4 convolution_add_fusion.5
  57.0 4.3 %collective-permute-done = bf16[64,1024]{1,0:T(8,128)(2,1)S(1)} collective-permute-done((bf16[64,1024]{1,0:T(8,128)(2,1)S(1)}, bf16[64,1024]{1,0:T(8,128)(2,1)S(1)}, u32[]{:S(2)}, u32[]{:S(2)}) %collective-permute-start) | collective-permute-done | bytes 131104 | tf_op jit(solution)/shard_map/while/body/eval_jaxpr/ppermute | solution.py:10
  61.3 4.6 %collective-permute-done.1 = f32[64,1024]{1,0:T(8,128)S(1)} collective-permute-done((f32[64,1024]{1,0:T(8,128)S(1)}, f32[64,1024]{1,0:T(8,128)S(1)}, u32[]{:S(2)}, u32[]{:S(2)}) %collective-permute-start.1) | collective-permute-done | bytes 262176 | tf_op jit(solution)/shard_map/while/body/eval_jaxpr/ppermute | solution.py:10
  65.9 0.7 %copy.22 = f32[1,64,1024]{2,1,0:T(8,128)} copy(f32[1,64,1024]{2,1,0:T(8,128)S(1)} %bitcast.32) | data formatting | bytes 524288
  66.7 0.3 copy-done
  (21 shorter events, 0.6 us)
Async XLA Ops:
  0.6 12.6 %all-to-all-start = ((bf16[8,32,1024]{2,1,0:T(8,128)(2,1)}), bf16[8,32,1024]{2,1,0:T(8,128)(2,1)S(1)}, u32[]{:S(2)}, u32[]{:S(2)}) async-start(bf16[8,32,1024]{2,1,0:T(8,128)(2,1)} %param.7), calls=%async_computation | async-start | bytes 1048576 | tf_op jit(solution)/shard_map/all_to_all | solution.py:14
  13.2 0.9 %copy-start.1 = (bf16[1,64,1024]{2,1,0:T(8,128)(2,1)S(1)}, bf16[1,64,1024]{2,1,0:T(8,128)(2,1)}, u32[]{:S(2)}) copy-start(bf16[1,64,1024]{2,1,0:T(8,128)(2,1)} %param.8) | copy-start | bytes 393220
  13.2 0.9 %copy-start.2 = (s32[1,256]{1,0:T(1,128)S(1)}, s32[1,256]{1,0:T(1,128)}, u32[]{:S(2)}) copy-start(s32[1,256]{1,0:T(1,128)} %param.9) | copy-start | bytes 3076
  14.1 7.4 %collective-permute-start = (bf16[64,1024]{1,0:T(8,128)(2,1)S(1)}, bf16[64,1024]{1,0:T(8,128)(2,1)S(1)}, u32[]{:S(2)}, u32[]{:S(2)}) collective-permute-start(bf16[64,1024]{1,0:T(8,128)(2,1)S(1)} %copy.12), channel_id=1, source_target_pairs={{0,8},{8,16},{16,24},{24,0},{1,9},{9,17},{17,25},{25,1},{2,10},{10... | collective-permute-start | bytes 393224 | tf_op jit(solution)/shard_map/while/body/eval_jaxpr/ppermute | solution.py:10
  18.7 9.8 %collective-permute-start.1 = (f32[64,1024]{1,0:T(8,128)S(1)}, f32[64,1024]{1,0:T(8,128)S(1)}, u32[]{:S(2)}, u32[]{:S(2)}) collective-permute-start(f32[64,1024]{1,0:T(8,128)S(1)} %convolution_add_fusion.4), channel_id=1, source_target_pairs={{0,8},{8,16},{16,24},{24,0},{1,9},{9,17},{17,25},{25,1},{2,10},{10... | collective-permute-start | bytes 786440 | tf_op jit(solution)/shard_map/while/body/eval_jaxpr/ppermute | solution.py:10
  28.6 7.2 %collective-permute-start = (bf16[64,1024]{1,0:T(8,128)(2,1)S(1)}, bf16[64,1024]{1,0:T(8,128)(2,1)S(1)}, u32[]{:S(2)}, u32[]{:S(2)}) collective-permute-start(bf16[64,1024]{1,0:T(8,128)(2,1)S(1)} %copy.12), channel_id=1, source_target_pairs={{0,8},{8,16},{16,24},{24,0},{1,9},{9,17},{17,25},{25,1},{2,10},{10... | collective-permute-start | bytes 393224 | tf_op jit(solution)/shard_map/while/body/eval_jaxpr/ppermute | solution.py:10
  31.6 9.4 %collective-permute-start.1 = (f32[64,1024]{1,0:T(8,128)S(1)}, f32[64,1024]{1,0:T(8,128)S(1)}, u32[]{:S(2)}, u32[]{:S(2)}) collective-permute-start(f32[64,1024]{1,0:T(8,128)S(1)} %convolution_add_fusion.4), channel_id=1, source_target_pairs={{0,8},{8,16},{16,24},{24,0},{1,9},{9,17},{17,25},{25,1},{2,10},{10... | collective-permute-start | bytes 786440 | tf_op jit(solution)/shard_map/while/body/eval_jaxpr/ppermute | solution.py:10
  41.0 7.8 %collective-permute-start = (bf16[64,1024]{1,0:T(8,128)(2,1)S(1)}, bf16[64,1024]{1,0:T(8,128)(2,1)S(1)}, u32[]{:S(2)}, u32[]{:S(2)}) collective-permute-start(bf16[64,1024]{1,0:T(8,128)(2,1)S(1)} %copy.12), channel_id=1, source_target_pairs={{0,8},{8,16},{16,24},{24,0},{1,9},{9,17},{17,25},{25,1},{2,10},{10... | collective-permute-start | bytes 393224 | tf_op jit(solution)/shard_map/while/body/eval_jaxpr/ppermute | solution.py:10
  44.1 9.4 %collective-permute-start.1 = (f32[64,1024]{1,0:T(8,128)S(1)}, f32[64,1024]{1,0:T(8,128)S(1)}, u32[]{:S(2)}, u32[]{:S(2)}) collective-permute-start(f32[64,1024]{1,0:T(8,128)S(1)} %convolution_add_fusion.4), channel_id=1, source_target_pairs={{0,8},{8,16},{16,24},{24,0},{1,9},{9,17},{17,25},{25,1},{2,10},{10... | collective-permute-start | bytes 786440 | tf_op jit(solution)/shard_map/while/body/eval_jaxpr/ppermute | solution.py:10
  53.5 7.8 %collective-permute-start = (bf16[64,1024]{1,0:T(8,128)(2,1)S(1)}, bf16[64,1024]{1,0:T(8,128)(2,1)S(1)}, u32[]{:S(2)}, u32[]{:S(2)}) collective-permute-start(bf16[64,1024]{1,0:T(8,128)(2,1)S(1)} %copy.12), channel_id=1, source_target_pairs={{0,8},{8,16},{16,24},{24,0},{1,9},{9,17},{17,25},{25,1},{2,10},{10... | collective-permute-start | bytes 393224 | tf_op jit(solution)/shard_map/while/body/eval_jaxpr/ppermute | solution.py:10
  56.5 9.4 %collective-permute-start.1 = (f32[64,1024]{1,0:T(8,128)S(1)}, f32[64,1024]{1,0:T(8,128)S(1)}, u32[]{:S(2)}, u32[]{:S(2)}) collective-permute-start(f32[64,1024]{1,0:T(8,128)S(1)} %convolution_add_fusion.4), channel_id=1, source_target_pairs={{0,8},{8,16},{16,24},{24,0},{1,9},{9,17},{17,25},{25,1},{2,10},{10... | collective-permute-start | bytes 786440 | tf_op jit(solution)/shard_map/while/body/eval_jaxpr/ppermute | solution.py:10
  65.9 1.1 %copy-start = (f32[256,1024]{1,0:T(8,128)}, f32[256,1024]{1,0:T(8,128)S(1)}, u32[]{:S(2)}) copy-start(f32[256,1024]{1,0:T(8,128)S(1)} %get-tuple-element.141) | copy-start | bytes 3145732
where the time goes:
time: 67.3 us; the launch traced here: 67 us
  waiting for transfers between devices  41.5 us (62%)
  starting transfers between devices  9.21 us (14%)
  matrix products  8.79 us (13%)
  local copies, waits for them, and re-layouts  4.32 us (6%)
  loops' own time  2.52 us (4%)
    ppermute x8, waiting for transfers between devices, shifted_2(): return lax.ppermute(value, axis, pairs)  33.2 us
    all_to_all x1, waiting for transfers between devices, local(): lax.all_to_all(text_emb, 'section', split_axis=0, concat_axis=1, tiled=True)  8.28 us
    dot_general x4, matrix products, cycle_step(): lax.dot_general(cov_piece, panel, (((1,), (1,)), ((), ())), preferred_ele...  6.39 us
    ppermute x8, starting transfers between devices, shifted_2(): return lax.ppermute(value, axis, pairs)  4.94 us
    all_to_all x1, starting transfers between devices, local(): lax.all_to_all(text_emb, 'section', split_axis=0, concat_axis=1, tiled=True)  4.27 us
    another operation x1, loops' own time, local(): lax.scan(cycle_step, (cov_own, start_sum, start_text), jnp.arange(cycle_l...  2.52 us
    dynamic_slice x4, local copies, waits for them, and re-layouts, local(): lax.scan(cycle_step, (cov_own, start_sum, start_text), jnp.arange(cycle_l...  2.32 us
    unnamed x7, local copies, waits for them, and re-layouts  1.94 us
  transfers between devices with their start and end apart: 9, of which 9 were waited for; matrix products, arithmetic and copies ran while one was open for 17% of the time, Pallas kernels for 0%

commit v1 on v0

v1 whole, which is shorter than its diff:
```python
import functools
import jax
import jax.numpy as jnp
from jax import lax
from jax.experimental import pallas as pl
from jax.experimental.pallas import tpu as pltpu
from jax.sharding import PartitionSpec as P

NT = (((1,), (1,)), ((), ()))
TN = (((0,), (0,)), ((), ()))


def hops(count):
    if count & (count - 1) == 0:
        return [[(i, i ^ k) for i in range(count)] for k in range(1, count)]
    return [[(i, (i + k) % count) for i in range(count)] for k in range(1, count)]


def block_of(me, k, count):
    return me ^ k if count & (count - 1) == 0 else (me - k + count) % count


def block_to(me, k, count):
    return me ^ k if count & (count - 1) == 0 else (me + k) % count


def coeff_kernel(count, rows, scale_ref, bias_ref, labels_ref, panel_ref, *refs):
    covs, (coeff_ref, own_ref), parts = refs[:count], refs[count:count + 2], refs[count + 2:]
    me = lax.axis_index("blk")
    scale, bias = scale_ref[0], bias_ref[0]
    panel = panel_ref[...]
    labels = labels_ref[...]
    for k in range(count):
        logits = scale * lax.dot_general(covs[k][...], panel, NT, preferred_element_type=jnp.float32) + bias
        ids = block_of(me, k, count) * rows + lax.broadcasted_iota(jnp.int32, logits.shape, 0)
        positive = (labels == ids).astype(jnp.float32)
        coeff = (scale * (jax.nn.sigmoid(logits) - positive)).astype(jnp.bfloat16)
        coeff_ref[k * rows:(k + 1) * rows, :] = coeff
        term = jnp.dot(coeff, panel, preferred_element_type=jnp.float32)
        if k == 0:
            own_ref[...] = term
        else:
            parts[k - 1][...] = term.astype(jnp.bfloat16)


def text_kernel(count, rows, coeff_ref, *refs):
    covs, out_ref = refs[:count], refs[count]
    total = None
    for k in range(count):
        term = lax.dot_general(coeff_ref[k * rows:(k + 1) * rows, :], covs[k][...], TN, preferred_element_type=jnp.float32)
        total = term if total is None else total + term
    out_ref[...] = total


def local(text_emb, covariate, labels, logit_scale, logit_bias):
    count = lax.axis_size("blk")
    rows, width = covariate.shape[1:]
    covs = [covariate[0]] + [lax.ppermute(covariate[0], "blk", p) for p in hops(count)]
    panel = lax.all_to_all(text_emb, "section", 0, 0, tiled=True).reshape(-1, width)
    texts = panel.shape[0]
    vmem = pl.BlockSpec(memory_space=pltpu.VMEM)
    smem = pl.BlockSpec(memory_space=pltpu.SMEM)
    coeff, own, *parts = pl.pallas_call(
        functools.partial(coeff_kernel, count, rows),
        out_shape=[jax.ShapeDtypeStruct((count * rows, texts), jnp.bfloat16), jax.ShapeDtypeStruct((rows, width), jnp.float32)]
        + [jax.ShapeDtypeStruct((rows, width), jnp.bfloat16)] * (count - 1),
        in_specs=[smem, smem] + [vmem] * (2 + count),
        out_specs=[vmem] * (1 + count),
        compiler_params=pltpu.CompilerParams(vmem_limit_bytes=32 * 2**20),
        cost_estimate=pl.CostEstimate(flops=4 * count * rows * texts * width, bytes_accessed=2**20, transcendentals=0),
        name="coeff",
    )(logit_scale, logit_bias, labels, panel, *covs)
    got = [lax.ppermute(part, "blk", p) for part, p in zip(parts, hops(count))]
    text_grad = pl.pallas_call(
        functools.partial(text_kernel, count, rows),
        out_shape=jax.ShapeDtypeStruct((texts, width), jnp.float32),
        in_specs=[vmem] * (1 + count),
        out_specs=vmem,
        compiler_params=pltpu.CompilerParams(vmem_limit_bytes=32 * 2**20),
        cost_estimate=pl.CostEstimate(flops=2 * count * rows * texts * width, bytes_accessed=2**20, transcendentals=0),
        name="text_grad",
    )(coeff, *covs)
    total = own
    for part in got:
        total = total + part.astype(jnp.float32)
    return text_grad[None], total[None]


def solution(mesh):
    return jax.shard_map(
        local,
        mesh=mesh,
        in_specs=(
            P(None, ("blk", "section"), None),
            P("section", "blk", None),
            P("section", "blk"),
            P(),
            P(),
        ),
        out_specs=(P("section", "blk", None), P("section", "blk", None)),
        check_vma=False,
    )
```

time: 67.3 us -> 37.6 us (0.56)
  the two profiles are of different devices: /device:TPU:2 before, /device:TPU:0 now
where the time goes in v1:
time: 37.6 us; the launch traced here: 37.4 us
  waiting for transfers between devices  16.6 us (44%)
  starting transfers between devices  14.2 us (38%)
  Pallas kernels  3.9 us (10%)
  between operations  1.97 us (5%)
  other arithmetic  0.76 us (2%)
    ppermute x3, waiting for transfers between devices, local(): lax.ppermute(covariate[0], 'blk', p)  9.58 us
    ppermute x3, waiting for transfers between devices, local(): got = [lax.ppermute(part, 'blk', p) for part, p in zip(parts, hops(count))]  6.97 us
    all_to_all x1, starting transfers between devices, local(): lax.all_to_all(text_emb, 'section', 0, 0, tiled=True).reshape(-1, width)  5.31 us
    ppermute x3, starting transfers between devices, local(): lax.ppermute(covariate[0], 'blk', p)  4.45 us
    ppermute x3, starting transfers between devices, local(): got = [lax.ppermute(part, 'blk', p) for part, p in zip(parts, hops(count))]  4.44 us
    pallas_call x1, Pallas kernels, local(): pl.pallas_call(functools.partial(coeff_kernel, count, rows), out_shape=[j...  2.21 us
    pallas_call x1, Pallas kernels, local(): pl.pallas_call(functools.partial(text_kernel, count, rows), out_shape=jax...  1.69 us
    broadcast_in_dim x1, other arithmetic, local(): return (text_grad[None], total[None])  0.76 us
  transfers between devices with their start and end apart: 7, of which 4 were waited for; matrix products, arithmetic and copies ran while one was open for 0% of the time, Pallas kernels for 5%

profile of v1, /device:TPU:0, one launch (start us, length us, event | category | flops | bytes accessed | tf_op | source)
XLA Modules:
  0.0 37.4 jit_solution(6236661068697592925)
XLA Ops:
  0.6 0.0 copy-start
  0.6 5.3 %all-to-all-start = ((bf16[8,32,1024]{2,1,0:T(8,128)(2,1)}), bf16[8,32,1024]{2,1,0:T(8,128)(2,1)S(1)}, u32[]{:S(2)}, u32[]{:S(2)}) async-start(bf16[8,32,1024]{2,1,0:T(8,128)(2,1)} %param.5), calls=%async_computation | async-start | bytes 1048576 | tf_op jit(solution)/shard_map/all_to_all | solution.py:59
  6.0 0.0 copy-done
  6.0 3.7 %collective-permute-start.2 = (bf16[64,1024]{1,0:T(8,128)(2,1)S(1)}, bf16[64,1024]{1,0:T(8,128)(2,1)S(1)}, u32[]{:S(2)}, u32[]{:S(2)}) collective-permute-start(bf16[64,1024]{1,0:T(8,128)(2,1)S(1)} %bitcast.6), channel_id=1, source_target_pairs={{0,24},{8,16},{16,8},{24,0},{1,25},{9,17},{17,9},{25,1},{2,26},{10... | collective-permute-start | bytes 393224 | tf_op jit(solution)/shard_map/ppermute | solution.py:58
  9.6 0.0 collective-permute-start.1
  9.6 0.8 %collective-permute-start = (bf16[64,1024]{1,0:T(8,128)(2,1)S(1)}, bf16[64,1024]{1,0:T(8,128)(2,1)S(1)}, u32[]{:S(2)}, u32[]{:S(2)}) collective-permute-start(bf16[64,1024]{1,0:T(8,128)(2,1)S(1)} %bitcast.8), channel_id=1, source_target_pairs={{0,8},{8,0},{16,24},{24,16},{1,9},{9,1},{17,25},{25,17},{2,10},{10... | collective-permute-start | bytes 393224 | tf_op jit(solution)/shard_map/ppermute | solution.py:58
  11.7 0.0 copy-start.1
  11.7 2.5 %collective-permute-done.2.refs_3_ = bf16[64,1024]{1,0:T(8,128)(2,1)S(1)} collective-permute-done((bf16[64,1024]{1,0:T(8,128)(2,1)S(1)}, bf16[64,1024]{1,0:T(8,128)(2,1)S(1)}, u32[]{:S(2)}, u32[]{:S(2)}) %collective-permute-start.2) | collective-permute-done | bytes 131104 | tf_op jit(solution)/shard_map/ppermute | solution.py:58
  14.2 7.1 %collective-permute-done.1.refs_2_ = bf16[64,1024]{1,0:T(8,128)(2,1)S(1)} collective-permute-done((bf16[64,1024]{1,0:T(8,128)(2,1)S(1)}, bf16[64,1024]{1,0:T(8,128)(2,1)S(1)}, u32[]{:S(2)}, u32[]{:S(2)}) %collective-permute-start.1) | collective-permute-done | bytes 131104 | tf_op jit(solution)/shard_map/ppermute | solution.py:58
  21.3 0.0 collective-permute-done.refs_1_
  21.3 0.0 all-to-all-done
  21.3 0.0 copy-done.1
  21.3 2.2 %coeff.1 = (bf16[256,256]{1,0:T(8,128)(2,1)S(1)}, f32[64,1024]{1,0:T(8,128)S(1)}, bf16[64,1024]{1,0:T(8,128)(2,1)S(1)}, bf16[64,1024]{1,0:T(8,128)(2,1)S(1)}, bf16[64,1024]{1,0:T(8,128)(2,1)S(1)}) custom-call(f32[1]{0:T(128)S(6)} %copy.7.scale_ref, f32[1]{0:T(128)S(6)} %copy.8.bias_ref, s32[1,256]{1,0:T(1,128)S(1)} %copy-done.1, ...), custom_call_target="tpu_custom_call" | custom-call | flops 268435456 | bytes 1048576 | tf_op jit(solution)/shard_map/coeff/pallas_call | solution.py:63
  23.5 0.1 collective-permute-start.3
  23.6 3.0 %collective-permute-start.4 = (bf16[64,1024]{1,0:T(8,128)(2,1)S(1)}, bf16[64,1024]{1,0:T(8,128)(2,1)S(1)}, u32[]{:S(2)}, u32[]{:S(2)}) collective-permute-start(bf16[64,1024]{1,0:T(8,128)(2,1)S(1)} %get-tuple-element.10), channel_id=1, source_target_pairs={{0,16},{8,24},{16,0},{24,8},{1,17},{9,25},{17,1},{25,9},{2,18},{10... | collective-permute-start | bytes 393224 | tf_op jit(solution)/shard_map/ppermute | solution.py:73
  26.6 1.3 %collective-permute-start.5 = (bf16[64,1024]{1,0:T(8,128)(2,1)S(1)}, bf16[64,1024]{1,0:T(8,128)(2,1)S(1)}, u32[]{:S(2)}, u32[]{:S(2)}) collective-permute-start(bf16[64,1024]{1,0:T(8,128)(2,1)S(1)} %get-tuple-element.11), channel_id=1, source_target_pairs={{0,24},{8,16},{16,8},{24,0},{1,25},{9,17},{17,9},{25,1},{2,26},{10... | collective-permute-start | bytes 393224 | tf_op jit(solution)/shard_map/ppermute | solution.py:73
  28.0 1.7 %text_grad.1 = f32[256,1024]{1,0:T(8,128)} custom-call(bf16[256,256]{1,0:T(8,128)(2,1)S(1)} %get-tuple-element.7.coeff_ref, bf16[64,1024]{1,0:T(8,128)(2,1)S(1)} %bitcast.10, bf16[64,1024]{1,0:T(8,128)(2,1)S(1)} %collective-permute-done.refs_1_, bf16[64,1024]{1,0:T(8,128)(2,1)S(1)} %collective-permute-done.1.refs_2_, ...), custom_call_target="tpu_custom_call" | custom-call | flops 134217728 | bytes 1048576 | tf_op jit(solution)/shard_map/text_grad/pallas_call | solution.py:74
  29.7 1.0 %collective-permute-done.3 = bf16[64,1024]{1,0:T(8,128)(2,1)S(1)} collective-permute-done((bf16[64,1024]{1,0:T(8,128)(2,1)S(1)}, bf16[64,1024]{1,0:T(8,128)(2,1)S(1)}, u32[]{:S(2)}, u32[]{:S(2)}) %collective-permute-start.3) | collective-permute-done | bytes 131104 | tf_op jit(solution)/shard_map/ppermute | solution.py:73
  30.7 6.0 %collective-permute-done.4 = bf16[64,1024]{1,0:T(8,128)(2,1)S(1)} collective-permute-done((bf16[64,1024]{1,0:T(8,128)(2,1)S(1)}, bf16[64,1024]{1,0:T(8,128)(2,1)S(1)}, u32[]{:S(2)}, u32[]{:S(2)}) %collective-permute-start.4) | collective-permute-done | bytes 131104 | tf_op jit(solution)/shard_map/ppermute | solution.py:73
  36.6 0.0 collective-permute-done.5
  36.6 0.8 %add_bitcast_fusion = f32[1,64,1024]{2,1,0:T(8,128)} fusion(bf16[64,1024]{1,0:T(8,128)(2,1)S(1)} %collective-permute-done.5, bf16[64,1024]{1,0:T(8,128)(2,1)S(1)} %collective-permute-done.4, f32[64,1024]{1,0:T(8,128)S(1)} %get-tuple-element.8, bf16[64,1024]{1,0:T(8,128)(2,1)S(1)} %collective-permute-done.3), kind=kLoop, calls=%fused_computation | loop fusion | flops 393216 | bytes 917504 | tf_op jit(solution)/shard_map/broadcast_in_dim | solution.py:86
Async XLA Ops:
  0.6 5.3 %copy-start = (bf16[1,64,1024]{2,1,0:T(8,128)(2,1)S(1)}, bf16[1,64,1024]{2,1,0:T(8,128)(2,1)}, u32[]{:S(2)}) copy-start(bf16[1,64,1024]{2,1,0:T(8,128)(2,1)} %param.6) | copy-start | bytes 393220
  0.6 20.7 %all-to-all-start = ((bf16[8,32,1024]{2,1,0:T(8,128)(2,1)}), bf16[8,32,1024]{2,1,0:T(8,128)(2,1)S(1)}, u32[]{:S(2)}, u32[]{:S(2)}) async-start(bf16[8,32,1024]{2,1,0:T(8,128)(2,1)} %param.5), calls=%async_computation | async-start | bytes 1048576 | tf_op jit(solution)/shard_map/all_to_all | solution.py:59
  6.0 8.3 %collective-permute-start.2 = (bf16[64,1024]{1,0:T(8,128)(2,1)S(1)}, bf16[64,1024]{1,0:T(8,128)(2,1)S(1)}, u32[]{:S(2)}, u32[]{:S(2)}) collective-permute-start(bf16[64,1024]{1,0:T(8,128)(2,1)S(1)} %bitcast.6), channel_id=1, source_target_pairs={{0,24},{8,16},{16,8},{24,0},{1,25},{9,17},{17,9},{25,1},{2,26},{10... | collective-permute-start | bytes 393224 | tf_op jit(solution)/shard_map/ppermute | solution.py:58
  9.6 11.7 %collective-permute-start.1 = (bf16[64,1024]{1,0:T(8,128)(2,1)S(1)}, bf16[64,1024]{1,0:T(8,128)(2,1)S(1)}, u32[]{:S(2)}, u32[]{:S(2)}) collective-permute-start(bf16[64,1024]{1,0:T(8,128)(2,1)S(1)} %bitcast.7), channel_id=1, source_target_pairs={{0,16},{8,24},{16,0},{24,8},{1,17},{9,25},{17,1},{25,9},{2,18},{10... | collective-permute-start | bytes 393224 | tf_op jit(solution)/shard_map/ppermute | solution.py:58
  9.6 11.7 %collective-permute-start = (bf16[64,1024]{1,0:T(8,128)(2,1)S(1)}, bf16[64,1024]{1,0:T(8,128)(2,1)S(1)}, u32[]{:S(2)}, u32[]{:S(2)}) collective-permute-start(bf16[64,1024]{1,0:T(8,128)(2,1)S(1)} %bitcast.8), channel_id=1, source_target_pairs={{0,8},{8,0},{16,24},{24,16},{1,9},{9,1},{17,25},{25,17},{2,10},{10... | collective-permute-start | bytes 393224 | tf_op jit(solution)/shard_map/ppermute | solution.py:58
  11.7 9.6 %copy-start.1 = (s32[1,256]{1,0:T(1,128)S(1)}, s32[1,256]{1,0:T(1,128)}, u32[]{:S(2)}) copy-start(s32[1,256]{1,0:T(1,128)} %labels_ref.1) | copy-start | bytes 3076
  23.5 7.1 %collective-permute-start.3 = (bf16[64,1024]{1,0:T(8,128)(2,1)S(1)}, bf16[64,1024]{1,0:T(8,128)(2,1)S(1)}, u32[]{:S(2)}, u32[]{:S(2)}) collective-permute-start(bf16[64,1024]{1,0:T(8,128)(2,1)S(1)} %get-tuple-element.9), channel_id=1, source_target_pairs={{0,8},{8,0},{16,24},{24,16},{1,9},{9,1},{17,25},{25,17},{2,10},{10... | collective-permute-start | bytes 393224 | tf_op jit(solution)/shard_map/ppermute | solution.py:73
  23.6 13.0 %collective-permute-start.4 = (bf16[64,1024]{1,0:T(8,128)(2,1)S(1)}, bf16[64,1024]{1,0:T(8,128)(2,1)S(1)}, u32[]{:S(2)}, u32[]{:S(2)}) collective-permute-start(bf16[64,1024]{1,0:T(8,128)(2,1)S(1)} %get-tuple-element.10), channel_id=1, source_target_pairs={{0,16},{8,24},{16,0},{24,8},{1,17},{9,25},{17,1},{25,9},{2,18},{10... | collective-permute-start | bytes 393224 | tf_op jit(solution)/shard_map/ppermute | solution.py:73
  26.6 10.0 %collective-permute-start.5 = (bf16[64,1024]{1,0:T(8,128)(2,1)S(1)}, bf16[64,1024]{1,0:T(8,128)(2,1)S(1)}, u32[]{:S(2)}, u32[]{:S(2)}) collective-permute-start(bf16[64,1024]{1,0:T(8,128)(2,1)S(1)} %get-tuple-element.11), channel_id=1, source_target_pairs={{0,24},{8,16},{16,8},{24,0},{1,25},{9,17},{17,9},{25,1},{2,26},{10... | collective-permute-start | bytes 393224 | tf_op jit(solution)/shard_map/ppermute | solution.py:73

commit v2 on v0

v2 whole, which is shorter than its diff:
```python
import functools

import jax
import jax.numpy as jnp
from jax import lax
from jax.experimental import pallas as pl
from jax.experimental.pallas import tpu as pltpu
from jax.sharding import PartitionSpec as P

NT = (((1,), (1,)), ((), ()))
TN = (((0,), (0,)), ((), ()))
VMEM = pl.BlockSpec(memory_space=pltpu.VMEM)
ANY = pl.BlockSpec(memory_space=pl.ANY)
MIB = 2**20
BF16, F32 = jnp.bfloat16, jnp.float32
SHAPE = jax.ShapeDtypeStruct
LONG = 10**11


def is_power(count):
    return count & (count - 1) == 0


def exchange(value, axis, k):
    count = lax.axis_size(axis)
    return lax.ppermute(value, axis, [(i, i ^ k if is_power(count) else (i + k) % count) for i in range(count)])


def source_block(me, k, count):
    return me ^ k if is_power(count) else lax.rem(me - k + count, jnp.int32(count))


def span(slot, rows):
    return pl.ds(pl.multiple_of(slot * rows, rows), rows)


def select_kernel(chips, *refs):
    core = lax.axis_index("section") % 2
    out = refs[-1]
    for k in range(chips):
        out[k] = refs[k][1 - core]


def pile_kernel(*refs):
    *parts, out = refs
    rows = parts[0].shape[0]
    for k, part in enumerate(parts):
        out[k * rows:(k + 1) * rows, :] = part[...]


def coeff_kernel(count, chips, params_ref, covs_ref, *refs):
    texts, (coeff_ref, own_ref, *part_refs, panel, prod) = refs[:chips + 1], refs[chips + 1:]
    rows = covs_ref.shape[0] // count
    if chips:
        section = lax.axis_index("section")
        chip, core = section // 2, section % 2
        piece = texts[0].shape[1]
        for k in range(chips):
            panel[span((chip ^ k) * 2 + core, piece), :] = texts[k][core]
            panel[span((chip ^ k) * 2 + 1 - core, piece), :] = texts[chips][k]
        text = panel[...]
    else:
        text = texts[0][...]
    labels, scale, bias = params_ref[0:1, :], params_ref[1:2, :], params_ref[2:3, :]
    logits = scale * lax.dot_general(covs_ref[...], text, NT, preferred_element_type=F32) + bias
    me = lax.axis_index("blk")
    row = lax.broadcasted_iota(jnp.int32, (rows, 1), 0)
    ids = jnp.concatenate([source_block(me, k, count) * rows + row for k in range(count)], axis=0)
    positive = (labels == ids.astype(F32)).astype(F32)
    coeff = (scale * (jax.nn.sigmoid(logits) - positive)).astype(BF16)
    coeff_ref[...] = coeff
    prod[...] = jnp.dot(coeff, text, preferred_element_type=F32)
    own_ref[...] = prod[0:rows, :]
    for k, ref in enumerate(part_refs, 1):
        ref[...] = prod[k * rows:(k + 1) * rows, :].astype(BF16)


def text_kernel(coeff_ref, covs_ref, out_ref):
    out_ref[...] = lax.dot_general(coeff_ref[...], covs_ref[...], TN, preferred_element_type=F32)


def call(kernel, name, out_shape, args, flops, scratch=(), limit=8, specs=None):
    many = isinstance(out_shape, list)
    return pl.pallas_call(
        kernel,
        out_shape=out_shape,
        in_specs=specs or [VMEM] * len(args),
        out_specs=[VMEM] * len(out_shape) if many else VMEM,
        scratch_shapes=list(scratch),
        compiler_params=pltpu.CompilerParams(vmem_limit_bytes=limit * MIB),
        cost_estimate=pl.CostEstimate(flops=flops, bytes_accessed=MIB, transcendentals=0),
        name=name,
    )(*args)


def fetch_covs(own, count):
    if count != 4:
        return [own] + [exchange(own, "blk", k) for k in range(1, count)], []
    far = exchange(own, "blk", 3)
    return [own, exchange(own, "blk", 1), exchange(far, "blk", 1), far], [far]


def fetch_texts(text_emb, early):
    groups, piece, width = text_emb.shape
    if not is_power(groups) or piece % 16:
        return [lax.all_to_all(text_emb, "section", 0, 0, tiled=True).reshape(-1, width)], 0
    chips = groups // 2
    chip = lax.axis_index("section") // 2
    by_chip = text_emb.reshape(chips, 2, piece, width)
    parts = [lax.dynamic_index_in_dim(by_chip, chip ^ k, 0, keepdims=False) for k in range(chips)]
    texts = parts[:1] + [exchange(parts[k], "section", 2 * k) for k in range(1, chips)]
    other = call(
        functools.partial(select_kernel, chips), "select", SHAPE((chips, piece, width), BF16),
        texts + early, LONG, specs=[VMEM] * chips + [ANY] * len(early))
    return texts + [exchange(other, "section", 1)], chips


def local(text_emb, covariate, labels, logit_scale, logit_bias):
    count = lax.axis_size("blk")
    rows, width = covariate.shape[1:]
    n_text = labels.shape[1]
    params = jnp.concatenate(
        [labels.astype(F32), jnp.broadcast_to(logit_scale[None], labels.shape), jnp.broadcast_to(logit_bias[None], labels.shape)])
    params = jnp.pad(params, ((0, 5), (0, 0)))
    covs, early = fetch_covs(covariate[0], count)
    texts, chips = fetch_texts(text_emb, early + [params])
    pile = call(pile_kernel, "pile", SHAPE((count * rows, width), BF16), covs, LONG)
    flops = 2 * count * rows * n_text * width
    coeff, own, *parts = call(
        functools.partial(coeff_kernel, count, chips), "coeff",
        [SHAPE((count * rows, n_text), BF16), SHAPE((rows, width), F32)] + [SHAPE((rows, width), BF16)] * (count - 1),
        [params, pile] + texts, 2 * flops, limit=16 if count == 4 else 40,
        scratch=[pltpu.VMEM((n_text, width) if chips else (8, 128), BF16), pltpu.VMEM((count * rows, width), F32)])
    got = [exchange(part, "blk", k if is_power(count) else -k) for k, part in enumerate(parts, 1)]
    text_grad = call(text_kernel, "text_grad", SHAPE((n_text, width), F32), [coeff, pile], flops, limit=16)
    total = own
    for part in got:
        total = total + part.astype(F32)
    return text_grad[None], total[None]


def solution(mesh):
    return jax.shard_map(
        local,
        mesh=mesh,
        in_specs=(
            P(None, ("blk", "section"), None),
            P("section", "blk", None),
            P("section", "blk"),
            P(),
            P(),
        ),
        out_specs=(P("section", "blk", None), P("section", "blk", None)),
        check_vma=False,
    )
```

time: 67.3 us -> 33.4 us (0.50)
  the two profiles are of different devices: /device:TPU:2 before, /device:TPU:0 now
where the time goes in v2:
time: 33.4 us; the launch traced here: 33.2 us
  starting transfers between devices  15.4 us (46%)
  waiting for transfers between devices  10.9 us (33%)
  Pallas kernels  2.18 us (7%)
  between operations  1.98 us (6%)
  local copies, waits for them, and re-layouts  1.89 us (6%)
  other arithmetic  0.85 us (3%)
    ppermute x10, starting transfers between devices, exchange(): lax.ppermute(value, axis, [(i, i ^ k if is_power(count) else (i + k) % co...  15.4 us
    ppermute x10, waiting for transfers between devices, exchange(): lax.ppermute(value, axis, [(i, i ^ k if is_power(count) else (i + k) % co...  10.9 us
    pallas_call x4, Pallas kernels, call(): pl.pallas_call(kernel, out_shape=out_shape, in_specs=specs or [VMEM] * le...  2.18 us
    squeeze x1, local copies, waits for them, and re-layouts, fetch_texts(): lax.dynamic_index_in_dim(by_chip, chip ^ k, 0, keepdims=False)  1.13 us
    broadcast_in_dim x1, other arithmetic, local(): return (text_grad[None], total[None])  0.77 us
  transfers between devices with their start and end apart: 10, of which 5 were waited for; matrix products, arithmetic and copies ran while one was open for 4% of the time, Pallas kernels for 4%

profile of v2, /device:TPU:0, one launch (start us, length us, event | category | flops | bytes accessed | tf_op | source)
XLA Modules:
  0.0 33.2 jit_solution(4307696848308547133)
XLA Ops:
  0.6 5.1 %collective-permute-start.1 = (bf16[64,1024]{1,0:T(8,128)(2,1)}, bf16[64,1024]{1,0:T(8,128)(2,1)S(1)}, u32[]{:S(2)}, u32[]{:S(2)}) collective-permute-start(bf16[64,1024]{1,0:T(8,128)(2,1)} %bitcast.15), channel_id=1, source_target_pairs={{0,24},{8,16},{16,8},{24,0},{1,25},{9,17},{17,9},{25,1},{2,26},{10... | collective-permute-start | bytes 393224 | tf_op jit(solution)/shard_map/ppermute | solution.py:26
  5.7 0.0 collective-permute-start
  5.7 1.1 %dynamic-slice_bitcast_fusion = (bf16[2,32,1024]{2,1,0:T(8,128)(2,1)S(1)}, bf16[2,32,1024]{2,1,0:T(8,128)(2,1)S(1)}, bf16[2,32,1024]{2,1,0:T(8,128)(2,1)S(1)}, bf16[2,32,1024]{2,1,0:T(8,128)(2,1)S(1)}) fusion(bf16[4,2,32,1024]{3,2,1,0:T(8,128)(2,1)} %bitcast.19, s32[]{:T(128)S(6)} %select_n.22, s32[]{:T(128)S(6)} %select_n.21, s32[]{:T(128)S(6)} %select_n.20, ...), kind=kLoop, calls=%fused_computation.1 | loop fusion | bytes 1048592 | tf_op jit(solution)/shard_map/jit(dynamic_index_in_dim)/squeeze | solution.py:110
  6.9 2.5 %collective-permute-start.5 = (bf16[2,32,1024]{2,1,0:T(8,128)(2,1)S(1)}, bf16[2,32,1024]{2,1,0:T(8,128)(2,1)S(1)}, u32[]{:S(2)}, u32[]{:S(2)}) collective-permute-start(bf16[2,32,1024]{2,1,0:T(8,128)(2,1)S(1)} %get-tuple-element.12), channel_id=1, source_target_pairs={{0,6},{1,7},{2,4},{3,5},{4,2},{5,3},{6,0},{7,1},{8,14},{9,15},{10,... | collective-permute-start | bytes 393224 | tf_op jit(solution)/shard_map/ppermute | solution.py:26
  9.4 0.5 %collective-permute-start.4 = (bf16[2,32,1024]{2,1,0:T(8,128)(2,1)S(1)}, bf16[2,32,1024]{2,1,0:T(8,128)(2,1)S(1)}, u32[]{:S(2)}, u32[]{:S(2)}) collective-permute-start(bf16[2,32,1024]{2,1,0:T(8,128)(2,1)S(1)} %get-tuple-element.13), channel_id=1, source_target_pairs={{0,4},{1,5},{2,6},{3,7},{4,0},{5,1},{6,2},{7,3},{8,12},{9,13},{10,... | collective-permute-start | bytes 393224 | tf_op jit(solution)/shard_map/ppermute | solution.py:26
  9.9 0.5 %collective-permute-start.3 = (bf16[2,32,1024]{2,1,0:T(8,128)(2,1)S(1)}, bf16[2,32,1024]{2,1,0:T(8,128)(2,1)S(1)}, u32[]{:S(2)}, u32[]{:S(2)}) collective-permute-start(bf16[2,32,1024]{2,1,0:T(8,128)(2,1)S(1)} %get-tuple-element.14), channel_id=1, source_target_pairs={{0,2},{1,3},{2,0},{3,1},{4,6},{5,7},{6,4},{7,5},{8,10},{9,11},{10,... | collective-permute-start | bytes 393224 | tf_op jit(solution)/shard_map/ppermute | solution.py:26
  11.7 0.1 pad.6.clone
  11.8 0.0 copy-start.1
  11.8 0.1 pad.7.clone
  11.9 0.6 %copy-done.1 = s32[1,256]{1,0:T(1,128)S(1)} copy-done((s32[1,256]{1,0:T(1,128)S(1)}, s32[1,256]{1,0:T(1,128)}, u32[]{:S(2)}) %copy-start.1) | copy-done | bytes 1048
  12.5 0.1 maximum_maximum_fusion
  12.6 0.0 collective-permute-done.1.refs_3_.refs_4_
  12.6 2.1 %collective-permute-start.2 = (bf16[64,1024]{1,0:T(8,128)(2,1)S(1)}, bf16[64,1024]{1,0:T(8,128)(2,1)S(1)}, u32[]{:S(2)}, u32[]{:S(2)}) collective-permute-start(bf16[64,1024]{1,0:T(8,128)(2,1)S(1)} %collective-permute-done.1.refs_3_.refs_4_), channel_id=1, source_target_pairs={{0,8},{8,0},{16,24},{24,16},{1,9},{9,1},{17,25},{25,17},{2,10},{10... | collective-permute-start | bytes 393224 | tf_op jit(solution)/shard_map/ppermute | solution.py:26
  14.7 0.0 collective-permute-done.5.refs_3_
  14.7 0.9 %collective-permute-done.4.refs_2_ = bf16[2,32,1024]{2,1,0:T(8,128)(2,1)S(1)} collective-permute-done((bf16[2,32,1024]{2,1,0:T(8,128)(2,1)S(1)}, bf16[2,32,1024]{2,1,0:T(8,128)(2,1)S(1)}, u32[]{:S(2)}, u32[]{:S(2)}) %collective-permute-start.4) | collective-permute-done | bytes 131104 | tf_op jit(solution)/shard_map/ppermute | solution.py:26
  15.6 0.1 collective-permute-done.3.refs_1_
  15.7 0.0 copy-start
  15.7 0.1 collective-permute-start.6
  15.8 0.0 collective-permute-done.refs_1_
  15.8 1.8 %collective-permute-done.2.refs_2_ = bf16[64,1024]{1,0:T(8,128)(2,1)S(1)} collective-permute-done((bf16[64,1024]{1,0:T(8,128)(2,1)S(1)}, bf16[64,1024]{1,0:T(8,128)(2,1)S(1)}, u32[]{:S(2)}, u32[]{:S(2)}) %collective-permute-start.2) | collective-permute-done | bytes 131104 | tf_op jit(solution)/shard_map/ppermute | solution.py:26
  17.6 0.0 copy-done
  17.7 0.0 collective-permute-done.6.refs_4_
  17.7 0.8 %coeff.1 = (bf16[256,256]{1,0:T(8,128)(2,1)S(1)}, f32[64,1024]{1,0:T(8,128)S(1)}, bf16[64,1024]{1,0:T(8,128)(2,1)S(1)}, bf16[64,1024]{1,0:T(8,128)(2,1)S(1)}, bf16[64,1024]{1,0:T(8,128)(2,1)S(1)}) custom-call(f32[8,256]{1,0:T(8,128)S(1)} %pad.4.refs_5_.params_ref, bf16[256,1024]{1,0:T(8,128)(2,1)S(1)} %pile.1.covs_ref, ...), custom_call_target="tpu_custom_call" | custom-call | flops 268435456 | bytes 1048576 | tf_op jit(solution)/shard_map/coeff/pallas_call | solution.py:84
  18.5 2.1 %collective-permute-start.7 = (bf16[64,1024]{1,0:T(8,128)(2,1)S(1)}, bf16[64,1024]{1,0:T(8,128)(2,1)S(1)}, u32[]{:S(2)}, u32[]{:S(2)}) collective-permute-start(bf16[64,1024]{1,0:T(8,128)(2,1)S(1)} %get-tuple-element.9), channel_id=1, source_target_pairs={{0,8},{8,0},{16,24},{24,16},{1,9},{9,1},{17,25},{25,17},{2,10},{10... | collective-permute-start | bytes 393224 | tf_op jit(solution)/shard_map/ppermute | solution.py:26
  20.6 0.0 collective-permute-start.8
  20.6 2.4 %collective-permute-start.9 = (bf16[64,1024]{1,0:T(8,128)(2,1)S(1)}, bf16[64,1024]{1,0:T(8,128)(2,1)S(1)}, u32[]{:S(2)}, u32[]{:S(2)}) collective-permute-start(bf16[64,1024]{1,0:T(8,128)(2,1)S(1)} %get-tuple-element.11), channel_id=1, source_target_pairs={{0,24},{8,16},{16,8},{24,0},{1,25},{9,17},{17,9},{25,1},{2,26},{10... | collective-permute-start | bytes 393224 | tf_op jit(solution)/shard_map/ppermute | solution.py:26
  23.0 1.3 %text_grad.1 = f32[256,1024]{1,0:T(8,128)} custom-call(bf16[256,256]{1,0:T(8,128)(2,1)S(1)} %get-tuple-element.7.coeff_ref, bf16[256,1024]{1,0:T(8,128)(2,1)S(1)} %pile.1.covs_ref), custom_call_target="tpu_custom_call" | custom-call | flops 134217728 | bytes 1048576 | tf_op jit(solution)/shard_map/text_grad/pallas_call | solution.py:84
  24.3 0.2 collective-permute-done.7
  24.5 7.9 %collective-permute-done.8 = bf16[64,1024]{1,0:T(8,128)(2,1)S(1)} collective-permute-done((bf16[64,1024]{1,0:T(8,128)(2,1)S(1)}, bf16[64,1024]{1,0:T(8,128)(2,1)S(1)}, u32[]{:S(2)}, u32[]{:S(2)}) %collective-permute-start.8) | collective-permute-done | bytes 131104 | tf_op jit(solution)/shard_map/ppermute | solution.py:26
  32.4 0.0 collective-permute-done.9
  32.4 0.8 %add_bitcast_fusion = f32[1,64,1024]{2,1,0:T(8,128)} fusion(bf16[64,1024]{1,0:T(8,128)(2,1)S(1)} %collective-permute-done.9, bf16[64,1024]{1,0:T(8,128)(2,1)S(1)} %collective-permute-done.8, f32[64,1024]{1,0:T(8,128)S(1)} %get-tuple-element.8, bf16[64,1024]{1,0:T(8,128)(2,1)S(1)} %collective-permute-done.7), kind=kLoop, calls=%fused_computation | loop fusion | flops 393216 | bytes 917504 | tf_op jit(solution)/shard_map/broadcast_in_dim | solution.py:139
  (4 shorter events, 0.1 us)
Async XLA Ops:
  0.6 11.9 %collective-permute-start.1 = (bf16[64,1024]{1,0:T(8,128)(2,1)}, bf16[64,1024]{1,0:T(8,128)(2,1)S(1)}, u32[]{:S(2)}, u32[]{:S(2)}) collective-permute-start(bf16[64,1024]{1,0:T(8,128)(2,1)} %bitcast.15), channel_id=1, source_target_pairs={{0,24},{8,16},{16,8},{24,0},{1,25},{9,17},{17,9},{25,1},{2,26},{10... | collective-permute-start | bytes 393224 | tf_op jit(solution)/shard_map/ppermute | solution.py:26
  5.7 10.0 %collective-permute-start = (bf16[64,1024]{1,0:T(8,128)(2,1)}, bf16[64,1024]{1,0:T(8,128)(2,1)S(1)}, u32[]{:S(2)}, u32[]{:S(2)}) collective-permute-start(bf16[64,1024]{1,0:T(8,128)(2,1)} %bitcast.16), channel_id=1, source_target_pairs={{0,8},{8,0},{16,24},{24,16},{1,9},{9,1},{17,25},{25,17},{2,10},{10... | collective-permute-start | bytes 393224 | tf_op jit(solution)/shard_map/ppermute | solution.py:26
  6.9 7.8 %collective-permute-start.5 = (bf16[2,32,1024]{2,1,0:T(8,128)(2,1)S(1)}, bf16[2,32,1024]{2,1,0:T(8,128)(2,1)S(1)}, u32[]{:S(2)}, u32[]{:S(2)}) collective-permute-start(bf16[2,32,1024]{2,1,0:T(8,128)(2,1)S(1)} %get-tuple-element.12), channel_id=1, source_target_pairs={{0,6},{1,7},{2,4},{3,5},{4,2},{5,3},{6,0},{7,1},{8,14},{9,15},{10,... | collective-permute-start | bytes 393224 | tf_op jit(solution)/shard_map/ppermute | solution.py:26
  9.4 6.2 %collective-permute-start.4 = (bf16[2,32,1024]{2,1,0:T(8,128)(2,1)S(1)}, bf16[2,32,1024]{2,1,0:T(8,128)(2,1)S(1)}, u32[]{:S(2)}, u32[]{:S(2)}) collective-permute-start(bf16[2,32,1024]{2,1,0:T(8,128)(2,1)S(1)} %get-tuple-element.13), channel_id=1, source_target_pairs={{0,4},{1,5},{2,6},{3,7},{4,0},{5,1},{6,2},{7,3},{8,12},{9,13},{10,... | collective-permute-start | bytes 393224 | tf_op jit(solution)/shard_map/ppermute | solution.py:26
  9.9 5.8 %collective-permute-start.3 = (bf16[2,32,1024]{2,1,0:T(8,128)(2,1)S(1)}, bf16[2,32,1024]{2,1,0:T(8,128)(2,1)S(1)}, u32[]{:S(2)}, u32[]{:S(2)}) collective-permute-start(bf16[2,32,1024]{2,1,0:T(8,128)(2,1)S(1)} %get-tuple-element.14), channel_id=1, source_target_pairs={{0,2},{1,3},{2,0},{3,1},{4,6},{5,7},{6,4},{7,5},{8,10},{9,11},{10,... | collective-permute-start | bytes 393224 | tf_op jit(solution)/shard_map/ppermute | solution.py:26
  11.8 0.7 %copy-start.1 = (s32[1,256]{1,0:T(1,128)S(1)}, s32[1,256]{1,0:T(1,128)}, u32[]{:S(2)}) copy-start(s32[1,256]{1,0:T(1,128)} %param.7) | copy-start | bytes 3076
  12.6 5.0 %collective-permute-start.2 = (bf16[64,1024]{1,0:T(8,128)(2,1)S(1)}, bf16[64,1024]{1,0:T(8,128)(2,1)S(1)}, u32[]{:S(2)}, u32[]{:S(2)}) collective-permute-start(bf16[64,1024]{1,0:T(8,128)(2,1)S(1)} %collective-permute-done.1.refs_3_.refs_4_), channel_id=1, source_target_pairs={{0,8},{8,0},{16,24},{24,16},{1,9},{9,1},{17,25},{25,17},{2,10},{10... | collective-permute-start | bytes 393224 | tf_op jit(solution)/shard_map/ppermute | solution.py:26
  15.7 1.9 %copy-start = (bf16[1,64,1024]{2,1,0:T(8,128)(2,1)S(1)}, bf16[1,64,1024]{2,1,0:T(8,128)(2,1)}, u32[]{:S(2)}) copy-start(bf16[1,64,1024]{2,1,0:T(8,128)(2,1)} %param.6) | copy-start | bytes 393220
  15.7 2.0 %collective-permute-start.6 = (bf16[4,32,1024]{2,1,0:T(8,128)(2,1)S(1)}, bf16[4,32,1024]{2,1,0:T(8,128)(2,1)S(1)}, u32[]{:S(2)}, u32[]{:S(2)}) collective-permute-start(bf16[4,32,1024]{2,1,0:T(8,128)(2,1)S(1)} %select.6), channel_id=1, source_target_pairs={{0,1},{1,0},{2,3},{3,2},{4,5},{5,4},{6,7},{7,6},{8,9},{9,8},{10,11... | collective-permute-start | bytes 786440 | tf_op jit(solution)/shard_map/ppermute | solution.py:26
  18.5 6.0 %collective-permute-start.7 = (bf16[64,1024]{1,0:T(8,128)(2,1)S(1)}, bf16[64,1024]{1,0:T(8,128)(2,1)S(1)}, u32[]{:S(2)}, u32[]{:S(2)}) collective-permute-start(bf16[64,1024]{1,0:T(8,128)(2,1)S(1)} %get-tuple-element.9), channel_id=1, source_target_pairs={{0,8},{8,0},{16,24},{24,16},{1,9},{9,1},{17,25},{25,17},{2,10},{10... | collective-permute-start | bytes 393224 | tf_op jit(solution)/shard_map/ppermute | solution.py:26
  20.6 11.8 %collective-permute-start.8 = (bf16[64,1024]{1,0:T(8,128)(2,1)S(1)}, bf16[64,1024]{1,0:T(8,128)(2,1)S(1)}, u32[]{:S(2)}, u32[]{:S(2)}) collective-permute-start(bf16[64,1024]{1,0:T(8,128)(2,1)S(1)} %get-tuple-element.10), channel_id=1, source_target_pairs={{0,16},{8,24},{16,0},{24,8},{1,17},{9,25},{17,1},{25,9},{2,18},{10... | collective-permute-start | bytes 393224 | tf_op jit(solution)/shard_map/ppermute | solution.py:26
  20.6 11.8 %collective-permute-start.9 = (bf16[64,1024]{1,0:T(8,128)(2,1)S(1)}, bf16[64,1024]{1,0:T(8,128)(2,1)S(1)}, u32[]{:S(2)}, u32[]{:S(2)}) collective-permute-start(bf16[64,1024]{1,0:T(8,128)(2,1)S(1)} %get-tuple-element.11), channel_id=1, source_target_pairs={{0,24},{8,16},{16,8},{24,0},{1,25},{9,17},{17,9},{25,1},{2,26},{10... | collective-permute-start | bytes 393224 | tf_op jit(solution)/shard_map/ppermute | solution.py:26

commit v3 on v2

--- a/solution.py
+++ b/solution.py
@@ -96,8 +96,8 @@
 def fetch_covs(own, count):
     if count != 4:
         return [own] + [exchange(own, "blk", k) for k in range(1, count)], []
-    far = exchange(own, "blk", 3)
-    return [own, exchange(own, "blk", 1), exchange(far, "blk", 1), far], [far]
+    two = exchange(own, "blk", 2)
+    return [own, exchange(own, "blk", 1), two, exchange(two, "blk", 1)], [two]
 
 
 def fetch_texts(text_emb, early):
@@ -131,7 +131,8 @@
         [SHAPE((count * rows, n_text), BF16), SHAPE((rows, width), F32)] + [SHAPE((rows, width), BF16)] * (count - 1),
         [params, pile] + texts, 2 * flops, limit=16 if count == 4 else 40,
         scratch=[pltpu.VMEM((n_text, width) if chips else (8, 128), BF16), pltpu.VMEM((count * rows, width), F32)])
-    got = [exchange(part, "blk", k if is_power(count) else -k) for k, part in enumerate(parts, 1)]
+    order = (2, 1, 3) if count == 4 else range(1, count)
+    got = [exchange(parts[k - 1], "blk", k if is_power(count) else -k) for k in order]
     text_grad = call(text_kernel, "text_grad", SHAPE((n_text, width), F32), [coeff, pile], flops, limit=16)
     total = own
     for part in got:

time: 33.4 us -> 31.9 us (0.955)
  the two profiles are of different devices: /device:TPU:0 before, /device:TPU:11 now
where the time goes in v3:
time: 31.9 us; the launch traced here: 31.7 us
  waiting for transfers between devices  14.4 us (45%)
  starting transfers between devices  10.5 us (33%)
  Pallas kernels  2.17 us (7%)
  between operations  1.97 us (6%)
  local copies, waits for them, and re-layouts  1.89 us (6%)
  other arithmetic  0.85 us (3%)
    ppermute x10, waiting for transfers between devices, exchange(): lax.ppermute(value, axis, [(i, i ^ k if is_power(count) else (i + k) % co...  14.4 us
    ppermute x10, starting transfers between devices, exchange(): lax.ppermute(value, axis, [(i, i ^ k if is_power(count) else (i + k) % co...  10.5 us
    pallas_call x4, Pallas kernels, call(): pl.pallas_call(kernel, out_shape=out_shape, in_specs=specs or [VMEM] * le...  2.17 us
    squeeze x1, local copies, waits for them, and re-layouts, fetch_texts(): lax.dynamic_index_in_dim(by_chip, chip ^ k, 0, keepdims=False)  1.13 us
    broadcast_in_dim x1, other arithmetic, local(): return (text_grad[None], total[None])  0.77 us
  transfers between devices with their start and end apart: 10, of which 5 were waited for; matrix products, arithmetic and copies ran while one was open for 4% of the time, Pallas kernels for 4%

profile of v3, /device:TPU:11, one launch (start us, length us, event | category | flops | bytes accessed | tf_op | source)
XLA Modules:
  0.0 31.7 jit_solution(6078332517615900051)
XLA Ops:
  0.6 2.4 %collective-permute-start.1 = (bf16[64,1024]{1,0:T(8,128)(2,1)}, bf16[64,1024]{1,0:T(8,128)(2,1)S(1)}, u32[]{:S(2)}, u32[]{:S(2)}) collective-permute-start(bf16[64,1024]{1,0:T(8,128)(2,1)} %bitcast.15), channel_id=1, source_target_pairs={{0,16},{8,24},{16,0},{24,8},{1,17},{9,25},{17,1},{25,9},{2,18},{10... | collective-permute-start | bytes 393224 | tf_op jit(solution)/shard_map/ppermute | solution.py:26
  3.0 0.2 collective-permute-start
  3.2 1.1 %dynamic-slice_bitcast_fusion = (bf16[2,32,1024]{2,1,0:T(8,128)(2,1)S(1)}, bf16[2,32,1024]{2,1,0:T(8,128)(2,1)S(1)}, bf16[2,32,1024]{2,1,0:T(8,128)(2,1)S(1)}, bf16[2,32,1024]{2,1,0:T(8,128)(2,1)S(1)}) fusion(bf16[4,2,32,1024]{3,2,1,0:T(8,128)(2,1)} %bitcast.19, s32[]{:T(128)S(6)} %select_n.22, s32[]{:T(128)S(6)} %select_n.21, s32[]{:T(128)S(6)} %select_n.20, ...), kind=kLoop, calls=%fused_computation.1 | loop fusion | bytes 1048592 | tf_op jit(solution)/shard_map/jit(dynamic_index_in_dim)/squeeze | solution.py:110
  4.3 1.3 %collective-permute-start.5 = (bf16[2,32,1024]{2,1,0:T(8,128)(2,1)S(1)}, bf16[2,32,1024]{2,1,0:T(8,128)(2,1)S(1)}, u32[]{:S(2)}, u32[]{:S(2)}) collective-permute-start(bf16[2,32,1024]{2,1,0:T(8,128)(2,1)S(1)} %get-tuple-element.12), channel_id=1, source_target_pairs={{0,6},{1,7},{2,4},{3,5},{4,2},{5,3},{6,0},{7,1},{8,14},{9,15},{10,... | collective-permute-start | bytes 393224 | tf_op jit(solution)/shard_map/ppermute | solution.py:26
  5.6 0.2 collective-permute-start.4
  5.8 1.2 %collective-permute-start.3 = (bf16[2,32,1024]{2,1,0:T(8,128)(2,1)S(1)}, bf16[2,32,1024]{2,1,0:T(8,128)(2,1)S(1)}, u32[]{:S(2)}, u32[]{:S(2)}) collective-permute-start(bf16[2,32,1024]{2,1,0:T(8,128)(2,1)S(1)} %get-tuple-element.14), channel_id=1, source_target_pairs={{0,2},{1,3},{2,0},{3,1},{4,6},{5,7},{6,4},{7,5},{8,10},{9,11},{10,... | collective-permute-start | bytes 393224 | tf_op jit(solution)/shard_map/ppermute | solution.py:26
  8.3 0.1 pad.6.clone
  8.4 0.0 copy-start.1
  8.4 0.1 pad.7.clone
  8.5 0.6 %copy-done.1 = s32[1,256]{1,0:T(1,128)S(1)} copy-done((s32[1,256]{1,0:T(1,128)S(1)}, s32[1,256]{1,0:T(1,128)}, u32[]{:S(2)}) %copy-start.1) | copy-done | bytes 1048
  9.1 0.1 maximum_maximum_fusion
  9.2 0.1 collective-permute-done.1.refs_2_.refs_4_
  9.2 1.3 %collective-permute-start.2 = (bf16[64,1024]{1,0:T(8,128)(2,1)S(1)}, bf16[64,1024]{1,0:T(8,128)(2,1)S(1)}, u32[]{:S(2)}, u32[]{:S(2)}) collective-permute-start(bf16[64,1024]{1,0:T(8,128)(2,1)S(1)} %collective-permute-done.1.refs_2_.refs_4_), channel_id=1, source_target_pairs={{0,8},{8,0},{16,24},{24,16},{1,9},{9,1},{17,25},{25,17},{2,10},{10... | collective-permute-start | bytes 393224 | tf_op jit(solution)/shard_map/ppermute | solution.py:26
  10.5 0.0 collective-permute-done.5.refs_3_
  10.5 2.4 %collective-permute-done.4.refs_2_ = bf16[2,32,1024]{2,1,0:T(8,128)(2,1)S(1)} collective-permute-done((bf16[2,32,1024]{2,1,0:T(8,128)(2,1)S(1)}, bf16[2,32,1024]{2,1,0:T(8,128)(2,1)S(1)}, u32[]{:S(2)}, u32[]{:S(2)}) %collective-permute-start.4) | collective-permute-done | bytes 131104 | tf_op jit(solution)/shard_map/ppermute | solution.py:26
  12.9 0.0 collective-permute-done.3.refs_1_
  12.9 0.0 copy-start
  13.0 1.2 %collective-permute-start.6 = (bf16[4,32,1024]{2,1,0:T(8,128)(2,1)S(1)}, bf16[4,32,1024]{2,1,0:T(8,128)(2,1)S(1)}, u32[]{:S(2)}, u32[]{:S(2)}) collective-permute-start(bf16[4,32,1024]{2,1,0:T(8,128)(2,1)S(1)} %select.6), channel_id=1, source_target_pairs={{0,1},{1,0},{2,3},{3,2},{4,5},{5,4},{6,7},{7,6},{8,9},{9,8},{10,11... | collective-permute-start | bytes 786440 | tf_op jit(solution)/shard_map/ppermute | solution.py:26
  14.2 0.0 collective-permute-done.refs_1_
  14.2 0.0 collective-permute-done.2.refs_3_
  14.2 0.0 copy-done
  14.2 1.1 %collective-permute-done.6.refs_4_ = bf16[4,32,1024]{2,1,0:T(8,128)(2,1)S(1)} collective-permute-done((bf16[4,32,1024]{2,1,0:T(8,128)(2,1)S(1)}, bf16[4,32,1024]{2,1,0:T(8,128)(2,1)S(1)}, u32[]{:S(2)}, u32[]{:S(2)}) %collective-permute-start.6) | collective-permute-done | bytes 262176 | tf_op jit(solution)/shard_map/ppermute | solution.py:26
  15.3 0.8 %coeff.1 = (bf16[256,256]{1,0:T(8,128)(2,1)S(1)}, f32[64,1024]{1,0:T(8,128)S(1)}, bf16[64,1024]{1,0:T(8,128)(2,1)S(1)}, bf16[64,1024]{1,0:T(8,128)(2,1)S(1)}, bf16[64,1024]{1,0:T(8,128)(2,1)S(1)}) custom-call(f32[8,256]{1,0:T(8,128)S(1)} %pad.4.refs_5_.params_ref, bf16[256,1024]{1,0:T(8,128)(2,1)S(1)} %pile.1.covs_ref, ...), custom_call_target="tpu_custom_call" | custom-call | flops 268435456 | bytes 1048576 | tf_op jit(solution)/shard_map/coeff/pallas_call | solution.py:84
  16.2 1.6 %collective-permute-start.7 = (bf16[64,1024]{1,0:T(8,128)(2,1)S(1)}, bf16[64,1024]{1,0:T(8,128)(2,1)S(1)}, u32[]{:S(2)}, u32[]{:S(2)}) collective-permute-start(bf16[64,1024]{1,0:T(8,128)(2,1)S(1)} %get-tuple-element.9), channel_id=1, source_target_pairs={{0,16},{8,24},{16,0},{24,8},{1,17},{9,25},{17,1},{25,9},{2,18},{10... | collective-permute-start | bytes 393224 | tf_op jit(solution)/shard_map/ppermute | solution.py:26
  17.8 0.1 collective-permute-start.8
  17.8 1.0 %collective-permute-start.9 = (bf16[64,1024]{1,0:T(8,128)(2,1)S(1)}, bf16[64,1024]{1,0:T(8,128)(2,1)S(1)}, u32[]{:S(2)}, u32[]{:S(2)}) collective-permute-start(bf16[64,1024]{1,0:T(8,128)(2,1)S(1)} %get-tuple-element.11), channel_id=1, source_target_pairs={{0,24},{8,16},{16,8},{24,0},{1,25},{9,17},{17,9},{25,1},{2,26},{10... | collective-permute-start | bytes 393224 | tf_op jit(solution)/shard_map/ppermute | solution.py:26
  18.9 1.3 %text_grad.1 = f32[256,1024]{1,0:T(8,128)} custom-call(bf16[256,256]{1,0:T(8,128)(2,1)S(1)} %get-tuple-element.7.coeff_ref, bf16[256,1024]{1,0:T(8,128)(2,1)S(1)} %pile.1.covs_ref), custom_call_target="tpu_custom_call" | custom-call | flops 134217728 | bytes 1048576 | tf_op jit(solution)/shard_map/text_grad/pallas_call | solution.py:84
  20.2 3.7 %collective-permute-done.7 = bf16[64,1024]{1,0:T(8,128)(2,1)S(1)} collective-permute-done((bf16[64,1024]{1,0:T(8,128)(2,1)S(1)}, bf16[64,1024]{1,0:T(8,128)(2,1)S(1)}, u32[]{:S(2)}, u32[]{:S(2)}) %collective-permute-start.7) | collective-permute-done | bytes 131104 | tf_op jit(solution)/shard_map/ppermute | solution.py:26
  23.9 0.0 collective-permute-done.8
  23.9 7.1 %collective-permute-done.9 = bf16[64,1024]{1,0:T(8,128)(2,1)S(1)} collective-permute-done((bf16[64,1024]{1,0:T(8,128)(2,1)S(1)}, bf16[64,1024]{1,0:T(8,128)(2,1)S(1)}, u32[]{:S(2)}, u32[]{:S(2)}) %collective-permute-start.9) | collective-permute-done | bytes 131104 | tf_op jit(solution)/shard_map/ppermute | solution.py:26
  31.0 0.8 %add_bitcast_fusion = f32[1,64,1024]{2,1,0:T(8,128)} fusion(bf16[64,1024]{1,0:T(8,128)(2,1)S(1)} %collective-permute-done.9, bf16[64,1024]{1,0:T(8,128)(2,1)S(1)} %collective-permute-done.8, f32[64,1024]{1,0:T(8,128)S(1)} %get-tuple-element.8, bf16[64,1024]{1,0:T(8,128)(2,1)S(1)} %collective-permute-done.7), kind=kLoop, calls=%fused_computation | loop fusion | flops 393216 | bytes 917504 | tf_op jit(solution)/shard_map/broadcast_in_dim | solution.py:140
  (4 shorter events, 0.1 us)
Async XLA Ops:
  0.6 8.6 %collective-permute-start.1 = (bf16[64,1024]{1,0:T(8,128)(2,1)}, bf16[64,1024]{1,0:T(8,128)(2,1)S(1)}, u32[]{:S(2)}, u32[]{:S(2)}) collective-permute-start(bf16[64,1024]{1,0:T(8,128)(2,1)} %bitcast.15), channel_id=1, source_target_pairs={{0,16},{8,24},{16,0},{24,8},{1,17},{9,25},{17,1},{25,9},{2,18},{10... | collective-permute-start | bytes 393224 | tf_op jit(solution)/shard_map/ppermute | solution.py:26
  3.0 11.2 %collective-permute-start = (bf16[64,1024]{1,0:T(8,128)(2,1)}, bf16[64,1024]{1,0:T(8,128)(2,1)S(1)}, u32[]{:S(2)}, u32[]{:S(2)}) collective-permute-start(bf16[64,1024]{1,0:T(8,128)(2,1)} %bitcast.16), channel_id=1, source_target_pairs={{0,8},{8,0},{16,24},{24,16},{1,9},{9,1},{17,25},{25,17},{2,10},{10... | collective-permute-start | bytes 393224 | tf_op jit(solution)/shard_map/ppermute | solution.py:26
  4.3 6.2 %collective-permute-start.5 = (bf16[2,32,1024]{2,1,0:T(8,128)(2,1)S(1)}, bf16[2,32,1024]{2,1,0:T(8,128)(2,1)S(1)}, u32[]{:S(2)}, u32[]{:S(2)}) collective-permute-start(bf16[2,32,1024]{2,1,0:T(8,128)(2,1)S(1)} %get-tuple-element.12), channel_id=1, source_target_pairs={{0,6},{1,7},{2,4},{3,5},{4,2},{5,3},{6,0},{7,1},{8,14},{9,15},{10,... | collective-permute-start | bytes 393224 | tf_op jit(solution)/shard_map/ppermute | solution.py:26
  5.6 7.4 %collective-permute-start.4 = (bf16[2,32,1024]{2,1,0:T(8,128)(2,1)S(1)}, bf16[2,32,1024]{2,1,0:T(8,128)(2,1)S(1)}, u32[]{:S(2)}, u32[]{:S(2)}) collective-permute-start(bf16[2,32,1024]{2,1,0:T(8,128)(2,1)S(1)} %get-tuple-element.13), channel_id=1, source_target_pairs={{0,4},{1,5},{2,6},{3,7},{4,0},{5,1},{6,2},{7,3},{8,12},{9,13},{10,... | collective-permute-start | bytes 393224 | tf_op jit(solution)/shard_map/ppermute | solution.py:26
  5.8 7.1 %collective-permute-start.3 = (bf16[2,32,1024]{2,1,0:T(8,128)(2,1)S(1)}, bf16[2,32,1024]{2,1,0:T(8,128)(2,1)S(1)}, u32[]{:S(2)}, u32[]{:S(2)}) collective-permute-start(bf16[2,32,1024]{2,1,0:T(8,128)(2,1)S(1)} %get-tuple-element.14), channel_id=1, source_target_pairs={{0,2},{1,3},{2,0},{3,1},{4,6},{5,7},{6,4},{7,5},{8,10},{9,11},{10,... | collective-permute-start | bytes 393224 | tf_op jit(solution)/shard_map/ppermute | solution.py:26
  8.4 0.7 %copy-start.1 = (s32[1,256]{1,0:T(1,128)S(1)}, s32[1,256]{1,0:T(1,128)}, u32[]{:S(2)}) copy-start(s32[1,256]{1,0:T(1,128)} %param.7) | copy-start | bytes 3076
  9.2 5.0 %collective-permute-start.2 = (bf16[64,1024]{1,0:T(8,128)(2,1)S(1)}, bf16[64,1024]{1,0:T(8,128)(2,1)S(1)}, u32[]{:S(2)}, u32[]{:S(2)}) collective-permute-start(bf16[64,1024]{1,0:T(8,128)(2,1)S(1)} %collective-permute-done.1.refs_2_.refs_4_), channel_id=1, source_target_pairs={{0,8},{8,0},{16,24},{24,16},{1,9},{9,1},{17,25},{25,17},{2,10},{10... | collective-permute-start | bytes 393224 | tf_op jit(solution)/shard_map/ppermute | solution.py:26
  12.9 1.2 %copy-start = (bf16[1,64,1024]{2,1,0:T(8,128)(2,1)S(1)}, bf16[1,64,1024]{2,1,0:T(8,128)(2,1)}, u32[]{:S(2)}) copy-start(bf16[1,64,1024]{2,1,0:T(8,128)(2,1)} %param.6) | copy-start | bytes 393220
  13.0 2.4 %collective-permute-start.6 = (bf16[4,32,1024]{2,1,0:T(8,128)(2,1)S(1)}, bf16[4,32,1024]{2,1,0:T(8,128)(2,1)S(1)}, u32[]{:S(2)}, u32[]{:S(2)}) collective-permute-start(bf16[4,32,1024]{2,1,0:T(8,128)(2,1)S(1)} %select.6), channel_id=1, source_target_pairs={{0,1},{1,0},{2,3},{3,2},{4,5},{5,4},{6,7},{7,6},{8,9},{9,8},{10,11... | collective-permute-start | bytes 786440 | tf_op jit(solution)/shard_map/ppermute | solution.py:26
  16.2 7.7 %collective-permute-start.7 = (bf16[64,1024]{1,0:T(8,128)(2,1)S(1)}, bf16[64,1024]{1,0:T(8,128)(2,1)S(1)}, u32[]{:S(2)}, u32[]{:S(2)}) collective-permute-start(bf16[64,1024]{1,0:T(8,128)(2,1)S(1)} %get-tuple-element.9), channel_id=1, source_target_pairs={{0,16},{8,24},{16,0},{24,8},{1,17},{9,25},{17,1},{25,9},{2,18},{10... | collective-permute-start | bytes 393224 | tf_op jit(solution)/shard_map/ppermute | solution.py:26
  17.8 6.1 %collective-permute-start.8 = (bf16[64,1024]{1,0:T(8,128)(2,1)S(1)}, bf16[64,1024]{1,0:T(8,128)(2,1)S(1)}, u32[]{:S(2)}, u32[]{:S(2)}) collective-permute-start(bf16[64,1024]{1,0:T(8,128)(2,1)S(1)} %get-tuple-element.10), channel_id=1, source_target_pairs={{0,8},{8,0},{16,24},{24,16},{1,9},{9,1},{17,25},{25,17},{2,10},{10... | collective-permute-start | bytes 393224 | tf_op jit(solution)/shard_map/ppermute | solution.py:26
  17.8 13.1 %collective-permute-start.9 = (bf16[64,1024]{1,0:T(8,128)(2,1)S(1)}, bf16[64,1024]{1,0:T(8,128)(2,1)S(1)}, u32[]{:S(2)}, u32[]{:S(2)}) collective-permute-start(bf16[64,1024]{1,0:T(8,128)(2,1)S(1)} %get-tuple-element.11), channel_id=1, source_target_pairs={{0,24},{8,16},{16,8},{24,0},{1,25},{9,17},{17,9},{25,1},{2,26},{10... | collective-permute-start | bytes 393224 | tf_op jit(solution)/shard_map/ppermute | solution.py:26

commit v4 on v3

--- a/solution.py
+++ b/solution.py
@@ -24,6 +24,13 @@
 def exchange(value, axis, k):
     count = lax.axis_size(axis)
     return lax.ppermute(value, axis, [(i, i ^ k if is_power(count) else (i + k) % count) for i in range(count)])
+
+
+def mixed(value, even, odd):
+    blocks, groups = lax.axis_size("blk"), lax.axis_size("section")
+    steps = [odd if s % 2 else even for s in range(groups)]
+    pairs = [(b * groups + s, (b ^ steps[s]) * groups + s) for b in range(blocks) for s in range(groups) if steps[s]]
+    return lax.ppermute(value, ("blk", "section"), pairs)
 
 
 def source_block(me, k, count):
@@ -71,8 +78,20 @@
     coeff_ref[...] = coeff
     prod[...] = jnp.dot(coeff, text, preferred_element_type=F32)
     own_ref[...] = prod[0:rows, :]
-    for k, ref in enumerate(part_refs, 1):
-        ref[...] = prod[k * rows:(k + 1) * rows, :].astype(BF16)
+    if two_cores(count):
+        odd = lax.axis_index("section") % 2
+        first, second, third, far = part_refs
+        first[...] = prod[2 * rows:3 * rows, :].astype(BF16)
+        second[...] = prod[span(3 - 2 * odd, rows), :].astype(BF16)
+        third[...] = prod[rows:2 * rows, :].astype(BF16)
+        far[...] = prod[3 * rows:4 * rows, :]
+    else:
+        for k, ref in enumerate(part_refs, 1):
+            ref[...] = prod[k * rows:(k + 1) * rows, :].astype(BF16)
+
+
+def add_kernel(part_ref, got_ref, out_ref):
+    out_ref[...] = (part_ref[...] + got_ref[...].astype(F32)).astype(BF16)
 
 
 def text_kernel(coeff_ref, covs_ref, out_ref):
@@ -91,6 +110,22 @@
         cost_estimate=pl.CostEstimate(flops=flops, bytes_accessed=MIB, transcendentals=0),
         name=name,
     )(*args)
+
+
+def two_cores(count):
+    return count == 4 and lax.axis_size("section") % 2 == 0
+
+
+def reduce_covs(own, parts, count):
+    if not two_cores(count):
+        got = [exchange(part, "blk", k if is_power(count) else -k) for k, part in enumerate(parts, 1)]
+        return sum((part.astype(F32) for part in got), own)
+    first, second, third, far = parts
+    got = [mixed(first, 2, 1), mixed(second, 3, 1), mixed(third, 1, 0)]
+    summed = call(add_kernel, "add", SHAPE(far.shape, BF16), [far, got[0]], 0)
+    got.append(mixed(summed, 0, 3))
+    odd = lax.axis_index("section") % 2 == 1
+    return own + jnp.where(odd, 0, got[0].astype(F32)) + sum(part.astype(F32) for part in got[1:])
 
 
 def fetch_covs(own, count):
@@ -119,24 +154,19 @@
     count = lax.axis_size("blk")
     rows, width = covariate.shape[1:]
     n_text = labels.shape[1]
-    params = jnp.concatenate(
-        [labels.astype(F32), jnp.broadcast_to(logit_scale[None], labels.shape), jnp.broadcast_to(logit_bias[None], labels.shape)])
-    params = jnp.pad(params, ((0, 5), (0, 0)))
+    row = lax.broadcasted_iota(jnp.int32, (8, n_text), 0)
+    params = jnp.where(row == 0, labels.astype(F32), jnp.where(row == 1, logit_scale[0], logit_bias[0]))
     covs, early = fetch_covs(covariate[0], count)
     texts, chips = fetch_texts(text_emb, early + [params])
     pile = call(pile_kernel, "pile", SHAPE((count * rows, width), BF16), covs, LONG)
     flops = 2 * count * rows * n_text * width
     coeff, own, *parts = call(
         functools.partial(coeff_kernel, count, chips), "coeff",
-        [SHAPE((count * rows, n_text), BF16), SHAPE((rows, width), F32)] + [SHAPE((rows, width), BF16)] * (count - 1),
+        [SHAPE((count * rows, n_text), BF16), SHAPE((rows, width), F32)] + [SHAPE((rows, width), BF16)] * (count - 1) + [SHAPE((rows, width), F32)] * two_cores(count),
         [params, pile] + texts, 2 * flops, limit=16 if count == 4 else 40,
         scratch=[pltpu.VMEM((n_text, width) if chips else (8, 128), BF16), pltpu.VMEM((count * rows, width), F32)])
-    order = (2, 1, 3) if count == 4 else range(1, count)
-    got = [exchange(parts[k - 1], "blk", k if is_power(count) else -k) for k in order]
     text_grad = call(text_kernel, "text_grad", SHAPE((n_text, width), F32), [coeff, pile], flops, limit=16)
-    total = own
-    for part in got:
-        total = total + part.astype(F32)
+    total = reduce_covs(own, parts, count)
     return text_grad[None], total[None]
 
 

time: 31.9 us -> 31.3 us (0.981)
  the two profiles are of different devices: /device:TPU:11 before, /device:TPU:1 now
where the time goes in v4:
time: 31.3 us; the launch traced here: 31.1 us
  starting transfers between devices  15 us (48%)
  waiting for transfers between devices  9.85 us (31%)
  Pallas kernels  2.21 us (7%)
  between operations  2.03 us (6%)
  local copies, waits for them, and re-layouts  1.15 us (4%)
  other arithmetic  0.87 us (3%)
    ppermute x7, starting transfers between devices, exchange(): lax.ppermute(value, axis, [(i, i ^ k if is_power(count) else (i + k) % co...  9.48 us
    ppermute x4, starting transfers between devices, mixed(): return lax.ppermute(value, ('blk', 'section'), pairs)  5.51 us
    ppermute x4, waiting for transfers between devices, mixed(): return lax.ppermute(value, ('blk', 'section'), pairs)  5.32 us
    ppermute x7, waiting for transfers between devices, exchange(): lax.ppermute(value, axis, [(i, i ^ k if is_power(count) else (i + k) % co...  4.53 us
    pallas_call x5, Pallas kernels, call(): pl.pallas_call(kernel, out_shape=out_shape, in_specs=specs or [VMEM] * le...  2.21 us
    squeeze x1, local copies, waits for them, and re-layouts, fetch_texts(): lax.dynamic_index_in_dim(by_chip, chip ^ k, 0, keepdims=False)  1.13 us
    broadcast_in_dim x1, other arithmetic, local(): return (text_grad[None], total[None])  0.79 us
  transfers between devices with their start and end apart: 11, of which 4 were waited for; matrix products, arithmetic and copies ran while one was open for 4% of the time, Pallas kernels for 4%

profile of v4, /device:TPU:1, one launch (start us, length us, event | category | flops | bytes accessed | tf_op | source)
XLA Modules:
  0.0 31.1 jit_solution(6058194586762312519)
XLA Ops:
  0.6 3.2 %collective-permute-start.1 = (bf16[64,1024]{1,0:T(8,128)(2,1)}, bf16[64,1024]{1,0:T(8,128)(2,1)S(1)}, u32[]{:S(2)}, u32[]{:S(2)}) collective-permute-start(bf16[64,1024]{1,0:T(8,128)(2,1)} %bitcast.18), channel_id=1, source_target_pairs={{0,16},{8,24},{16,0},{24,8},{1,17},{9,25},{17,1},{25,9},{2,18},{10... | collective-permute-start | bytes 393224 | tf_op jit(solution)/shard_map/ppermute | solution.py:26
  3.8 1.3 %collective-permute-start = (bf16[64,1024]{1,0:T(8,128)(2,1)}, bf16[64,1024]{1,0:T(8,128)(2,1)S(1)}, u32[]{:S(2)}, u32[]{:S(2)}) collective-permute-start(bf16[64,1024]{1,0:T(8,128)(2,1)} %bitcast.19), channel_id=1, source_target_pairs={{0,8},{8,0},{16,24},{24,16},{1,9},{9,1},{17,25},{25,17},{2,10},{10... | collective-permute-start | bytes 393224 | tf_op jit(solution)/shard_map/ppermute | solution.py:26
  5.1 1.1 %dynamic-slice_bitcast_fusion = (bf16[2,32,1024]{2,1,0:T(8,128)(2,1)S(1)}, bf16[2,32,1024]{2,1,0:T(8,128)(2,1)S(1)}, bf16[2,32,1024]{2,1,0:T(8,128)(2,1)S(1)}, bf16[2,32,1024]{2,1,0:T(8,128)(2,1)S(1)}) fusion(bf16[4,2,32,1024]{3,2,1,0:T(8,128)(2,1)} %bitcast.22, s32[]{:T(128)S(6)} %select_n.47, s32[]{:T(128)S(6)} %select_n.46, s32[]{:T(128)S(6)} %select_n.45, ...), kind=kLoop, calls=%fused_computation.1 | loop fusion | bytes 1048592 | tf_op jit(solution)/shard_map/jit(dynamic_index_in_dim)/squeeze | solution.py:145
  6.3 2.2 %collective-permute-start.5 = (bf16[2,32,1024]{2,1,0:T(8,128)(2,1)S(1)}, bf16[2,32,1024]{2,1,0:T(8,128)(2,1)S(1)}, u32[]{:S(2)}, u32[]{:S(2)}) collective-permute-start(bf16[2,32,1024]{2,1,0:T(8,128)(2,1)S(1)} %get-tuple-element.14), channel_id=1, source_target_pairs={{0,6},{1,7},{2,4},{3,5},{4,2},{5,3},{6,0},{7,1},{8,14},{9,15},{10,... | collective-permute-start | bytes 393224 | tf_op jit(solution)/shard_map/ppermute | solution.py:26
  8.5 0.2 collective-permute-start.4
  8.7 0.3 collective-permute-start.3
  9.6 0.0 copy-start.1
  10.3 0.0 copy-done.1
  10.3 0.1 broadcast_select_fusion.refs_5_.params_ref
  10.4 0.0 collective-permute-done.1.refs_2_.refs_4_
  10.4 0.9 %collective-permute-start.2 = (bf16[64,1024]{1,0:T(8,128)(2,1)S(1)}, bf16[64,1024]{1,0:T(8,128)(2,1)S(1)}, u32[]{:S(2)}, u32[]{:S(2)}) collective-permute-start(bf16[64,1024]{1,0:T(8,128)(2,1)S(1)} %collective-permute-done.1.refs_2_.refs_4_), channel_id=1, source_target_pairs={{0,8},{8,0},{16,24},{24,16},{1,9},{9,1},{17,25},{25,17},{2,10},{10... | collective-permute-start | bytes 393224 | tf_op jit(solution)/shard_map/ppermute | solution.py:26
  11.4 0.0 collective-permute-done.5.refs_3_
  11.4 3.4 %collective-permute-done.4.refs_2_ = bf16[2,32,1024]{2,1,0:T(8,128)(2,1)S(1)} collective-permute-done((bf16[2,32,1024]{2,1,0:T(8,128)(2,1)S(1)}, bf16[2,32,1024]{2,1,0:T(8,128)(2,1)S(1)}, u32[]{:S(2)}, u32[]{:S(2)}) %collective-permute-start.4) | collective-permute-done | bytes 131104 | tf_op jit(solution)/shard_map/ppermute | solution.py:26
  14.8 0.0 collective-permute-done.3.refs_1_
  14.8 0.0 copy-start
  14.8 1.3 %collective-permute-start.6 = (bf16[4,32,1024]{2,1,0:T(8,128)(2,1)S(1)}, bf16[4,32,1024]{2,1,0:T(8,128)(2,1)S(1)}, u32[]{:S(2)}, u32[]{:S(2)}) collective-permute-start(bf16[4,32,1024]{2,1,0:T(8,128)(2,1)S(1)} %select.7), channel_id=1, source_target_pairs={{0,1},{1,0},{2,3},{3,2},{4,5},{5,4},{6,7},{7,6},{8,9},{9,8},{10,11... | collective-permute-start | bytes 786440 | tf_op jit(solution)/shard_map/ppermute | solution.py:26
  16.1 0.0 collective-permute-done.refs_1_
  16.1 0.0 collective-permute-done.2.refs_3_
  16.1 0.0 copy-done
  16.2 1.1 %collective-permute-done.6.refs_4_ = bf16[4,32,1024]{2,1,0:T(8,128)(2,1)S(1)} collective-permute-done((bf16[4,32,1024]{2,1,0:T(8,128)(2,1)S(1)}, bf16[4,32,1024]{2,1,0:T(8,128)(2,1)S(1)}, u32[]{:S(2)}, u32[]{:S(2)}) %collective-permute-start.6) | collective-permute-done | bytes 262176 | tf_op jit(solution)/shard_map/ppermute | solution.py:26
  17.3 0.8 %coeff.1 = (bf16[256,256]{1,0:T(8,128)(2,1)S(1)}, f32[64,1024]{1,0:T(8,128)S(1)}, bf16[64,1024]{1,0:T(8,128)(2,1)S(1)}, bf16[64,1024]{1,0:T(8,128)(2,1)S(1)}, bf...) custom-call(f32[8,256]{1,0:T(8,128)S(1)} %broadcast_select_fusion.refs_5_.params_ref, ...), custom_call_target="tpu_custom_call" | custom-call | flops 268435456 | bytes 1048576 | tf_op jit(solution)/shard_map/coeff/pallas_call | solution.py:103
  18.1 0.2 collective-permute-start.7
  18.4 1.3 %collective-permute-start.8 = (bf16[64,1024]{1,0:T(8,128)(2,1)S(1)}, bf16[64,1024]{1,0:T(8,128)(2,1)S(1)}, u32[]{:S(2)}, u32[]{:S(2)}) collective-permute-start(bf16[64,1024]{1,0:T(8,128)(2,1)S(1)} %get-tuple-element.11), channel_id=1, source_target_pairs={{0,24},{1,9},{2,26},{3,11},{4,28},{5,13},{6,30},{7,15},{8,16},{9,1... | collective-permute-start | bytes 393224 | tf_op jit(solution)/shard_map/ppermute | solution.py:33
  19.7 0.7 %collective-permute-start.9 = (bf16[64,1024]{1,0:T(8,128)(2,1)S(1)}, bf16[64,1024]{1,0:T(8,128)(2,1)S(1)}, u32[]{:S(2)}, u32[]{:S(2)}) collective-permute-start(bf16[64,1024]{1,0:T(8,128)(2,1)S(1)} %get-tuple-element.12), channel_id=1, source_target_pairs={{0,8},{2,10},{4,12},{6,14},{8,0},{10,2},{12,4},{14,6},{16,24},{18,... | collective-permute-start | bytes 393224 | tf_op jit(solution)/shard_map/ppermute | solution.py:33
  20.3 1.7 %collective-permute-done.7.got_ref = bf16[64,1024]{1,0:T(8,128)(2,1)S(1)} collective-permute-done((bf16[64,1024]{1,0:T(8,128)(2,1)S(1)}, bf16[64,1024]{1,0:T(8,128)(2,1)S(1)}, u32[]{:S(2)}, u32[]{:S(2)}) %collective-permute-start.7) | collective-permute-done | bytes 131104 | tf_op jit(solution)/shard_map/ppermute | solution.py:33
  22.1 3.3 %collective-permute-start.10 = (bf16[64,1024]{1,0:T(8,128)(2,1)S(1)}, bf16[64,1024]{1,0:T(8,128)(2,1)S(1)}, u32[]{:S(2)}, u32[]{:S(2)}) collective-permute-start(bf16[64,1024]{1,0:T(8,128)(2,1)S(1)} %add.44), channel_id=1, source_target_pairs={{1,25},{3,27},{5,29},{7,31},{9,17},{11,19},{13,21},{15,23},{17,9},... | collective-permute-start | bytes 393224 | tf_op jit(solution)/shard_map/ppermute | solution.py:33
  25.4 1.3 %text_grad.1 = f32[256,1024]{1,0:T(8,128)} custom-call(bf16[256,256]{1,0:T(8,128)(2,1)S(1)} %get-tuple-element.8.coeff_ref, bf16[256,1024]{1,0:T(8,128)(2,1)S(1)} %pile.1.covs_ref), custom_call_target="tpu_custom_call" | custom-call | flops 134217728 | bytes 1048576 | tf_op jit(solution)/shard_map/text_grad/pallas_call | solution.py:103
  26.7 0.0 collective-permute-done.8
  26.7 0.0 collective-permute-done.9
  26.7 3.6 %collective-permute-done.10 = bf16[64,1024]{1,0:T(8,128)(2,1)S(1)} collective-permute-done((bf16[64,1024]{1,0:T(8,128)(2,1)S(1)}, bf16[64,1024]{1,0:T(8,128)(2,1)S(1)}, u32[]{:S(2)}, u32[]{:S(2)}) %collective-permute-start.10) | collective-permute-done | bytes 131104 | tf_op jit(solution)/shard_map/ppermute | solution.py:33
  30.3 0.8 %add_bitcast_fusion = f32[1,64,1024]{2,1,0:T(8,128)} fusion(bf16[64,1024]{1,0:T(8,128)(2,1)S(1)} %collective-permute-done.10, bf16[64,1024]{1,0:T(8,128)(2,1)S(1)} %collective-permute-done.9, bf16[64,1024]{1,0:T(8,128)(2,1)S(1)} %collective-permute-done.8, f32[64,1024]{1,0:T(8,128)S(1)} %get-tuple-element.9, ...), kind=kLoop, calls=%fused_computation | loop fusion | flops 589824 | bytes 1048577 | tf_op jit(solution)/shard_map/broadcast_in_dim | solution.py:170
  (6 shorter events, 0.1 us)
Async XLA Ops:
  0.6 9.8 %collective-permute-start.1 = (bf16[64,1024]{1,0:T(8,128)(2,1)}, bf16[64,1024]{1,0:T(8,128)(2,1)S(1)}, u32[]{:S(2)}, u32[]{:S(2)}) collective-permute-start(bf16[64,1024]{1,0:T(8,128)(2,1)} %bitcast.18), channel_id=1, source_target_pairs={{0,16},{8,24},{16,0},{24,8},{1,17},{9,25},{17,1},{25,9},{2,18},{10... | collective-permute-start | bytes 393224 | tf_op jit(solution)/shard_map/ppermute | solution.py:26
  3.8 12.3 %collective-permute-start = (bf16[64,1024]{1,0:T(8,128)(2,1)}, bf16[64,1024]{1,0:T(8,128)(2,1)S(1)}, u32[]{:S(2)}, u32[]{:S(2)}) collective-permute-start(bf16[64,1024]{1,0:T(8,128)(2,1)} %bitcast.19), channel_id=1, source_target_pairs={{0,8},{8,0},{16,24},{24,16},{1,9},{9,1},{17,25},{25,17},{2,10},{10... | collective-permute-start | bytes 393224 | tf_op jit(solution)/shard_map/ppermute | solution.py:26
  6.3 5.1 %collective-permute-start.5 = (bf16[2,32,1024]{2,1,0:T(8,128)(2,1)S(1)}, bf16[2,32,1024]{2,1,0:T(8,128)(2,1)S(1)}, u32[]{:S(2)}, u32[]{:S(2)}) collective-permute-start(bf16[2,32,1024]{2,1,0:T(8,128)(2,1)S(1)} %get-tuple-element.14), channel_id=1, source_target_pairs={{0,6},{1,7},{2,4},{3,5},{4,2},{5,3},{6,0},{7,1},{8,14},{9,15},{10,... | collective-permute-start | bytes 393224 | tf_op jit(solution)/shard_map/ppermute | solution.py:26
  8.5 6.3 %collective-permute-start.4 = (bf16[2,32,1024]{2,1,0:T(8,128)(2,1)S(1)}, bf16[2,32,1024]{2,1,0:T(8,128)(2,1)S(1)}, u32[]{:S(2)}, u32[]{:S(2)}) collective-permute-start(bf16[2,32,1024]{2,1,0:T(8,128)(2,1)S(1)} %get-tuple-element.15), channel_id=1, source_target_pairs={{0,4},{1,5},{2,6},{3,7},{4,0},{5,1},{6,2},{7,3},{8,12},{9,13},{10,... | collective-permute-start | bytes 393224 | tf_op jit(solution)/shard_map/ppermute | solution.py:26
  8.7 6.1 %collective-permute-start.3 = (bf16[2,32,1024]{2,1,0:T(8,128)(2,1)S(1)}, bf16[2,32,1024]{2,1,0:T(8,128)(2,1)S(1)}, u32[]{:S(2)}, u32[]{:S(2)}) collective-permute-start(bf16[2,32,1024]{2,1,0:T(8,128)(2,1)S(1)} %get-tuple-element.16), channel_id=1, source_target_pairs={{0,2},{1,3},{2,0},{3,1},{4,6},{5,7},{6,4},{7,5},{8,10},{9,11},{10,... | collective-permute-start | bytes 393224 | tf_op jit(solution)/shard_map/ppermute | solution.py:26
  9.6 0.7 %copy-start.1 = (s32[1,256]{1,0:T(1,128)S(1)}, s32[1,256]{1,0:T(1,128)}, u32[]{:S(2)}) copy-start(s32[1,256]{1,0:T(1,128)} %param.7) | copy-start | bytes 3076
  10.4 5.7 %collective-permute-start.2 = (bf16[64,1024]{1,0:T(8,128)(2,1)S(1)}, bf16[64,1024]{1,0:T(8,128)(2,1)S(1)}, u32[]{:S(2)}, u32[]{:S(2)}) collective-permute-start(bf16[64,1024]{1,0:T(8,128)(2,1)S(1)} %collective-permute-done.1.refs_2_.refs_4_), channel_id=1, source_target_pairs={{0,8},{8,0},{16,24},{24,16},{1,9},{9,1},{17,25},{25,17},{2,10},{10... | collective-permute-start | bytes 393224 | tf_op jit(solution)/shard_map/ppermute | solution.py:26
  14.8 1.4 %copy-start = (bf16[1,64,1024]{2,1,0:T(8,128)(2,1)S(1)}, bf16[1,64,1024]{2,1,0:T(8,128)(2,1)}, u32[]{:S(2)}) copy-start(bf16[1,64,1024]{2,1,0:T(8,128)(2,1)} %param.6) | copy-start | bytes 393220
  14.8 2.5 %collective-permute-start.6 = (bf16[4,32,1024]{2,1,0:T(8,128)(2,1)S(1)}, bf16[4,32,1024]{2,1,0:T(8,128)(2,1)S(1)}, u32[]{:S(2)}, u32[]{:S(2)}) collective-permute-start(bf16[4,32,1024]{2,1,0:T(8,128)(2,1)S(1)} %select.7), channel_id=1, source_target_pairs={{0,1},{1,0},{2,3},{3,2},{4,5},{5,4},{6,7},{7,6},{8,9},{9,8},{10,11... | collective-permute-start | bytes 786440 | tf_op jit(solution)/shard_map/ppermute | solution.py:26
  18.1 3.9 %collective-permute-start.7 = (bf16[64,1024]{1,0:T(8,128)(2,1)S(1)}, bf16[64,1024]{1,0:T(8,128)(2,1)S(1)}, u32[]{:S(2)}, u32[]{:S(2)}) collective-permute-start(bf16[64,1024]{1,0:T(8,128)(2,1)S(1)} %get-tuple-element.10), channel_id=1, source_target_pairs={{0,16},{1,9},{2,18},{3,11},{4,20},{5,13},{6,22},{7,15},{8,24},{9,1... | collective-permute-start | bytes 393224 | tf_op jit(solution)/shard_map/ppermute | solution.py:33
  18.4 8.3 %collective-permute-start.8 = (bf16[64,1024]{1,0:T(8,128)(2,1)S(1)}, bf16[64,1024]{1,0:T(8,128)(2,1)S(1)}, u32[]{:S(2)}, u32[]{:S(2)}) collective-permute-start(bf16[64,1024]{1,0:T(8,128)(2,1)S(1)} %get-tuple-element.11), channel_id=1, source_target_pairs={{0,24},{1,9},{2,26},{3,11},{4,28},{5,13},{6,30},{7,15},{8,16},{9,1... | collective-permute-start | bytes 393224 | tf_op jit(solution)/shard_map/ppermute | solution.py:33
  19.7 7.0 %collective-permute-start.9 = (bf16[64,1024]{1,0:T(8,128)(2,1)S(1)}, bf16[64,1024]{1,0:T(8,128)(2,1)S(1)}, u32[]{:S(2)}, u32[]{:S(2)}) collective-permute-start(bf16[64,1024]{1,0:T(8,128)(2,1)S(1)} %get-tuple-element.12), channel_id=1, source_target_pairs={{0,8},{2,10},{4,12},{6,14},{8,0},{10,2},{12,4},{14,6},{16,24},{18,... | collective-permute-start | bytes 393224 | tf_op jit(solution)/shard_map/ppermute | solution.py:33
  22.1 8.3 %collective-permute-start.10 = (bf16[64,1024]{1,0:T(8,128)(2,1)S(1)}, bf16[64,1024]{1,0:T(8,128)(2,1)S(1)}, u32[]{:S(2)}, u32[]{:S(2)}) collective-permute-start(bf16[64,1024]{1,0:T(8,128)(2,1)S(1)} %add.44), channel_id=1, source_target_pairs={{1,25},{3,27},{5,29},{7,31},{9,17},{11,19},{13,21},{15,23},{17,9},... | collective-permute-start | bytes 393224 | tf_op jit(solution)/shard_map/ppermute | solution.py:33

commit v5 on v4

--- a/solution.py
+++ b/solution.py
@@ -42,10 +42,26 @@
 
 
 def select_kernel(chips, *refs):
-    core = lax.axis_index("section") % 2
+    section = lax.axis_index("section")
+    chip, core = section // 2, section % 2
     out = refs[-1]
-    for k in range(chips):
+    out[0] = refs[0][chip, 1 - core]
+    for k in range(1, chips):
         out[k] = refs[k][1 - core]
+
+
+def sort_kernel(first_ref, second_ref, one_ref, two_ref):
+    odd = lax.axis_index("section") % 2
+
+    @pl.when(odd == 1)
+    def _():
+        one_ref[...] = first_ref[...]
+        two_ref[...] = second_ref[...]
+
+    @pl.when(odd == 0)
+    def _():
+        one_ref[...] = second_ref[...]
+        two_ref[...] = first_ref[...]
 
 
 def pile_kernel(*refs):
@@ -56,38 +72,41 @@
 
 
 def coeff_kernel(count, chips, params_ref, covs_ref, *refs):
-    texts, (coeff_ref, own_ref, *part_refs, panel, prod) = refs[:chips + 1], refs[chips + 1:]
+    texts, (coeff_ref, own_ref, *part_refs, panel) = refs[:chips + 1], refs[chips + 1:]
     rows = covs_ref.shape[0] // count
     if chips:
         section = lax.axis_index("section")
         chip, core = section // 2, section % 2
-        piece = texts[0].shape[1]
+        piece = texts[0].shape[2]
         for k in range(chips):
-            panel[span((chip ^ k) * 2 + core, piece), :] = texts[k][core]
+            panel[span((chip ^ k) * 2 + core, piece), :] = texts[k][core] if k else texts[0][chip, core]
             panel[span((chip ^ k) * 2 + 1 - core, piece), :] = texts[chips][k]
-        text = panel[...]
+        text_ref = panel
     else:
-        text = texts[0][...]
+        text_ref = texts[0]
     labels, scale, bias = params_ref[0:1, :], params_ref[1:2, :], params_ref[2:3, :]
-    logits = scale * lax.dot_general(covs_ref[...], text, NT, preferred_element_type=F32) + bias
+    logits = scale * lax.dot_general(covs_ref[...], text_ref[...], NT, preferred_element_type=F32) + bias
     me = lax.axis_index("blk")
     row = lax.broadcasted_iota(jnp.int32, (rows, 1), 0)
     ids = jnp.concatenate([source_block(me, k, count) * rows + row for k in range(count)], axis=0)
     positive = (labels == ids.astype(F32)).astype(F32)
     coeff = (scale * (jax.nn.sigmoid(logits) - positive)).astype(BF16)
     coeff_ref[...] = coeff
-    prod[...] = jnp.dot(coeff, text, preferred_element_type=F32)
-    own_ref[...] = prod[0:rows, :]
-    if two_cores(count):
-        odd = lax.axis_index("section") % 2
-        first, second, third, far = part_refs
-        first[...] = prod[2 * rows:3 * rows, :].astype(BF16)
-        second[...] = prod[span(3 - 2 * odd, rows), :].astype(BF16)
-        third[...] = prod[rows:2 * rows, :].astype(BF16)
-        far[...] = prod[3 * rows:4 * rows, :]
-    else:
-        for k, ref in enumerate(part_refs, 1):
-            ref[...] = prod[k * rows:(k + 1) * rows, :].astype(BF16)
+    step = min(256, text_ref.shape[1])
+    for at in range(0, text_ref.shape[1], step):
+        columns = slice(at, at + step)
+        prod = jnp.dot(coeff, text_ref[:, columns], preferred_element_type=F32)
+        blocks = [prod[k * rows:(k + 1) * rows, :] for k in range(count)]
+        own_ref[:, columns] = blocks[0]
+        if two_cores(count):
+            first, second, third, far = part_refs
+            first[:, columns] = blocks[2].astype(BF16)
+            second[:, columns] = jnp.where(lax.axis_index("section") % 2 == 1, blocks[1], blocks[3]).astype(BF16)
+            third[:, columns] = blocks[1].astype(BF16)
+            far[:, columns] = blocks[3]
+        else:
+            for ref, block in zip(part_refs, blocks[1:]):
+                ref[:, columns] = block.astype(BF16)
 
 
 def add_kernel(part_ref, got_ref, out_ref):
@@ -131,8 +150,9 @@
 def fetch_covs(own, count):
     if count != 4:
         return [own] + [exchange(own, "blk", k) for k in range(1, count)], []
-    two = exchange(own, "blk", 2)
-    return [own, exchange(own, "blk", 1), two, exchange(two, "blk", 1)], [two]
+    got = [mixed(own, 2, 1), mixed(own, 1, 2)]
+    one, two = call(sort_kernel, "sort", [SHAPE(own.shape, BF16)] * 2, got, 0)
+    return [own, one, two, exchange(two, "blk", 1)], [two]
 
 
 def fetch_texts(text_emb, early):
@@ -142,8 +162,8 @@
     chips = groups // 2
     chip = lax.axis_index("section") // 2
     by_chip = text_emb.reshape(chips, 2, piece, width)
-    parts = [lax.dynamic_index_in_dim(by_chip, chip ^ k, 0, keepdims=False) for k in range(chips)]
-    texts = parts[:1] + [exchange(parts[k], "section", 2 * k) for k in range(1, chips)]
+    parts = [lax.dynamic_index_in_dim(by_chip, chip ^ k, 0, keepdims=False) for k in range(1, chips)]
+    texts = [by_chip] + [exchange(part, "section", 2 * k) for k, part in enumerate(parts, 1)]
     other = call(
         functools.partial(select_kernel, chips), "select", SHAPE((chips, piece, width), BF16),
         texts + early, LONG, specs=[VMEM] * chips + [ANY] * len(early))
@@ -164,7 +184,7 @@
         functools.partial(coeff_kernel, count, chips), "coeff",
         [SHAPE((count * rows, n_text), BF16), SHAPE((rows, width), F32)] + [SHAPE((rows, width), BF16)] * (count - 1) + [SHAPE((rows, width), F32)] * two_cores(count),
         [params, pile] + texts, 2 * flops, limit=16 if count == 4 else 40,
-        scratch=[pltpu.VMEM((n_text, width) if chips else (8, 128), BF16), pltpu.VMEM((count * rows, width), F32)])
+        scratch=[pltpu.VMEM((n_text, width) if chips else (16, 128), BF16)])
     text_grad = call(text_kernel, "text_grad", SHAPE((n_text, width), F32), [coeff, pile], flops, limit=16)
     total = reduce_covs(own, parts, count)
     return text_grad[None], total[None]

time: 31.3 us -> 30.9 us (0.987)
  starting transfers between devices: 15 us -> 14.5 us
    ppermute x7 -> x5, starting transfers between devices: 9.48 us -> 5.89 us  [exchange(): lax.ppermute(value, axis, [(i, i ^ k if is_power(count) else (i + k) % co...]
    ppermute x4 -> x6, starting transfers between devices: 5.51 us -> 8.61 us  [mixed(): return lax.ppermute(value, ('blk', 'section'), pairs)]
    ppermute x4 -> x6, waiting for transfers between devices: 5.32 us -> 6.36 us  [mixed(): return lax.ppermute(value, ('blk', 'section'), pairs)]
    ppermute x7 -> x5, waiting for transfers between devices: 4.53 us -> 3.54 us  [exchange(): lax.ppermute(value, axis, [(i, i ^ k if is_power(count) else (i + k) % co...]
    pallas_call x5 -> x6, Pallas kernels: 2.21 us -> 2.22 us  [call(): pl.pallas_call(kernel, out_shape=out_shape, in_specs=specs or [VMEM] * le...]
  transfers between devices with their start and end apart: 11 -> 11, of which waited for: 4 -> 5; matrix products, arithmetic and copies ran while one was open for 4% -> 4% of each run, Pallas kernels for 4% -> 5%
where the time goes in v5:
time: 30.9 us; the launch traced here: 30.7 us
  starting transfers between devices  14.5 us (47%)
  waiting for transfers between devices  9.9 us (32%)
  Pallas kernels  2.22 us (7%)
  between operations  2.05 us (7%)
  local copies, waits for them, and re-layouts  1.14 us (4%)
  other arithmetic  0.87 us (3%)
    ppermute x6, starting transfers between devices, mixed(): return lax.ppermute(value, ('blk', 'section'), pairs)  8.61 us
    ppermute x6, waiting for transfers between devices, mixed(): return lax.ppermute(value, ('blk', 'section'), pairs)  6.36 us
    ppermute x5, starting transfers between devices, exchange(): lax.ppermute(value, axis, [(i, i ^ k if is_power(count) else (i + k) % co...  5.89 us
    ppermute x5, waiting for transfers between devices, exchange(): lax.ppermute(value, axis, [(i, i ^ k if is_power(count) else (i + k) % co...  3.54 us
    pallas_call x6, Pallas kernels, call(): pl.pallas_call(kernel, out_shape=out_shape, in_specs=specs or [VMEM] * le...  2.22 us
    squeeze x1, local copies, waits for them, and re-layouts, fetch_texts(): lax.dynamic_index_in_dim(by_chip, chip ^ k, 0, keepdims=False)  1.11 us
    broadcast_in_dim x1, other arithmetic, local(): return (text_grad[None], total[None])  0.79 us
  transfers between devices with their start and end apart: 11, of which 5 were waited for; matrix products, arithmetic and copies ran while one was open for 4% of the time, Pallas kernels for 5%

profile of v5, /device:TPU:1, one launch (start us, length us, event | category | flops | bytes accessed | tf_op | source)
XLA Modules:
  0.0 30.7 jit_solution(10041023101671343722)
XLA Ops:
  0.6 3.2 %collective-permute-start.1 = (bf16[64,1024]{1,0:T(8,128)(2,1)}, bf16[64,1024]{1,0:T(8,128)(2,1)S(1)}, u32[]{:S(2)}, u32[]{:S(2)}) collective-permute-start(bf16[64,1024]{1,0:T(8,128)(2,1)} %bitcast.19), channel_id=1, source_target_pairs={{0,8},{1,17},{2,10},{3,19},{4,12},{5,21},{6,14},{7,23},{8,0},{9,25... | collective-permute-start | bytes 393224 | tf_op jit(solution)/shard_map/ppermute | solution.py:33
  3.8 1.3 %collective-permute-start = (bf16[64,1024]{1,0:T(8,128)(2,1)}, bf16[64,1024]{1,0:T(8,128)(2,1)S(1)}, u32[]{:S(2)}, u32[]{:S(2)}) collective-permute-start(bf16[64,1024]{1,0:T(8,128)(2,1)} %bitcast.20), channel_id=1, source_target_pairs={{0,16},{1,9},{2,18},{3,11},{4,20},{5,13},{6,22},{7,15},{8,24},{9,1... | collective-permute-start | bytes 393224 | tf_op jit(solution)/shard_map/ppermute | solution.py:33
  5.1 1.1 %dynamic-slice_bitcast_fusion = (bf16[2,32,1024]{2,1,0:T(8,128)(2,1)S(1)}, bf16[2,32,1024]{2,1,0:T(8,128)(2,1)S(1)}, bf16[2,32,1024]{2,1,0:T(8,128)(2,1)S(1)}) fusion(bf16[4,2,32,1024]{3,2,1,0:T(8,128)(2,1)} %bitcast.16, s32[]{:T(128)S(6)} %select_n.43, s32[]{:T(128)S(6)} %select_n.42, s32[]{:T(128)S(6)} %select_n.41), kind=kLoop, calls=%fused_computation.1 | loop fusion | bytes 786444 | tf_op jit(solution)/shard_map/jit(dynamic_index_in_dim)/squeeze | solution.py:165
  6.3 2.2 %collective-permute-start.5 = (bf16[2,32,1024]{2,1,0:T(8,128)(2,1)S(1)}, bf16[2,32,1024]{2,1,0:T(8,128)(2,1)S(1)}, u32[]{:S(2)}, u32[]{:S(2)}) collective-permute-start(bf16[2,32,1024]{2,1,0:T(8,128)(2,1)S(1)} %get-tuple-element.18), channel_id=1, source_target_pairs={{0,6},{1,7},{2,4},{3,5},{4,2},{5,3},{6,0},{7,1},{8,14},{9,15},{10,... | collective-permute-start | bytes 393224 | tf_op jit(solution)/shard_map/ppermute | solution.py:26
  8.5 0.2 collective-permute-start.4
  8.7 0.3 collective-permute-start.3
  9.6 0.0 copy-start.2
  10.3 0.0 copy-done.2
  10.3 0.1 broadcast_select_fusion.refs_5_.params_ref
  10.4 0.0 collective-permute-done.1.second_ref
  10.4 0.1 collective-permute-done.first_ref
  10.5 0.0 copy-start.1
  10.5 1.8 %collective-permute-start.2 = (bf16[64,1024]{1,0:T(8,128)(2,1)S(1)}, bf16[64,1024]{1,0:T(8,128)(2,1)S(1)}, u32[]{:S(2)}, u32[]{:S(2)}) collective-permute-start(bf16[64,1024]{1,0:T(8,128)(2,1)S(1)} %get-tuple-element.11.refs_2_.refs_4_), channel_id=1, source_target_pairs={{0,8},{8,0},{16,24},{24,16},{1,9},{9,1},{17,25},{25,17},{2,10},{10... | collective-permute-start | bytes 393224 | tf_op jit(solution)/shard_map/ppermute | solution.py:26
  12.3 0.0 collective-permute-done.5.refs_3_
  12.4 2.4 %collective-permute-done.4.refs_2_ = bf16[2,32,1024]{2,1,0:T(8,128)(2,1)S(1)} collective-permute-done((bf16[2,32,1024]{2,1,0:T(8,128)(2,1)S(1)}, bf16[2,32,1024]{2,1,0:T(8,128)(2,1)S(1)}, u32[]{:S(2)}, u32[]{:S(2)}) %collective-permute-start.4) | collective-permute-done | bytes 131104 | tf_op jit(solution)/shard_map/ppermute | solution.py:26
  14.8 0.0 collective-permute-done.3.refs_1_
  14.8 0.0 copy-done
  14.8 1.3 %collective-permute-start.6 = (bf16[4,32,1024]{2,1,0:T(8,128)(2,1)S(1)}, bf16[4,32,1024]{2,1,0:T(8,128)(2,1)S(1)}, u32[]{:S(2)}, u32[]{:S(2)}) collective-permute-start(bf16[4,32,1024]{2,1,0:T(8,128)(2,1)S(1)} %select.7), channel_id=1, source_target_pairs={{0,1},{1,0},{2,3},{3,2},{4,5},{5,4},{6,7},{7,6},{8,9},{9,8},{10,11... | collective-permute-start | bytes 786440 | tf_op jit(solution)/shard_map/ppermute | solution.py:26
  16.1 0.0 collective-permute-done.2.refs_3_
  16.1 0.0 copy-done.1
  16.2 1.1 %collective-permute-done.6.refs_4_ = bf16[4,32,1024]{2,1,0:T(8,128)(2,1)S(1)} collective-permute-done((bf16[4,32,1024]{2,1,0:T(8,128)(2,1)S(1)}, bf16[4,32,1024]{2,1,0:T(8,128)(2,1)S(1)}, u32[]{:S(2)}, u32[]{:S(2)}) %collective-permute-start.6) | collective-permute-done | bytes 262176 | tf_op jit(solution)/shard_map/ppermute | solution.py:26
  17.3 0.8 %coeff.1 = (bf16[256,256]{1,0:T(8,128)(2,1)S(1)}, f32[64,1024]{1,0:T(8,128)S(1)}, bf16[64,1024]{1,0:T(8,128)(2,1)S(1)}, bf16[64,1024]{1,0:T(8,128)(2,1)S(1)}, bf...) custom-call(f32[8,256]{1,0:T(8,128)S(1)} %broadcast_select_fusion.refs_5_.params_ref, ...), custom_call_target="tpu_custom_call" | custom-call | flops 268435456 | bytes 1048576 | tf_op jit(solution)/shard_map/coeff/pallas_call | solution.py:122
  18.1 0.2 collective-permute-start.7
  18.4 1.3 %collective-permute-start.8 = (bf16[64,1024]{1,0:T(8,128)(2,1)S(1)}, bf16[64,1024]{1,0:T(8,128)(2,1)S(1)}, u32[]{:S(2)}, u32[]{:S(2)}) collective-permute-start(bf16[64,1024]{1,0:T(8,128)(2,1)S(1)} %get-tuple-element.15), channel_id=1, source_target_pairs={{0,24},{1,9},{2,26},{3,11},{4,28},{5,13},{6,30},{7,15},{8,16},{9,1... | collective-permute-start | bytes 393224 | tf_op jit(solution)/shard_map/ppermute | solution.py:33
  19.6 0.7 %collective-permute-start.9 = (bf16[64,1024]{1,0:T(8,128)(2,1)S(1)}, bf16[64,1024]{1,0:T(8,128)(2,1)S(1)}, u32[]{:S(2)}, u32[]{:S(2)}) collective-permute-start(bf16[64,1024]{1,0:T(8,128)(2,1)S(1)} %get-tuple-element.16), channel_id=1, source_target_pairs={{0,8},{2,10},{4,12},{6,14},{8,0},{10,2},{12,4},{14,6},{16,24},{18,... | collective-permute-start | bytes 393224 | tf_op jit(solution)/shard_map/ppermute | solution.py:33
  20.3 1.7 %collective-permute-done.7.got_ref = bf16[64,1024]{1,0:T(8,128)(2,1)S(1)} collective-permute-done((bf16[64,1024]{1,0:T(8,128)(2,1)S(1)}, bf16[64,1024]{1,0:T(8,128)(2,1)S(1)}, u32[]{:S(2)}, u32[]{:S(2)}) %collective-permute-start.7) | collective-permute-done | bytes 131104 | tf_op jit(solution)/shard_map/ppermute | solution.py:33
  22.0 1.9 %collective-permute-start.10 = (bf16[64,1024]{1,0:T(8,128)(2,1)S(1)}, bf16[64,1024]{1,0:T(8,128)(2,1)S(1)}, u32[]{:S(2)}, u32[]{:S(2)}) collective-permute-start(bf16[64,1024]{1,0:T(8,128)(2,1)S(1)} %add.40), channel_id=1, source_target_pairs={{1,25},{3,27},{5,29},{7,31},{9,17},{11,19},{13,21},{15,23},{17,9},... | collective-permute-start | bytes 393224 | tf_op jit(solution)/shard_map/ppermute | solution.py:33
  24.0 1.3 %text_grad.1 = f32[256,1024]{1,0:T(8,128)} custom-call(bf16[256,256]{1,0:T(8,128)(2,1)S(1)} %get-tuple-element.12.coeff_ref, bf16[256,1024]{1,0:T(8,128)(2,1)S(1)} %pile.1.covs_ref), custom_call_target="tpu_custom_call" | custom-call | flops 134217728 | bytes 1048576 | tf_op jit(solution)/shard_map/text_grad/pallas_call | solution.py:122
  25.3 0.0 collective-permute-done.8
  25.3 0.0 collective-permute-done.9
  25.3 4.6 %collective-permute-done.10 = bf16[64,1024]{1,0:T(8,128)(2,1)S(1)} collective-permute-done((bf16[64,1024]{1,0:T(8,128)(2,1)S(1)}, bf16[64,1024]{1,0:T(8,128)(2,1)S(1)}, u32[]{:S(2)}, u32[]{:S(2)}) %collective-permute-start.10) | collective-permute-done | bytes 131104 | tf_op jit(solution)/shard_map/ppermute | solution.py:33
  29.9 0.8 %add_bitcast_fusion = f32[1,64,1024]{2,1,0:T(8,128)} fusion(bf16[64,1024]{1,0:T(8,128)(2,1)S(1)} %collective-permute-done.10, bf16[64,1024]{1,0:T(8,128)(2,1)S(1)} %collective-permute-done.9, bf16[64,1024]{1,0:T(8,128)(2,1)S(1)} %collective-permute-done.8, f32[64,1024]{1,0:T(8,128)S(1)} %get-tuple-element.13, ...), kind=kLoop, calls=%fused_computation | loop fusion | flops 589824 | bytes 1048577 | tf_op jit(solution)/shard_map/broadcast_in_dim | solution.py:190
  (8 shorter events, 0.1 us)
Async XLA Ops:
  0.6 9.8 %collective-permute-start.1 = (bf16[64,1024]{1,0:T(8,128)(2,1)}, bf16[64,1024]{1,0:T(8,128)(2,1)S(1)}, u32[]{:S(2)}, u32[]{:S(2)}) collective-permute-start(bf16[64,1024]{1,0:T(8,128)(2,1)} %bitcast.19), channel_id=1, source_target_pairs={{0,8},{1,17},{2,10},{3,19},{4,12},{5,21},{6,14},{7,23},{8,0},{9,25... | collective-permute-start | bytes 393224 | tf_op jit(solution)/shard_map/ppermute | solution.py:33
  3.8 6.6 %collective-permute-start = (bf16[64,1024]{1,0:T(8,128)(2,1)}, bf16[64,1024]{1,0:T(8,128)(2,1)S(1)}, u32[]{:S(2)}, u32[]{:S(2)}) collective-permute-start(bf16[64,1024]{1,0:T(8,128)(2,1)} %bitcast.20), channel_id=1, source_target_pairs={{0,16},{1,9},{2,18},{3,11},{4,20},{5,13},{6,22},{7,15},{8,24},{9,1... | collective-permute-start | bytes 393224 | tf_op jit(solution)/shard_map/ppermute | solution.py:33
  5.1 9.6 %copy-start = (bf16[8,32,1024]{2,1,0:T(8,128)(2,1)S(1)}, bf16[8,32,1024]{2,1,0:T(8,128)(2,1)}, u32[]{:S(2)}) copy-start(bf16[8,32,1024]{2,1,0:T(8,128)(2,1)} %param.5) | copy-start | bytes 1572868
  6.3 6.1 %collective-permute-start.5 = (bf16[2,32,1024]{2,1,0:T(8,128)(2,1)S(1)}, bf16[2,32,1024]{2,1,0:T(8,128)(2,1)S(1)}, u32[]{:S(2)}, u32[]{:S(2)}) collective-permute-start(bf16[2,32,1024]{2,1,0:T(8,128)(2,1)S(1)} %get-tuple-element.18), channel_id=1, source_target_pairs={{0,6},{1,7},{2,4},{3,5},{4,2},{5,3},{6,0},{7,1},{8,14},{9,15},{10,... | collective-permute-start | bytes 393224 | tf_op jit(solution)/shard_map/ppermute | solution.py:26
  8.5 6.3 %collective-permute-start.4 = (bf16[2,32,1024]{2,1,0:T(8,128)(2,1)S(1)}, bf16[2,32,1024]{2,1,0:T(8,128)(2,1)S(1)}, u32[]{:S(2)}, u32[]{:S(2)}) collective-permute-start(bf16[2,32,1024]{2,1,0:T(8,128)(2,1)S(1)} %get-tuple-element.19), channel_id=1, source_target_pairs={{0,4},{1,5},{2,6},{3,7},{4,0},{5,1},{6,2},{7,3},{8,12},{9,13},{10,... | collective-permute-start | bytes 393224 | tf_op jit(solution)/shard_map/ppermute | solution.py:26
  8.7 6.1 %collective-permute-start.3 = (bf16[2,32,1024]{2,1,0:T(8,128)(2,1)S(1)}, bf16[2,32,1024]{2,1,0:T(8,128)(2,1)S(1)}, u32[]{:S(2)}, u32[]{:S(2)}) collective-permute-start(bf16[2,32,1024]{2,1,0:T(8,128)(2,1)S(1)} %get-tuple-element.20), channel_id=1, source_target_pairs={{0,2},{1,3},{2,0},{3,1},{4,6},{5,7},{6,4},{7,5},{8,10},{9,11},{10,... | collective-permute-start | bytes 393224 | tf_op jit(solution)/shard_map/ppermute | solution.py:26
  9.6 0.7 %copy-start.2 = (s32[1,256]{1,0:T(1,128)S(1)}, s32[1,256]{1,0:T(1,128)}, u32[]{:S(2)}) copy-start(s32[1,256]{1,0:T(1,128)} %param.7) | copy-start | bytes 3076
  10.5 5.6 %copy-start.1 = (bf16[1,64,1024]{2,1,0:T(8,128)(2,1)S(1)}, bf16[1,64,1024]{2,1,0:T(8,128)(2,1)}, u32[]{:S(2)}) copy-start(bf16[1,64,1024]{2,1,0:T(8,128)(2,1)} %param.6) | copy-start | bytes 393220
  10.5 5.6 %collective-permute-start.2 = (bf16[64,1024]{1,0:T(8,128)(2,1)S(1)}, bf16[64,1024]{1,0:T(8,128)(2,1)S(1)}, u32[]{:S(2)}, u32[]{:S(2)}) collective-permute-start(bf16[64,1024]{1,0:T(8,128)(2,1)S(1)} %get-tuple-element.11.refs_2_.refs_4_), channel_id=1, source_target_pairs={{0,8},{8,0},{16,24},{24,16},{1,9},{9,1},{17,25},{25,17},{2,10},{10... | collective-permute-start | bytes 393224 | tf_op jit(solution)/shard_map/ppermute | solution.py:26
  14.8 2.5 %collective-permute-start.6 = (bf16[4,32,1024]{2,1,0:T(8,128)(2,1)S(1)}, bf16[4,32,1024]{2,1,0:T(8,128)(2,1)S(1)}, u32[]{:S(2)}, u32[]{:S(2)}) collective-permute-start(bf16[4,32,1024]{2,1,0:T(8,128)(2,1)S(1)} %select.7), channel_id=1, source_target_pairs={{0,1},{1,0},{2,3},{3,2},{4,5},{5,4},{6,7},{7,6},{8,9},{9,8},{10,11... | collective-permute-start | bytes 786440 | tf_op jit(solution)/shard_map/ppermute | solution.py:26
  18.1 3.9 %collective-permute-start.7 = (bf16[64,1024]{1,0:T(8,128)(2,1)S(1)}, bf16[64,1024]{1,0:T(8,128)(2,1)S(1)}, u32[]{:S(2)}, u32[]{:S(2)}) collective-permute-start(bf16[64,1024]{1,0:T(8,128)(2,1)S(1)} %get-tuple-element.14), channel_id=1, source_target_pairs={{0,16},{1,9},{2,18},{3,11},{4,20},{5,13},{6,22},{7,15},{8,24},{9,1... | collective-permute-start | bytes 393224 | tf_op jit(solution)/shard_map/ppermute | solution.py:33
  18.4 6.9 %collective-permute-start.8 = (bf16[64,1024]{1,0:T(8,128)(2,1)S(1)}, bf16[64,1024]{1,0:T(8,128)(2,1)S(1)}, u32[]{:S(2)}, u32[]{:S(2)}) collective-permute-start(bf16[64,1024]{1,0:T(8,128)(2,1)S(1)} %get-tuple-element.15), channel_id=1, source_target_pairs={{0,24},{1,9},{2,26},{3,11},{4,28},{5,13},{6,30},{7,15},{8,16},{9,1... | collective-permute-start | bytes 393224 | tf_op jit(solution)/shard_map/ppermute | solution.py:33
  19.6 5.6 %collective-permute-start.9 = (bf16[64,1024]{1,0:T(8,128)(2,1)S(1)}, bf16[64,1024]{1,0:T(8,128)(2,1)S(1)}, u32[]{:S(2)}, u32[]{:S(2)}) collective-permute-start(bf16[64,1024]{1,0:T(8,128)(2,1)S(1)} %get-tuple-element.16), channel_id=1, source_target_pairs={{0,8},{2,10},{4,12},{6,14},{8,0},{10,2},{12,4},{14,6},{16,24},{18,... | collective-permute-start | bytes 393224 | tf_op jit(solution)/shard_map/ppermute | solution.py:33
  22.0 7.9 %collective-permute-start.10 = (bf16[64,1024]{1,0:T(8,128)(2,1)S(1)}, bf16[64,1024]{1,0:T(8,128)(2,1)S(1)}, u32[]{:S(2)}, u32[]{:S(2)}) collective-permute-start(bf16[64,1024]{1,0:T(8,128)(2,1)S(1)} %add.40), channel_id=1, source_target_pairs={{1,25},{3,27},{5,29},{7,31},{9,17},{11,19},{13,21},{15,23},{17,9},... | collective-permute-start | bytes 393224 | tf_op jit(solution)/shard_map/ppermute | solution.py:33

commit v6 on v5

--- a/solution.py
+++ b/solution.py
@@ -109,11 +109,12 @@
                 ref[:, columns] = block.astype(BF16)
 
 
-def add_kernel(part_ref, got_ref, out_ref):
+def add_kernel(part_ref, got_ref, token_ref, out_ref):
     out_ref[...] = (part_ref[...] + got_ref[...].astype(F32)).astype(BF16)
 
 
-def text_kernel(coeff_ref, covs_ref, out_ref):
+def text_kernel(coeff_ref, covs_ref, out_ref, token_ref):
+    token_ref[...] = jnp.zeros_like(token_ref)
     out_ref[...] = lax.dot_general(coeff_ref[...], covs_ref[...], TN, preferred_element_type=F32)
 
 
@@ -135,13 +136,13 @@
     return count == 4 and lax.axis_size("section") % 2 == 0
 
 
-def reduce_covs(own, parts, count):
+def reduce_covs(own, parts, count, token):
     if not two_cores(count):
         got = [exchange(part, "blk", k if is_power(count) else -k) for k, part in enumerate(parts, 1)]
         return sum((part.astype(F32) for part in got), own)
     first, second, third, far = parts
     got = [mixed(first, 2, 1), mixed(second, 3, 1), mixed(third, 1, 0)]
-    summed = call(add_kernel, "add", SHAPE(far.shape, BF16), [far, got[0]], 0)
+    summed = call(add_kernel, "add", SHAPE(far.shape, BF16), [far, got[0], token], 0)
     got.append(mixed(summed, 0, 3))
     odd = lax.axis_index("section") % 2 == 1
     return own + jnp.where(odd, 0, got[0].astype(F32)) + sum(part.astype(F32) for part in got[1:])
@@ -185,8 +186,8 @@
         [SHAPE((count * rows, n_text), BF16), SHAPE((rows, width), F32)] + [SHAPE((rows, width), BF16)] * (count - 1) + [SHAPE((rows, width), F32)] * two_cores(count),
         [params, pile] + texts, 2 * flops, limit=16 if count == 4 else 40,
         scratch=[pltpu.VMEM((n_text, width) if chips else (16, 128), BF16)])
-    text_grad = call(text_kernel, "text_grad", SHAPE((n_text, width), F32), [coeff, pile], flops, limit=16)
-    total = reduce_covs(own, parts, count)
+    text_grad, token = call(text_kernel, "text_grad", [SHAPE((n_text, width), F32), SHAPE((8, 128), F32)], [coeff, pile], flops, limit=16)
+    total = reduce_covs(own, parts, count, token)
     return text_grad[None], total[None]
 
 

time: 30.9 us -> 30.9 us (level)
  transfers between devices with their start and end apart: 11 -> 11, of which waited for: 5 -> 6; matrix products, arithmetic and copies ran while one was open for 4% -> 4% of each run, Pallas kernels for 5% -> 5%
where the time goes in v6:
time: 30.9 us; the launch traced here: 30.7 us
  starting transfers between devices  14.5 us (47%)
  waiting for transfers between devices  9.89 us (32%)
  Pallas kernels  2.23 us (7%)
  between operations  2.04 us (7%)
  local copies, waits for them, and re-layouts  1.14 us (4%)
  other arithmetic  0.87 us (3%)
    ppermute x6, starting transfers between devices, mixed(): return lax.ppermute(value, ('blk', 'section'), pairs)  8.61 us
    ppermute x6, waiting for transfers between devices, mixed(): return lax.ppermute(value, ('blk', 'section'), pairs)  6.36 us
    ppermute x5, starting transfers between devices, exchange(): lax.ppermute(value, axis, [(i, i ^ k if is_power(count) else (i + k) % co...  5.89 us
    ppermute x5, waiting for transfers between devices, exchange(): lax.ppermute(value, axis, [(i, i ^ k if is_power(count) else (i + k) % co...  3.53 us
    pallas_call x6, Pallas kernels, call(): pl.pallas_call(kernel, out_shape=out_shape, in_specs=specs or [VMEM] * le...  2.23 us
    squeeze x1, local copies, waits for them, and re-layouts, fetch_texts(): lax.dynamic_index_in_dim(by_chip, chip ^ k, 0, keepdims=False)  1.11 us
    broadcast_in_dim x1, other arithmetic, local(): return (text_grad[None], total[None])  0.79 us
  transfers between devices with their start and end apart: 11, of which 6 were waited for; matrix products, arithmetic and copies ran while one was open for 4% of the time, Pallas kernels for 5%

profile of v6, /device:TPU:1, one launch (start us, length us, event | category | flops | bytes accessed | tf_op | source)
XLA Modules:
  0.0 30.7 jit_solution(14762363607919932614)
XLA Ops:
  0.6 3.2 %collective-permute-start.1 = (bf16[64,1024]{1,0:T(8,128)(2,1)}, bf16[64,1024]{1,0:T(8,128)(2,1)S(1)}, u32[]{:S(2)}, u32[]{:S(2)}) collective-permute-start(bf16[64,1024]{1,0:T(8,128)(2,1)} %bitcast.19), channel_id=1, source_target_pairs={{0,8},{1,17},{2,10},{3,19},{4,12},{5,21},{6,14},{7,23},{8,0},{9,25... | collective-permute-start | bytes 393224 | tf_op jit(solution)/shard_map/ppermute | solution.py:33
  3.8 1.3 %collective-permute-start = (bf16[64,1024]{1,0:T(8,128)(2,1)}, bf16[64,1024]{1,0:T(8,128)(2,1)S(1)}, u32[]{:S(2)}, u32[]{:S(2)}) collective-permute-start(bf16[64,1024]{1,0:T(8,128)(2,1)} %bitcast.20), channel_id=1, source_target_pairs={{0,16},{1,9},{2,18},{3,11},{4,20},{5,13},{6,22},{7,15},{8,24},{9,1... | collective-permute-start | bytes 393224 | tf_op jit(solution)/shard_map/ppermute | solution.py:33
  5.1 1.1 %dynamic-slice_bitcast_fusion = (bf16[2,32,1024]{2,1,0:T(8,128)(2,1)S(1)}, bf16[2,32,1024]{2,1,0:T(8,128)(2,1)S(1)}, bf16[2,32,1024]{2,1,0:T(8,128)(2,1)S(1)}) fusion(bf16[4,2,32,1024]{3,2,1,0:T(8,128)(2,1)} %bitcast.16, s32[]{:T(128)S(6)} %select_n.43, s32[]{:T(128)S(6)} %select_n.42, s32[]{:T(128)S(6)} %select_n.41), kind=kLoop, calls=%fused_computation.1 | loop fusion | bytes 786444 | tf_op jit(solution)/shard_map/jit(dynamic_index_in_dim)/squeeze | solution.py:166
  6.2 2.2 %collective-permute-start.5 = (bf16[2,32,1024]{2,1,0:T(8,128)(2,1)S(1)}, bf16[2,32,1024]{2,1,0:T(8,128)(2,1)S(1)}, u32[]{:S(2)}, u32[]{:S(2)}) collective-permute-start(bf16[2,32,1024]{2,1,0:T(8,128)(2,1)S(1)} %get-tuple-element.22), channel_id=1, source_target_pairs={{0,6},{1,7},{2,4},{3,5},{4,2},{5,3},{6,0},{7,1},{8,14},{9,15},{10,... | collective-permute-start | bytes 393224 | tf_op jit(solution)/shard_map/ppermute | solution.py:26
  8.5 0.2 collective-permute-start.4
  8.7 0.3 collective-permute-start.3
  9.6 0.0 copy-start.2
  10.3 0.0 copy-done.2
  10.3 0.1 broadcast_select_fusion.refs_5_.params_ref
  10.4 0.0 collective-permute-done.1.second_ref
  10.4 0.1 collective-permute-done.first_ref
  10.5 0.0 copy-start.1
  10.5 1.8 %collective-permute-start.2 = (bf16[64,1024]{1,0:T(8,128)(2,1)S(1)}, bf16[64,1024]{1,0:T(8,128)(2,1)S(1)}, u32[]{:S(2)}, u32[]{:S(2)}) collective-permute-start(bf16[64,1024]{1,0:T(8,128)(2,1)S(1)} %get-tuple-element.13.refs_2_.refs_4_), channel_id=1, source_target_pairs={{0,8},{8,0},{16,24},{24,16},{1,9},{9,1},{17,25},{25,17},{2,10},{10... | collective-permute-start | bytes 393224 | tf_op jit(solution)/shard_map/ppermute | solution.py:26
  12.3 0.0 collective-permute-done.5.refs_3_
  12.4 2.4 %collective-permute-done.4.refs_2_ = bf16[2,32,1024]{2,1,0:T(8,128)(2,1)S(1)} collective-permute-done((bf16[2,32,1024]{2,1,0:T(8,128)(2,1)S(1)}, bf16[2,32,1024]{2,1,0:T(8,128)(2,1)S(1)}, u32[]{:S(2)}, u32[]{:S(2)}) %collective-permute-start.4) | collective-permute-done | bytes 131104 | tf_op jit(solution)/shard_map/ppermute | solution.py:26
  14.8 0.0 collective-permute-done.3.refs_1_
  14.8 0.0 copy-done
  14.8 1.3 %collective-permute-start.6 = (bf16[4,32,1024]{2,1,0:T(8,128)(2,1)S(1)}, bf16[4,32,1024]{2,1,0:T(8,128)(2,1)S(1)}, u32[]{:S(2)}, u32[]{:S(2)}) collective-permute-start(bf16[4,32,1024]{2,1,0:T(8,128)(2,1)S(1)} %select.7), channel_id=1, source_target_pairs={{0,1},{1,0},{2,3},{3,2},{4,5},{5,4},{6,7},{7,6},{8,9},{9,8},{10,11... | collective-permute-start | bytes 786440 | tf_op jit(solution)/shard_map/ppermute | solution.py:26
  16.1 0.0 collective-permute-done.2.refs_3_
  16.1 0.0 copy-done.1
  16.2 1.1 %collective-permute-done.6.refs_4_ = bf16[4,32,1024]{2,1,0:T(8,128)(2,1)S(1)} collective-permute-done((bf16[4,32,1024]{2,1,0:T(8,128)(2,1)S(1)}, bf16[4,32,1024]{2,1,0:T(8,128)(2,1)S(1)}, u32[]{:S(2)}, u32[]{:S(2)}) %collective-permute-start.6) | collective-permute-done | bytes 262176 | tf_op jit(solution)/shard_map/ppermute | solution.py:26
  17.3 0.8 %coeff.1 = (bf16[256,256]{1,0:T(8,128)(2,1)S(1)}, f32[64,1024]{1,0:T(8,128)S(1)}, bf16[64,1024]{1,0:T(8,128)(2,1)S(1)}, bf16[64,1024]{1,0:T(8,128)(2,1)S(1)}, bf...) custom-call(f32[8,256]{1,0:T(8,128)S(1)} %broadcast_select_fusion.refs_5_.params_ref, ...), custom_call_target="tpu_custom_call" | custom-call | flops 268435456 | bytes 1048576 | tf_op jit(solution)/shard_map/coeff/pallas_call | solution.py:123
  18.1 0.2 collective-permute-start.7
  18.4 1.3 %collective-permute-start.8 = (bf16[64,1024]{1,0:T(8,128)(2,1)S(1)}, bf16[64,1024]{1,0:T(8,128)(2,1)S(1)}, u32[]{:S(2)}, u32[]{:S(2)}) collective-permute-start(bf16[64,1024]{1,0:T(8,128)(2,1)S(1)} %get-tuple-element.18), channel_id=1, source_target_pairs={{0,24},{1,9},{2,26},{3,11},{4,28},{5,13},{6,30},{7,15},{8,16},{9,1... | collective-permute-start | bytes 393224 | tf_op jit(solution)/shard_map/ppermute | solution.py:33
  19.6 0.7 %collective-permute-start.9 = (bf16[64,1024]{1,0:T(8,128)(2,1)S(1)}, bf16[64,1024]{1,0:T(8,128)(2,1)S(1)}, u32[]{:S(2)}, u32[]{:S(2)}) collective-permute-start(bf16[64,1024]{1,0:T(8,128)(2,1)S(1)} %get-tuple-element.19), channel_id=1, source_target_pairs={{0,8},{2,10},{4,12},{6,14},{8,0},{10,2},{12,4},{14,6},{16,24},{18,... | collective-permute-start | bytes 393224 | tf_op jit(solution)/shard_map/ppermute | solution.py:33
  20.3 1.3 %text_grad.1 = (f32[256,1024]{1,0:T(8,128)}, f32[8,128]{1,0:T(8,128)S(1)}) custom-call(bf16[256,256]{1,0:T(8,128)(2,1)S(1)} %get-tuple-element.14.coeff_ref, bf16[256,1024]{1,0:T(8,128)(2,1)S(1)} %pile.1.covs_ref), custom_call_target="tpu_custom_call" | custom-call | flops 134217728 | bytes 1048576 | tf_op jit(solution)/shard_map/text_grad/pallas_call | solution.py:123
  21.6 0.4 %collective-permute-done.7.got_ref = bf16[64,1024]{1,0:T(8,128)(2,1)S(1)} collective-permute-done((bf16[64,1024]{1,0:T(8,128)(2,1)S(1)}, bf16[64,1024]{1,0:T(8,128)(2,1)S(1)}, u32[]{:S(2)}, u32[]{:S(2)}) %collective-permute-start.7) | collective-permute-done | bytes 131104 | tf_op jit(solution)/shard_map/ppermute | solution.py:33
  22.0 1.9 %collective-permute-start.10 = (bf16[64,1024]{1,0:T(8,128)(2,1)S(1)}, bf16[64,1024]{1,0:T(8,128)(2,1)S(1)}, u32[]{:S(2)}, u32[]{:S(2)}) collective-permute-start(bf16[64,1024]{1,0:T(8,128)(2,1)S(1)} %add.40), channel_id=1, source_target_pairs={{1,25},{3,27},{5,29},{7,31},{9,17},{11,19},{13,21},{15,23},{17,9},... | collective-permute-start | bytes 393224 | tf_op jit(solution)/shard_map/ppermute | solution.py:33
  24.0 0.7 %collective-permute-done.8 = bf16[64,1024]{1,0:T(8,128)(2,1)S(1)} collective-permute-done((bf16[64,1024]{1,0:T(8,128)(2,1)S(1)}, bf16[64,1024]{1,0:T(8,128)(2,1)S(1)}, u32[]{:S(2)}, u32[]{:S(2)}) %collective-permute-start.8) | collective-permute-done | bytes 131104 | tf_op jit(solution)/shard_map/ppermute | solution.py:33
  24.7 0.0 collective-permute-done.9
  24.7 5.2 %collective-permute-done.10 = bf16[64,1024]{1,0:T(8,128)(2,1)S(1)} collective-permute-done((bf16[64,1024]{1,0:T(8,128)(2,1)S(1)}, bf16[64,1024]{1,0:T(8,128)(2,1)S(1)}, u32[]{:S(2)}, u32[]{:S(2)}) %collective-permute-start.10) | collective-permute-done | bytes 131104 | tf_op jit(solution)/shard_map/ppermute | solution.py:33
  29.9 0.8 %add_bitcast_fusion = f32[1,64,1024]{2,1,0:T(8,128)} fusion(bf16[64,1024]{1,0:T(8,128)(2,1)S(1)} %collective-permute-done.10, bf16[64,1024]{1,0:T(8,128)(2,1)S(1)} %collective-permute-done.9, bf16[64,1024]{1,0:T(8,128)(2,1)S(1)} %collective-permute-done.8, f32[64,1024]{1,0:T(8,128)S(1)} %get-tuple-element.16, ...), kind=kLoop, calls=%fused_computation | loop fusion | flops 589824 | bytes 1048577 | tf_op jit(solution)/shard_map/broadcast_in_dim | solution.py:191
  (8 shorter events, 0.1 us)
Async XLA Ops:
  0.6 9.8 %collective-permute-start.1 = (bf16[64,1024]{1,0:T(8,128)(2,1)}, bf16[64,1024]{1,0:T(8,128)(2,1)S(1)}, u32[]{:S(2)}, u32[]{:S(2)}) collective-permute-start(bf16[64,1024]{1,0:T(8,128)(2,1)} %bitcast.19), channel_id=1, source_target_pairs={{0,8},{1,17},{2,10},{3,19},{4,12},{5,21},{6,14},{7,23},{8,0},{9,25... | collective-permute-start | bytes 393224 | tf_op jit(solution)/shard_map/ppermute | solution.py:33
  3.8 6.6 %collective-permute-start = (bf16[64,1024]{1,0:T(8,128)(2,1)}, bf16[64,1024]{1,0:T(8,128)(2,1)S(1)}, u32[]{:S(2)}, u32[]{:S(2)}) collective-permute-start(bf16[64,1024]{1,0:T(8,128)(2,1)} %bitcast.20), channel_id=1, source_target_pairs={{0,16},{1,9},{2,18},{3,11},{4,20},{5,13},{6,22},{7,15},{8,24},{9,1... | collective-permute-start | bytes 393224 | tf_op jit(solution)/shard_map/ppermute | solution.py:33
  5.1 9.6 %copy-start = (bf16[8,32,1024]{2,1,0:T(8,128)(2,1)S(1)}, bf16[8,32,1024]{2,1,0:T(8,128)(2,1)}, u32[]{:S(2)}) copy-start(bf16[8,32,1024]{2,1,0:T(8,128)(2,1)} %param.5) | copy-start | bytes 1572868
  6.2 6.1 %collective-permute-start.5 = (bf16[2,32,1024]{2,1,0:T(8,128)(2,1)S(1)}, bf16[2,32,1024]{2,1,0:T(8,128)(2,1)S(1)}, u32[]{:S(2)}, u32[]{:S(2)}) collective-permute-start(bf16[2,32,1024]{2,1,0:T(8,128)(2,1)S(1)} %get-tuple-element.22), channel_id=1, source_target_pairs={{0,6},{1,7},{2,4},{3,5},{4,2},{5,3},{6,0},{7,1},{8,14},{9,15},{10,... | collective-permute-start | bytes 393224 | tf_op jit(solution)/shard_map/ppermute | solution.py:26
  8.5 6.3 %collective-permute-start.4 = (bf16[2,32,1024]{2,1,0:T(8,128)(2,1)S(1)}, bf16[2,32,1024]{2,1,0:T(8,128)(2,1)S(1)}, u32[]{:S(2)}, u32[]{:S(2)}) collective-permute-start(bf16[2,32,1024]{2,1,0:T(8,128)(2,1)S(1)} %get-tuple-element.23), channel_id=1, source_target_pairs={{0,4},{1,5},{2,6},{3,7},{4,0},{5,1},{6,2},{7,3},{8,12},{9,13},{10,... | collective-permute-start | bytes 393224 | tf_op jit(solution)/shard_map/ppermute | solution.py:26
  8.7 6.1 %collective-permute-start.3 = (bf16[2,32,1024]{2,1,0:T(8,128)(2,1)S(1)}, bf16[2,32,1024]{2,1,0:T(8,128)(2,1)S(1)}, u32[]{:S(2)}, u32[]{:S(2)}) collective-permute-start(bf16[2,32,1024]{2,1,0:T(8,128)(2,1)S(1)} %get-tuple-element.24), channel_id=1, source_target_pairs={{0,2},{1,3},{2,0},{3,1},{4,6},{5,7},{6,4},{7,5},{8,10},{9,11},{10,... | collective-permute-start | bytes 393224 | tf_op jit(solution)/shard_map/ppermute | solution.py:26
  9.6 0.7 %copy-start.2 = (s32[1,256]{1,0:T(1,128)S(1)}, s32[1,256]{1,0:T(1,128)}, u32[]{:S(2)}) copy-start(s32[1,256]{1,0:T(1,128)} %param.7) | copy-start | bytes 3076
  10.5 5.6 %copy-start.1 = (bf16[1,64,1024]{2,1,0:T(8,128)(2,1)S(1)}, bf16[1,64,1024]{2,1,0:T(8,128)(2,1)}, u32[]{:S(2)}) copy-start(bf16[1,64,1024]{2,1,0:T(8,128)(2,1)} %param.6) | copy-start | bytes 393220
  10.5 5.6 %collective-permute-start.2 = (bf16[64,1024]{1,0:T(8,128)(2,1)S(1)}, bf16[64,1024]{1,0:T(8,128)(2,1)S(1)}, u32[]{:S(2)}, u32[]{:S(2)}) collective-permute-start(bf16[64,1024]{1,0:T(8,128)(2,1)S(1)} %get-tuple-element.13.refs_2_.refs_4_), channel_id=1, source_target_pairs={{0,8},{8,0},{16,24},{24,16},{1,9},{9,1},{17,25},{25,17},{2,10},{10... | collective-permute-start | bytes 393224 | tf_op jit(solution)/shard_map/ppermute | solution.py:26
  14.8 2.5 %collective-permute-start.6 = (bf16[4,32,1024]{2,1,0:T(8,128)(2,1)S(1)}, bf16[4,32,1024]{2,1,0:T(8,128)(2,1)S(1)}, u32[]{:S(2)}, u32[]{:S(2)}) collective-permute-start(bf16[4,32,1024]{2,1,0:T(8,128)(2,1)S(1)} %select.7), channel_id=1, source_target_pairs={{0,1},{1,0},{2,3},{3,2},{4,5},{5,4},{6,7},{7,6},{8,9},{9,8},{10,11... | collective-permute-start | bytes 786440 | tf_op jit(solution)/shard_map/ppermute | solution.py:26
  18.1 3.9 %collective-permute-start.7 = (bf16[64,1024]{1,0:T(8,128)(2,1)S(1)}, bf16[64,1024]{1,0:T(8,128)(2,1)S(1)}, u32[]{:S(2)}, u32[]{:S(2)}) collective-permute-start(bf16[64,1024]{1,0:T(8,128)(2,1)S(1)} %get-tuple-element.17), channel_id=1, source_target_pairs={{0,16},{1,9},{2,18},{3,11},{4,20},{5,13},{6,22},{7,15},{8,24},{9,1... | collective-permute-start | bytes 393224 | tf_op jit(solution)/shard_map/ppermute | solution.py:33
  18.4 6.3 %collective-permute-start.8 = (bf16[64,1024]{1,0:T(8,128)(2,1)S(1)}, bf16[64,1024]{1,0:T(8,128)(2,1)S(1)}, u32[]{:S(2)}, u32[]{:S(2)}) collective-permute-start(bf16[64,1024]{1,0:T(8,128)(2,1)S(1)} %get-tuple-element.18), channel_id=1, source_target_pairs={{0,24},{1,9},{2,26},{3,11},{4,28},{5,13},{6,30},{7,15},{8,16},{9,1... | collective-permute-start | bytes 393224 | tf_op jit(solution)/shard_map/ppermute | solution.py:33
  19.6 5.0 %collective-permute-start.9 = (bf16[64,1024]{1,0:T(8,128)(2,1)S(1)}, bf16[64,1024]{1,0:T(8,128)(2,1)S(1)}, u32[]{:S(2)}, u32[]{:S(2)}) collective-permute-start(bf16[64,1024]{1,0:T(8,128)(2,1)S(1)} %get-tuple-element.19), channel_id=1, source_target_pairs={{0,8},{2,10},{4,12},{6,14},{8,0},{10,2},{12,4},{14,6},{16,24},{18,... | collective-permute-start | bytes 393224 | tf_op jit(solution)/shard_map/ppermute | solution.py:33
  22.0 7.8 %collective-permute-start.10 = (bf16[64,1024]{1,0:T(8,128)(2,1)S(1)}, bf16[64,1024]{1,0:T(8,128)(2,1)S(1)}, u32[]{:S(2)}, u32[]{:S(2)}) collective-permute-start(bf16[64,1024]{1,0:T(8,128)(2,1)S(1)} %add.40), channel_id=1, source_target_pairs={{1,25},{3,27},{5,29},{7,31},{9,17},{11,19},{13,21},{15,23},{17,9},... | collective-permute-start | bytes 393224 | tf_op jit(solution)/shard_map/ppermute | solution.py:33

commit v7 on v5

--- a/solution.py
+++ b/solution.py
@@ -140,7 +140,8 @@
         got = [exchange(part, "blk", k if is_power(count) else -k) for k, part in enumerate(parts, 1)]
         return sum((part.astype(F32) for part in got), own)
     first, second, third, far = parts
-    got = [mixed(first, 2, 1), mixed(second, 3, 1), mixed(third, 1, 0)]
+    near = mixed(third, 1, 0)
+    got = [mixed(first, 2, 1), mixed(second, 3, 1), near]
     summed = call(add_kernel, "add", SHAPE(far.shape, BF16), [far, got[0]], 0)
     got.append(mixed(summed, 0, 3))
     odd = lax.axis_index("section") % 2 == 1

time: 30.9 us -> 30.9 us (level)
  no operation moved by 1% of the time
where the time goes in v7:
time: 30.9 us; the launch traced here: 30.7 us
  starting transfers between devices  14.5 us (47%)
  waiting for transfers between devices  9.9 us (32%)
  Pallas kernels  2.22 us (7%)
  between operations  2.05 us (7%)
  local copies, waits for them, and re-layouts  1.14 us (4%)
  other arithmetic  0.87 us (3%)
    ppermute x6, starting transfers between devices, mixed(): return lax.ppermute(value, ('blk', 'section'), pairs)  8.61 us
    ppermute x6, waiting for transfers between devices, mixed(): return lax.ppermute(value, ('blk', 'section'), pairs)  6.36 us
    ppermute x5, starting transfers between devices, exchange(): lax.ppermute(value, axis, [(i, i ^ k if is_power(count) else (i + k) % co...  5.89 us
    ppermute x5, waiting for transfers between devices, exchange(): lax.ppermute(value, axis, [(i, i ^ k if is_power(count) else (i + k) % co...  3.54 us
    pallas_call x6, Pallas kernels, call(): pl.pallas_call(kernel, out_shape=out_shape, in_specs=specs or [VMEM] * le...  2.22 us
    squeeze x1, local copies, waits for them, and re-layouts, fetch_texts(): lax.dynamic_index_in_dim(by_chip, chip ^ k, 0, keepdims=False)  1.11 us
    broadcast_in_dim x1, other arithmetic, local(): return (text_grad[None], total[None])  0.79 us
  transfers between devices with their start and end apart: 11, of which 5 were waited for; matrix products, arithmetic and copies ran while one was open for 4% of the time, Pallas kernels for 5%

profile of v7, /device:TPU:1, one launch (start us, length us, event | category | flops | bytes accessed | tf_op | source)
XLA Modules:
  0.0 30.7 jit_solution(10041023101671343722)
XLA Ops:
  0.6 3.2 %collective-permute-start.1 = (bf16[64,1024]{1,0:T(8,128)(2,1)}, bf16[64,1024]{1,0:T(8,128)(2,1)S(1)}, u32[]{:S(2)}, u32[]{:S(2)}) collective-permute-start(bf16[64,1024]{1,0:T(8,128)(2,1)} %bitcast.19), channel_id=1, source_target_pairs={{0,8},{1,17},{2,10},{3,19},{4,12},{5,21},{6,14},{7,23},{8,0},{9,25... | collective-permute-start | bytes 393224 | tf_op jit(solution)/shard_map/ppermute | solution.py:33
  3.8 1.3 %collective-permute-start = (bf16[64,1024]{1,0:T(8,128)(2,1)}, bf16[64,1024]{1,0:T(8,128)(2,1)S(1)}, u32[]{:S(2)}, u32[]{:S(2)}) collective-permute-start(bf16[64,1024]{1,0:T(8,128)(2,1)} %bitcast.20), channel_id=1, source_target_pairs={{0,16},{1,9},{2,18},{3,11},{4,20},{5,13},{6,22},{7,15},{8,24},{9,1... | collective-permute-start | bytes 393224 | tf_op jit(solution)/shard_map/ppermute | solution.py:33
  5.1 1.1 %dynamic-slice_bitcast_fusion = (bf16[2,32,1024]{2,1,0:T(8,128)(2,1)S(1)}, bf16[2,32,1024]{2,1,0:T(8,128)(2,1)S(1)}, bf16[2,32,1024]{2,1,0:T(8,128)(2,1)S(1)}) fusion(bf16[4,2,32,1024]{3,2,1,0:T(8,128)(2,1)} %bitcast.16, s32[]{:T(128)S(6)} %select_n.43, s32[]{:T(128)S(6)} %select_n.42, s32[]{:T(128)S(6)} %select_n.41), kind=kLoop, calls=%fused_computation.1 | loop fusion | bytes 786444 | tf_op jit(solution)/shard_map/jit(dynamic_index_in_dim)/squeeze | solution.py:166
  6.3 2.2 %collective-permute-start.5 = (bf16[2,32,1024]{2,1,0:T(8,128)(2,1)S(1)}, bf16[2,32,1024]{2,1,0:T(8,128)(2,1)S(1)}, u32[]{:S(2)}, u32[]{:S(2)}) collective-permute-start(bf16[2,32,1024]{2,1,0:T(8,128)(2,1)S(1)} %get-tuple-element.18), channel_id=1, source_target_pairs={{0,6},{1,7},{2,4},{3,5},{4,2},{5,3},{6,0},{7,1},{8,14},{9,15},{10,... | collective-permute-start | bytes 393224 | tf_op jit(solution)/shard_map/ppermute | solution.py:26
  8.5 0.2 collective-permute-start.4
  8.7 0.3 collective-permute-start.3
  9.6 0.0 copy-start.2
  10.3 0.0 copy-done.2
  10.3 0.1 broadcast_select_fusion.refs_5_.params_ref
  10.4 0.0 collective-permute-done.1.second_ref
  10.4 0.1 collective-permute-done.first_ref
  10.5 0.0 copy-start.1
  10.5 1.8 %collective-permute-start.2 = (bf16[64,1024]{1,0:T(8,128)(2,1)S(1)}, bf16[64,1024]{1,0:T(8,128)(2,1)S(1)}, u32[]{:S(2)}, u32[]{:S(2)}) collective-permute-start(bf16[64,1024]{1,0:T(8,128)(2,1)S(1)} %get-tuple-element.11.refs_2_.refs_4_), channel_id=1, source_target_pairs={{0,8},{8,0},{16,24},{24,16},{1,9},{9,1},{17,25},{25,17},{2,10},{10... | collective-permute-start | bytes 393224 | tf_op jit(solution)/shard_map/ppermute | solution.py:26
  12.3 0.0 collective-permute-done.5.refs_3_
  12.4 2.4 %collective-permute-done.4.refs_2_ = bf16[2,32,1024]{2,1,0:T(8,128)(2,1)S(1)} collective-permute-done((bf16[2,32,1024]{2,1,0:T(8,128)(2,1)S(1)}, bf16[2,32,1024]{2,1,0:T(8,128)(2,1)S(1)}, u32[]{:S(2)}, u32[]{:S(2)}) %collective-permute-start.4) | collective-permute-done | bytes 131104 | tf_op jit(solution)/shard_map/ppermute | solution.py:26
  14.8 0.0 collective-permute-done.3.refs_1_
  14.8 0.0 copy-done
  14.8 1.3 %collective-permute-start.6 = (bf16[4,32,1024]{2,1,0:T(8,128)(2,1)S(1)}, bf16[4,32,1024]{2,1,0:T(8,128)(2,1)S(1)}, u32[]{:S(2)}, u32[]{:S(2)}) collective-permute-start(bf16[4,32,1024]{2,1,0:T(8,128)(2,1)S(1)} %select.7), channel_id=1, source_target_pairs={{0,1},{1,0},{2,3},{3,2},{4,5},{5,4},{6,7},{7,6},{8,9},{9,8},{10,11... | collective-permute-start | bytes 786440 | tf_op jit(solution)/shard_map/ppermute | solution.py:26
  16.1 0.0 collective-permute-done.2.refs_3_
  16.1 0.0 copy-done.1
  16.2 1.1 %collective-permute-done.6.refs_4_ = bf16[4,32,1024]{2,1,0:T(8,128)(2,1)S(1)} collective-permute-done((bf16[4,32,1024]{2,1,0:T(8,128)(2,1)S(1)}, bf16[4,32,1024]{2,1,0:T(8,128)(2,1)S(1)}, u32[]{:S(2)}, u32[]{:S(2)}) %collective-permute-start.6) | collective-permute-done | bytes 262176 | tf_op jit(solution)/shard_map/ppermute | solution.py:26
  17.3 0.8 %coeff.1 = (bf16[256,256]{1,0:T(8,128)(2,1)S(1)}, f32[64,1024]{1,0:T(8,128)S(1)}, bf16[64,1024]{1,0:T(8,128)(2,1)S(1)}, bf16[64,1024]{1,0:T(8,128)(2,1)S(1)}, bf...) custom-call(f32[8,256]{1,0:T(8,128)S(1)} %broadcast_select_fusion.refs_5_.params_ref, ...), custom_call_target="tpu_custom_call" | custom-call | flops 268435456 | bytes 1048576 | tf_op jit(solution)/shard_map/coeff/pallas_call | solution.py:122
  18.1 0.2 collective-permute-start.7
  18.4 1.3 %collective-permute-start.8 = (bf16[64,1024]{1,0:T(8,128)(2,1)S(1)}, bf16[64,1024]{1,0:T(8,128)(2,1)S(1)}, u32[]{:S(2)}, u32[]{:S(2)}) collective-permute-start(bf16[64,1024]{1,0:T(8,128)(2,1)S(1)} %get-tuple-element.15), channel_id=1, source_target_pairs={{0,24},{1,9},{2,26},{3,11},{4,28},{5,13},{6,30},{7,15},{8,16},{9,1... | collective-permute-start | bytes 393224 | tf_op jit(solution)/shard_map/ppermute | solution.py:33
  19.6 0.7 %collective-permute-start.9 = (bf16[64,1024]{1,0:T(8,128)(2,1)S(1)}, bf16[64,1024]{1,0:T(8,128)(2,1)S(1)}, u32[]{:S(2)}, u32[]{:S(2)}) collective-permute-start(bf16[64,1024]{1,0:T(8,128)(2,1)S(1)} %get-tuple-element.16), channel_id=1, source_target_pairs={{0,8},{2,10},{4,12},{6,14},{8,0},{10,2},{12,4},{14,6},{16,24},{18,... | collective-permute-start | bytes 393224 | tf_op jit(solution)/shard_map/ppermute | solution.py:33
  20.3 1.7 %collective-permute-done.7.got_ref = bf16[64,1024]{1,0:T(8,128)(2,1)S(1)} collective-permute-done((bf16[64,1024]{1,0:T(8,128)(2,1)S(1)}, bf16[64,1024]{1,0:T(8,128)(2,1)S(1)}, u32[]{:S(2)}, u32[]{:S(2)}) %collective-permute-start.7) | collective-permute-done | bytes 131104 | tf_op jit(solution)/shard_map/ppermute | solution.py:33
  22.0 1.9 %collective-permute-start.10 = (bf16[64,1024]{1,0:T(8,128)(2,1)S(1)}, bf16[64,1024]{1,0:T(8,128)(2,1)S(1)}, u32[]{:S(2)}, u32[]{:S(2)}) collective-permute-start(bf16[64,1024]{1,0:T(8,128)(2,1)S(1)} %add.40), channel_id=1, source_target_pairs={{1,25},{3,27},{5,29},{7,31},{9,17},{11,19},{13,21},{15,23},{17,9},... | collective-permute-start | bytes 393224 | tf_op jit(solution)/shard_map/ppermute | solution.py:33
  24.0 1.3 %text_grad.1 = f32[256,1024]{1,0:T(8,128)} custom-call(bf16[256,256]{1,0:T(8,128)(2,1)S(1)} %get-tuple-element.12.coeff_ref, bf16[256,1024]{1,0:T(8,128)(2,1)S(1)} %pile.1.covs_ref), custom_call_target="tpu_custom_call" | custom-call | flops 134217728 | bytes 1048576 | tf_op jit(solution)/shard_map/text_grad/pallas_call | solution.py:122
  25.3 0.0 collective-permute-done.8
  25.3 0.0 collective-permute-done.9
  25.3 4.6 %collective-permute-done.10 = bf16[64,1024]{1,0:T(8,128)(2,1)S(1)} collective-permute-done((bf16[64,1024]{1,0:T(8,128)(2,1)S(1)}, bf16[64,1024]{1,0:T(8,128)(2,1)S(1)}, u32[]{:S(2)}, u32[]{:S(2)}) %collective-permute-start.10) | collective-permute-done | bytes 131104 | tf_op jit(solution)/shard_map/ppermute | solution.py:33
  29.9 0.8 %add_bitcast_fusion = f32[1,64,1024]{2,1,0:T(8,128)} fusion(bf16[64,1024]{1,0:T(8,128)(2,1)S(1)} %collective-permute-done.10, bf16[64,1024]{1,0:T(8,128)(2,1)S(1)} %collective-permute-done.9, bf16[64,1024]{1,0:T(8,128)(2,1)S(1)} %collective-permute-done.8, f32[64,1024]{1,0:T(8,128)S(1)} %get-tuple-element.13, ...), kind=kLoop, calls=%fused_computation | loop fusion | flops 589824 | bytes 1048577 | tf_op jit(solution)/shard_map/broadcast_in_dim | solution.py:191
  (8 shorter events, 0.1 us)
Async XLA Ops:
  0.6 9.8 %collective-permute-start.1 = (bf16[64,1024]{1,0:T(8,128)(2,1)}, bf16[64,1024]{1,0:T(8,128)(2,1)S(1)}, u32[]{:S(2)}, u32[]{:S(2)}) collective-permute-start(bf16[64,1024]{1,0:T(8,128)(2,1)} %bitcast.19), channel_id=1, source_target_pairs={{0,8},{1,17},{2,10},{3,19},{4,12},{5,21},{6,14},{7,23},{8,0},{9,25... | collective-permute-start | bytes 393224 | tf_op jit(solution)/shard_map/ppermute | solution.py:33
  3.8 6.6 %collective-permute-start = (bf16[64,1024]{1,0:T(8,128)(2,1)}, bf16[64,1024]{1,0:T(8,128)(2,1)S(1)}, u32[]{:S(2)}, u32[]{:S(2)}) collective-permute-start(bf16[64,1024]{1,0:T(8,128)(2,1)} %bitcast.20), channel_id=1, source_target_pairs={{0,16},{1,9},{2,18},{3,11},{4,20},{5,13},{6,22},{7,15},{8,24},{9,1... | collective-permute-start | bytes 393224 | tf_op jit(solution)/shard_map/ppermute | solution.py:33
  5.1 9.6 %copy-start = (bf16[8,32,1024]{2,1,0:T(8,128)(2,1)S(1)}, bf16[8,32,1024]{2,1,0:T(8,128)(2,1)}, u32[]{:S(2)}) copy-start(bf16[8,32,1024]{2,1,0:T(8,128)(2,1)} %param.5) | copy-start | bytes 1572868
  6.3 6.1 %collective-permute-start.5 = (bf16[2,32,1024]{2,1,0:T(8,128)(2,1)S(1)}, bf16[2,32,1024]{2,1,0:T(8,128)(2,1)S(1)}, u32[]{:S(2)}, u32[]{:S(2)}) collective-permute-start(bf16[2,32,1024]{2,1,0:T(8,128)(2,1)S(1)} %get-tuple-element.18), channel_id=1, source_target_pairs={{0,6},{1,7},{2,4},{3,5},{4,2},{5,3},{6,0},{7,1},{8,14},{9,15},{10,... | collective-permute-start | bytes 393224 | tf_op jit(solution)/shard_map/ppermute | solution.py:26
  8.5 6.3 %collective-permute-start.4 = (bf16[2,32,1024]{2,1,0:T(8,128)(2,1)S(1)}, bf16[2,32,1024]{2,1,0:T(8,128)(2,1)S(1)}, u32[]{:S(2)}, u32[]{:S(2)}) collective-permute-start(bf16[2,32,1024]{2,1,0:T(8,128)(2,1)S(1)} %get-tuple-element.19), channel_id=1, source_target_pairs={{0,4},{1,5},{2,6},{3,7},{4,0},{5,1},{6,2},{7,3},{8,12},{9,13},{10,... | collective-permute-start | bytes 393224 | tf_op jit(solution)/shard_map/ppermute | solution.py:26
  8.7 6.1 %collective-permute-start.3 = (bf16[2,32,1024]{2,1,0:T(8,128)(2,1)S(1)}, bf16[2,32,1024]{2,1,0:T(8,128)(2,1)S(1)}, u32[]{:S(2)}, u32[]{:S(2)}) collective-permute-start(bf16[2,32,1024]{2,1,0:T(8,128)(2,1)S(1)} %get-tuple-element.20), channel_id=1, source_target_pairs={{0,2},{1,3},{2,0},{3,1},{4,6},{5,7},{6,4},{7,5},{8,10},{9,11},{10,... | collective-permute-start | bytes 393224 | tf_op jit(solution)/shard_map/ppermute | solution.py:26
  9.6 0.7 %copy-start.2 = (s32[1,256]{1,0:T(1,128)S(1)}, s32[1,256]{1,0:T(1,128)}, u32[]{:S(2)}) copy-start(s32[1,256]{1,0:T(1,128)} %param.7) | copy-start | bytes 3076
  10.5 5.6 %copy-start.1 = (bf16[1,64,1024]{2,1,0:T(8,128)(2,1)S(1)}, bf16[1,64,1024]{2,1,0:T(8,128)(2,1)}, u32[]{:S(2)}) copy-start(bf16[1,64,1024]{2,1,0:T(8,128)(2,1)} %param.6) | copy-start | bytes 393220
  10.5 5.6 %collective-permute-start.2 = (bf16[64,1024]{1,0:T(8,128)(2,1)S(1)}, bf16[64,1024]{1,0:T(8,128)(2,1)S(1)}, u32[]{:S(2)}, u32[]{:S(2)}) collective-permute-start(bf16[64,1024]{1,0:T(8,128)(2,1)S(1)} %get-tuple-element.11.refs_2_.refs_4_), channel_id=1, source_target_pairs={{0,8},{8,0},{16,24},{24,16},{1,9},{9,1},{17,25},{25,17},{2,10},{10... | collective-permute-start | bytes 393224 | tf_op jit(solution)/shard_map/ppermute | solution.py:26
  14.8 2.5 %collective-permute-start.6 = (bf16[4,32,1024]{2,1,0:T(8,128)(2,1)S(1)}, bf16[4,32,1024]{2,1,0:T(8,128)(2,1)S(1)}, u32[]{:S(2)}, u32[]{:S(2)}) collective-permute-start(bf16[4,32,1024]{2,1,0:T(8,128)(2,1)S(1)} %select.7), channel_id=1, source_target_pairs={{0,1},{1,0},{2,3},{3,2},{4,5},{5,4},{6,7},{7,6},{8,9},{9,8},{10,11... | collective-permute-start | bytes 786440 | tf_op jit(solution)/shard_map/ppermute | solution.py:26
  18.1 3.9 %collective-permute-start.7 = (bf16[64,1024]{1,0:T(8,128)(2,1)S(1)}, bf16[64,1024]{1,0:T(8,128)(2,1)S(1)}, u32[]{:S(2)}, u32[]{:S(2)}) collective-permute-start(bf16[64,1024]{1,0:T(8,128)(2,1)S(1)} %get-tuple-element.14), channel_id=1, source_target_pairs={{0,16},{1,9},{2,18},{3,11},{4,20},{5,13},{6,22},{7,15},{8,24},{9,1... | collective-permute-start | bytes 393224 | tf_op jit(solution)/shard_map/ppermute | solution.py:33
  18.4 6.9 %collective-permute-start.8 = (bf16[64,1024]{1,0:T(8,128)(2,1)S(1)}, bf16[64,1024]{1,0:T(8,128)(2,1)S(1)}, u32[]{:S(2)}, u32[]{:S(2)}) collective-permute-start(bf16[64,1024]{1,0:T(8,128)(2,1)S(1)} %get-tuple-element.15), channel_id=1, source_target_pairs={{0,24},{1,9},{2,26},{3,11},{4,28},{5,13},{6,30},{7,15},{8,16},{9,1... | collective-permute-start | bytes 393224 | tf_op jit(solution)/shard_map/ppermute | solution.py:33
  19.6 5.6 %collective-permute-start.9 = (bf16[64,1024]{1,0:T(8,128)(2,1)S(1)}, bf16[64,1024]{1,0:T(8,128)(2,1)S(1)}, u32[]{:S(2)}, u32[]{:S(2)}) collective-permute-start(bf16[64,1024]{1,0:T(8,128)(2,1)S(1)} %get-tuple-element.16), channel_id=1, source_target_pairs={{0,8},{2,10},{4,12},{6,14},{8,0},{10,2},{12,4},{14,6},{16,24},{18,... | collective-permute-start | bytes 393224 | tf_op jit(solution)/shard_map/ppermute | solution.py:33
  22.0 7.9 %collective-permute-start.10 = (bf16[64,1024]{1,0:T(8,128)(2,1)S(1)}, bf16[64,1024]{1,0:T(8,128)(2,1)S(1)}, u32[]{:S(2)}, u32[]{:S(2)}) collective-permute-start(bf16[64,1024]{1,0:T(8,128)(2,1)S(1)} %add.40), channel_id=1, source_target_pairs={{1,25},{3,27},{5,29},{7,31},{9,17},{11,19},{13,21},{15,23},{17,9},... | collective-permute-start | bytes 393224 | tf_op jit(solution)/shard_map/ppermute | solution.py:33

commit v8 on v5

--- a/solution.py
+++ b/solution.py
@@ -140,7 +140,8 @@
         got = [exchange(part, "blk", k if is_power(count) else -k) for k, part in enumerate(parts, 1)]
         return sum((part.astype(F32) for part in got), own)
     first, second, third, far = parts
-    got = [mixed(first, 2, 1), mixed(second, 3, 1), mixed(third, 1, 0)]
+    straight = mixed(second, 3, 1)
+    got = [mixed(first, 2, 1), straight, mixed(third, 1, 0)]
     summed = call(add_kernel, "add", SHAPE(far.shape, BF16), [far, got[0]], 0)
     got.append(mixed(summed, 0, 3))
     odd = lax.axis_index("section") % 2 == 1

time: 30.9 us -> 30.9 us (level)
  no operation moved by 1% of the time
where the time goes in v8:
time: 30.9 us; the launch traced here: 30.7 us
  starting transfers between devices  14.5 us (47%)
  waiting for transfers between devices  9.9 us (32%)
  Pallas kernels  2.22 us (7%)
  between operations  2.05 us (7%)
  local copies, waits for them, and re-layouts  1.14 us (4%)
  other arithmetic  0.87 us (3%)
    ppermute x6, starting transfers between devices, mixed(): return lax.ppermute(value, ('blk', 'section'), pairs)  8.61 us
    ppermute x6, waiting for transfers between devices, mixed(): return lax.ppermute(value, ('blk', 'section'), pairs)  6.36 us
    ppermute x5, starting transfers between devices, exchange(): lax.ppermute(value, axis, [(i, i ^ k if is_power(count) else (i + k) % co...  5.89 us
    ppermute x5, waiting for transfers between devices, exchange(): lax.ppermute(value, axis, [(i, i ^ k if is_power(count) else (i + k) % co...  3.54 us
    pallas_call x6, Pallas kernels, call(): pl.pallas_call(kernel, out_shape=out_shape, in_specs=specs or [VMEM] * le...  2.22 us
    squeeze x1, local copies, waits for them, and re-layouts, fetch_texts(): lax.dynamic_index_in_dim(by_chip, chip ^ k, 0, keepdims=False)  1.11 us
    broadcast_in_dim x1, other arithmetic, local(): return (text_grad[None], total[None])  0.79 us
  transfers between devices with their start and end apart: 11, of which 5 were waited for; matrix products, arithmetic and copies ran while one was open for 4% of the time, Pallas kernels for 5%

profile of v8, /device:TPU:1, one launch (start us, length us, event | category | flops | bytes accessed | tf_op | source)
XLA Modules:
  0.0 30.7 jit_solution(10041023101671343722)
XLA Ops:
  0.6 3.2 %collective-permute-start.1 = (bf16[64,1024]{1,0:T(8,128)(2,1)}, bf16[64,1024]{1,0:T(8,128)(2,1)S(1)}, u32[]{:S(2)}, u32[]{:S(2)}) collective-permute-start(bf16[64,1024]{1,0:T(8,128)(2,1)} %bitcast.19), channel_id=1, source_target_pairs={{0,8},{1,17},{2,10},{3,19},{4,12},{5,21},{6,14},{7,23},{8,0},{9,25... | collective-permute-start | bytes 393224 | tf_op jit(solution)/shard_map/ppermute | solution.py:33
  3.8 1.3 %collective-permute-start = (bf16[64,1024]{1,0:T(8,128)(2,1)}, bf16[64,1024]{1,0:T(8,128)(2,1)S(1)}, u32[]{:S(2)}, u32[]{:S(2)}) collective-permute-start(bf16[64,1024]{1,0:T(8,128)(2,1)} %bitcast.20), channel_id=1, source_target_pairs={{0,16},{1,9},{2,18},{3,11},{4,20},{5,13},{6,22},{7,15},{8,24},{9,1... | collective-permute-start | bytes 393224 | tf_op jit(solution)/shard_map/ppermute | solution.py:33
  5.1 1.1 %dynamic-slice_bitcast_fusion = (bf16[2,32,1024]{2,1,0:T(8,128)(2,1)S(1)}, bf16[2,32,1024]{2,1,0:T(8,128)(2,1)S(1)}, bf16[2,32,1024]{2,1,0:T(8,128)(2,1)S(1)}) fusion(bf16[4,2,32,1024]{3,2,1,0:T(8,128)(2,1)} %bitcast.16, s32[]{:T(128)S(6)} %select_n.43, s32[]{:T(128)S(6)} %select_n.42, s32[]{:T(128)S(6)} %select_n.41), kind=kLoop, calls=%fused_computation.1 | loop fusion | bytes 786444 | tf_op jit(solution)/shard_map/jit(dynamic_index_in_dim)/squeeze | solution.py:166
  6.3 2.2 %collective-permute-start.5 = (bf16[2,32,1024]{2,1,0:T(8,128)(2,1)S(1)}, bf16[2,32,1024]{2,1,0:T(8,128)(2,1)S(1)}, u32[]{:S(2)}, u32[]{:S(2)}) collective-permute-start(bf16[2,32,1024]{2,1,0:T(8,128)(2,1)S(1)} %get-tuple-element.18), channel_id=1, source_target_pairs={{0,6},{1,7},{2,4},{3,5},{4,2},{5,3},{6,0},{7,1},{8,14},{9,15},{10,... | collective-permute-start | bytes 393224 | tf_op jit(solution)/shard_map/ppermute | solution.py:26
  8.5 0.2 collective-permute-start.4
  8.7 0.3 collective-permute-start.3
  9.6 0.0 copy-start.2
  10.3 0.0 copy-done.2
  10.3 0.1 broadcast_select_fusion.refs_5_.params_ref
  10.4 0.0 collective-permute-done.1.second_ref
  10.4 0.1 collective-permute-done.first_ref
  10.5 0.0 copy-start.1
  10.5 1.8 %collective-permute-start.2 = (bf16[64,1024]{1,0:T(8,128)(2,1)S(1)}, bf16[64,1024]{1,0:T(8,128)(2,1)S(1)}, u32[]{:S(2)}, u32[]{:S(2)}) collective-permute-start(bf16[64,1024]{1,0:T(8,128)(2,1)S(1)} %get-tuple-element.11.refs_2_.refs_4_), channel_id=1, source_target_pairs={{0,8},{8,0},{16,24},{24,16},{1,9},{9,1},{17,25},{25,17},{2,10},{10... | collective-permute-start | bytes 393224 | tf_op jit(solution)/shard_map/ppermute | solution.py:26
  12.3 0.0 collective-permute-done.5.refs_3_
  12.4 2.4 %collective-permute-done.4.refs_2_ = bf16[2,32,1024]{2,1,0:T(8,128)(2,1)S(1)} collective-permute-done((bf16[2,32,1024]{2,1,0:T(8,128)(2,1)S(1)}, bf16[2,32,1024]{2,1,0:T(8,128)(2,1)S(1)}, u32[]{:S(2)}, u32[]{:S(2)}) %collective-permute-start.4) | collective-permute-done | bytes 131104 | tf_op jit(solution)/shard_map/ppermute | solution.py:26
  14.8 0.0 collective-permute-done.3.refs_1_
  14.8 0.0 copy-done
  14.8 1.3 %collective-permute-start.6 = (bf16[4,32,1024]{2,1,0:T(8,128)(2,1)S(1)}, bf16[4,32,1024]{2,1,0:T(8,128)(2,1)S(1)}, u32[]{:S(2)}, u32[]{:S(2)}) collective-permute-start(bf16[4,32,1024]{2,1,0:T(8,128)(2,1)S(1)} %select.7), channel_id=1, source_target_pairs={{0,1},{1,0},{2,3},{3,2},{4,5},{5,4},{6,7},{7,6},{8,9},{9,8},{10,11... | collective-permute-start | bytes 786440 | tf_op jit(solution)/shard_map/ppermute | solution.py:26
  16.1 0.0 collective-permute-done.2.refs_3_
  16.1 0.0 copy-done.1
  16.2 1.1 %collective-permute-done.6.refs_4_ = bf16[4,32,1024]{2,1,0:T(8,128)(2,1)S(1)} collective-permute-done((bf16[4,32,1024]{2,1,0:T(8,128)(2,1)S(1)}, bf16[4,32,1024]{2,1,0:T(8,128)(2,1)S(1)}, u32[]{:S(2)}, u32[]{:S(2)}) %collective-permute-start.6) | collective-permute-done | bytes 262176 | tf_op jit(solution)/shard_map/ppermute | solution.py:26
  17.3 0.8 %coeff.1 = (bf16[256,256]{1,0:T(8,128)(2,1)S(1)}, f32[64,1024]{1,0:T(8,128)S(1)}, bf16[64,1024]{1,0:T(8,128)(2,1)S(1)}, bf16[64,1024]{1,0:T(8,128)(2,1)S(1)}, bf...) custom-call(f32[8,256]{1,0:T(8,128)S(1)} %broadcast_select_fusion.refs_5_.params_ref, ...), custom_call_target="tpu_custom_call" | custom-call | flops 268435456 | bytes 1048576 | tf_op jit(solution)/shard_map/coeff/pallas_call | solution.py:122
  18.1 0.2 collective-permute-start.7
  18.4 1.3 %collective-permute-start.8 = (bf16[64,1024]{1,0:T(8,128)(2,1)S(1)}, bf16[64,1024]{1,0:T(8,128)(2,1)S(1)}, u32[]{:S(2)}, u32[]{:S(2)}) collective-permute-start(bf16[64,1024]{1,0:T(8,128)(2,1)S(1)} %get-tuple-element.15), channel_id=1, source_target_pairs={{0,24},{1,9},{2,26},{3,11},{4,28},{5,13},{6,30},{7,15},{8,16},{9,1... | collective-permute-start | bytes 393224 | tf_op jit(solution)/shard_map/ppermute | solution.py:33
  19.6 0.7 %collective-permute-start.9 = (bf16[64,1024]{1,0:T(8,128)(2,1)S(1)}, bf16[64,1024]{1,0:T(8,128)(2,1)S(1)}, u32[]{:S(2)}, u32[]{:S(2)}) collective-permute-start(bf16[64,1024]{1,0:T(8,128)(2,1)S(1)} %get-tuple-element.16), channel_id=1, source_target_pairs={{0,8},{2,10},{4,12},{6,14},{8,0},{10,2},{12,4},{14,6},{16,24},{18,... | collective-permute-start | bytes 393224 | tf_op jit(solution)/shard_map/ppermute | solution.py:33
  20.3 1.7 %collective-permute-done.7.got_ref = bf16[64,1024]{1,0:T(8,128)(2,1)S(1)} collective-permute-done((bf16[64,1024]{1,0:T(8,128)(2,1)S(1)}, bf16[64,1024]{1,0:T(8,128)(2,1)S(1)}, u32[]{:S(2)}, u32[]{:S(2)}) %collective-permute-start.7) | collective-permute-done | bytes 131104 | tf_op jit(solution)/shard_map/ppermute | solution.py:33
  22.0 1.9 %collective-permute-start.10 = (bf16[64,1024]{1,0:T(8,128)(2,1)S(1)}, bf16[64,1024]{1,0:T(8,128)(2,1)S(1)}, u32[]{:S(2)}, u32[]{:S(2)}) collective-permute-start(bf16[64,1024]{1,0:T(8,128)(2,1)S(1)} %add.40), channel_id=1, source_target_pairs={{1,25},{3,27},{5,29},{7,31},{9,17},{11,19},{13,21},{15,23},{17,9},... | collective-permute-start | bytes 393224 | tf_op jit(solution)/shard_map/ppermute | solution.py:33
  24.0 1.3 %text_grad.1 = f32[256,1024]{1,0:T(8,128)} custom-call(bf16[256,256]{1,0:T(8,128)(2,1)S(1)} %get-tuple-element.12.coeff_ref, bf16[256,1024]{1,0:T(8,128)(2,1)S(1)} %pile.1.covs_ref), custom_call_target="tpu_custom_call" | custom-call | flops 134217728 | bytes 1048576 | tf_op jit(solution)/shard_map/text_grad/pallas_call | solution.py:122
  25.3 0.0 collective-permute-done.8
  25.3 0.0 collective-permute-done.9
  25.3 4.6 %collective-permute-done.10 = bf16[64,1024]{1,0:T(8,128)(2,1)S(1)} collective-permute-done((bf16[64,1024]{1,0:T(8,128)(2,1)S(1)}, bf16[64,1024]{1,0:T(8,128)(2,1)S(1)}, u32[]{:S(2)}, u32[]{:S(2)}) %collective-permute-start.10) | collective-permute-done | bytes 131104 | tf_op jit(solution)/shard_map/ppermute | solution.py:33
  29.9 0.8 %add_bitcast_fusion = f32[1,64,1024]{2,1,0:T(8,128)} fusion(bf16[64,1024]{1,0:T(8,128)(2,1)S(1)} %collective-permute-done.10, bf16[64,1024]{1,0:T(8,128)(2,1)S(1)} %collective-permute-done.9, bf16[64,1024]{1,0:T(8,128)(2,1)S(1)} %collective-permute-done.8, f32[64,1024]{1,0:T(8,128)S(1)} %get-tuple-element.13, ...), kind=kLoop, calls=%fused_computation | loop fusion | flops 589824 | bytes 1048577 | tf_op jit(solution)/shard_map/broadcast_in_dim | solution.py:191
  (8 shorter events, 0.1 us)
Async XLA Ops:
  0.6 9.8 %collective-permute-start.1 = (bf16[64,1024]{1,0:T(8,128)(2,1)}, bf16[64,1024]{1,0:T(8,128)(2,1)S(1)}, u32[]{:S(2)}, u32[]{:S(2)}) collective-permute-start(bf16[64,1024]{1,0:T(8,128)(2,1)} %bitcast.19), channel_id=1, source_target_pairs={{0,8},{1,17},{2,10},{3,19},{4,12},{5,21},{6,14},{7,23},{8,0},{9,25... | collective-permute-start | bytes 393224 | tf_op jit(solution)/shard_map/ppermute | solution.py:33
  3.8 6.6 %collective-permute-start = (bf16[64,1024]{1,0:T(8,128)(2,1)}, bf16[64,1024]{1,0:T(8,128)(2,1)S(1)}, u32[]{:S(2)}, u32[]{:S(2)}) collective-permute-start(bf16[64,1024]{1,0:T(8,128)(2,1)} %bitcast.20), channel_id=1, source_target_pairs={{0,16},{1,9},{2,18},{3,11},{4,20},{5,13},{6,22},{7,15},{8,24},{9,1... | collective-permute-start | bytes 393224 | tf_op jit(solution)/shard_map/ppermute | solution.py:33
  5.1 9.6 %copy-start = (bf16[8,32,1024]{2,1,0:T(8,128)(2,1)S(1)}, bf16[8,32,1024]{2,1,0:T(8,128)(2,1)}, u32[]{:S(2)}) copy-start(bf16[8,32,1024]{2,1,0:T(8,128)(2,1)} %param.5) | copy-start | bytes 1572868
  6.3 6.1 %collective-permute-start.5 = (bf16[2,32,1024]{2,1,0:T(8,128)(2,1)S(1)}, bf16[2,32,1024]{2,1,0:T(8,128)(2,1)S(1)}, u32[]{:S(2)}, u32[]{:S(2)}) collective-permute-start(bf16[2,32,1024]{2,1,0:T(8,128)(2,1)S(1)} %get-tuple-element.18), channel_id=1, source_target_pairs={{0,6},{1,7},{2,4},{3,5},{4,2},{5,3},{6,0},{7,1},{8,14},{9,15},{10,... | collective-permute-start | bytes 393224 | tf_op jit(solution)/shard_map/ppermute | solution.py:26
  8.5 6.3 %collective-permute-start.4 = (bf16[2,32,1024]{2,1,0:T(8,128)(2,1)S(1)}, bf16[2,32,1024]{2,1,0:T(8,128)(2,1)S(1)}, u32[]{:S(2)}, u32[]{:S(2)}) collective-permute-start(bf16[2,32,1024]{2,1,0:T(8,128)(2,1)S(1)} %get-tuple-element.19), channel_id=1, source_target_pairs={{0,4},{1,5},{2,6},{3,7},{4,0},{5,1},{6,2},{7,3},{8,12},{9,13},{10,... | collective-permute-start | bytes 393224 | tf_op jit(solution)/shard_map/ppermute | solution.py:26
  8.7 6.1 %collective-permute-start.3 = (bf16[2,32,1024]{2,1,0:T(8,128)(2,1)S(1)}, bf16[2,32,1024]{2,1,0:T(8,128)(2,1)S(1)}, u32[]{:S(2)}, u32[]{:S(2)}) collective-permute-start(bf16[2,32,1024]{2,1,0:T(8,128)(2,1)S(1)} %get-tuple-element.20), channel_id=1, source_target_pairs={{0,2},{1,3},{2,0},{3,1},{4,6},{5,7},{6,4},{7,5},{8,10},{9,11},{10,... | collective-permute-start | bytes 393224 | tf_op jit(solution)/shard_map/ppermute | solution.py:26
  9.6 0.7 %copy-start.2 = (s32[1,256]{1,0:T(1,128)S(1)}, s32[1,256]{1,0:T(1,128)}, u32[]{:S(2)}) copy-start(s32[1,256]{1,0:T(1,128)} %param.7) | copy-start | bytes 3076
  10.5 5.6 %copy-start.1 = (bf16[1,64,1024]{2,1,0:T(8,128)(2,1)S(1)}, bf16[1,64,1024]{2,1,0:T(8,128)(2,1)}, u32[]{:S(2)}) copy-start(bf16[1,64,1024]{2,1,0:T(8,128)(2,1)} %param.6) | copy-start | bytes 393220
  10.5 5.6 %collective-permute-start.2 = (bf16[64,1024]{1,0:T(8,128)(2,1)S(1)}, bf16[64,1024]{1,0:T(8,128)(2,1)S(1)}, u32[]{:S(2)}, u32[]{:S(2)}) collective-permute-start(bf16[64,1024]{1,0:T(8,128)(2,1)S(1)} %get-tuple-element.11.refs_2_.refs_4_), channel_id=1, source_target_pairs={{0,8},{8,0},{16,24},{24,16},{1,9},{9,1},{17,25},{25,17},{2,10},{10... | collective-permute-start | bytes 393224 | tf_op jit(solution)/shard_map/ppermute | solution.py:26
  14.8 2.5 %collective-permute-start.6 = (bf16[4,32,1024]{2,1,0:T(8,128)(2,1)S(1)}, bf16[4,32,1024]{2,1,0:T(8,128)(2,1)S(1)}, u32[]{:S(2)}, u32[]{:S(2)}) collective-permute-start(bf16[4,32,1024]{2,1,0:T(8,128)(2,1)S(1)} %select.7), channel_id=1, source_target_pairs={{0,1},{1,0},{2,3},{3,2},{4,5},{5,4},{6,7},{7,6},{8,9},{9,8},{10,11... | collective-permute-start | bytes 786440 | tf_op jit(solution)/shard_map/ppermute | solution.py:26
  18.1 3.9 %collective-permute-start.7 = (bf16[64,1024]{1,0:T(8,128)(2,1)S(1)}, bf16[64,1024]{1,0:T(8,128)(2,1)S(1)}, u32[]{:S(2)}, u32[]{:S(2)}) collective-permute-start(bf16[64,1024]{1,0:T(8,128)(2,1)S(1)} %get-tuple-element.14), channel_id=1, source_target_pairs={{0,16},{1,9},{2,18},{3,11},{4,20},{5,13},{6,22},{7,15},{8,24},{9,1... | collective-permute-start | bytes 393224 | tf_op jit(solution)/shard_map/ppermute | solution.py:33
  18.4 6.9 %collective-permute-start.8 = (bf16[64,1024]{1,0:T(8,128)(2,1)S(1)}, bf16[64,1024]{1,0:T(8,128)(2,1)S(1)}, u32[]{:S(2)}, u32[]{:S(2)}) collective-permute-start(bf16[64,1024]{1,0:T(8,128)(2,1)S(1)} %get-tuple-element.15), channel_id=1, source_target_pairs={{0,24},{1,9},{2,26},{3,11},{4,28},{5,13},{6,30},{7,15},{8,16},{9,1... | collective-permute-start | bytes 393224 | tf_op jit(solution)/shard_map/ppermute | solution.py:33
  19.6 5.6 %collective-permute-start.9 = (bf16[64,1024]{1,0:T(8,128)(2,1)S(1)}, bf16[64,1024]{1,0:T(8,128)(2,1)S(1)}, u32[]{:S(2)}, u32[]{:S(2)}) collective-permute-start(bf16[64,1024]{1,0:T(8,128)(2,1)S(1)} %get-tuple-element.16), channel_id=1, source_target_pairs={{0,8},{2,10},{4,12},{6,14},{8,0},{10,2},{12,4},{14,6},{16,24},{18,... | collective-permute-start | bytes 393224 | tf_op jit(solution)/shard_map/ppermute | solution.py:33
  22.0 7.9 %collective-permute-start.10 = (bf16[64,1024]{1,0:T(8,128)(2,1)S(1)}, bf16[64,1024]{1,0:T(8,128)(2,1)S(1)}, u32[]{:S(2)}, u32[]{:S(2)}) collective-permute-start(bf16[64,1024]{1,0:T(8,128)(2,1)S(1)} %add.40), channel_id=1, source_target_pairs={{1,25},{3,27},{5,29},{7,31},{9,17},{11,19},{13,21},{15,23},{17,9},... | collective-permute-start | bytes 393224 | tf_op jit(solution)/shard_map/ppermute | solution.py:33
